TPU v7x, 32 devices: a whole 2x2x4 slice. The times are simulated.
32 devices in a mesh: groups: 2 (over x), rows: 16 (over z, y, core).
Axes of the slice: x: 2, y: 2, z: 4, core: 2. Of those that a mesh axis runs over, the one named last changes fastest.
Arguments:
- embeddings: bfloat16 [65536, 768], P(('groups', 'rows')), parts along dimension 0, may hold values from -6 to 6
- cluster_id: int32 [65536, 1], P(('groups', 'rows')), parts along dimension 0, may hold values from 0 to 511; in each aligned block of 2048 rows (0 to 2047, 2048 to 4095, ...) at most 16 rows name the same one
Outputs:
- nearest: float32 [65536], P(('groups', 'rows')), parts along dimension 0
There are 2 independent parts, one for each index of `groups`. A program takes and returns all parts, laid end to end along the dimension named above; each array names one. Nothing has to cross between parts.
Inputs may be any that keep to these rules, and one draw needn't show every extreme that they name: `cluster_id`: in each aligned block of 2048 rows (the rows of one device) no cluster is named by more than 16 rows, a bound that some block reaches; every cluster is named somewhere.
All inputs are finite; a program needn't handle non-finite values.
Results may differ from a plain program's by a relative error of at most 0.0018.
Values may be sent and summed in bfloat16 or wider, within the bound.
No kernel may reach another device: no remote copies, remote signals or barrier semaphores. Data moves between devices by JAX's collectives and lax.ppermute only.
A program may use at most 128 MiB of HBM per device.

v0:
```python
import jax
import jax.numpy as jnp
from jax import lax
from jax.sharding import PartitionSpec as P

CLUSTERS = 512
MOST = 16


def cluster_best(pair):
    blocks, flags = pair
    peers, owned, most, width = blocks.shape
    slots = peers * most
    members = jnp.transpose(blocks, (1, 0, 2, 3)).reshape(owned, slots, width)
    valid = jnp.transpose(flags, (1, 0, 2)).reshape(owned, slots) > 0.5
    off_diagonal = jnp.logical_not(jnp.eye(slots, dtype=bool))

    def one_cluster(item):
        rows_of, valid_of = item
        gram = jnp.dot(rows_of, rows_of.T, preferred_element_type=jnp.float32)
        keep = valid_of[None, :] & off_diagonal
        return jnp.max(jnp.where(keep, gram, jnp.float32(-1.0)), axis=1)

    best = lax.map(one_cluster, (members, valid))
    return jnp.transpose(best.reshape(owned, peers, most), (1, 0, 2))


def local(embeddings, cluster_id):
    labels = cluster_id[:, 0]
    count = labels.shape[0]
    width = embeddings.shape[1]
    peers = lax.axis_size("rows")
    owned = CLUSTERS // peers
    values = embeddings.astype(jnp.float32)
    unit = (values * lax.rsqrt(jnp.sum(values * values, axis=1, keepdims=True) + 1e-06)).astype(
        jnp.bfloat16
    )
    positions = jnp.arange(count, dtype=jnp.int32)
    same_before = (labels[:, None] == labels[None, :]) & (positions[None, :] < positions[:, None])
    ranks = jnp.sum(same_before.astype(jnp.int32), axis=1)
    cluster_hot = (labels[:, None] == jnp.arange(CLUSTERS, dtype=jnp.int32)[None, :]).astype(
        jnp.float32
    )
    rank_hot = (ranks[:, None] == jnp.arange(MOST, dtype=jnp.int32)[None, :]).astype(jnp.float32)
    numbered = rank_hot * (positions + 1).astype(jnp.float32)[:, None]
    filled = jnp.dot(cluster_hot.T, rank_hot, precision=lax.Precision.HIGHEST)
    member_pos = jnp.dot(cluster_hot.T, numbered, precision=lax.Precision.HIGHEST)
    member_idx = member_pos.astype(jnp.int32) - 1
    member_idx = jnp.where(member_idx < 0, count, member_idx).reshape(CLUSTERS * MOST)
    padded = jnp.concatenate([unit, jnp.zeros((1, width), jnp.bfloat16)], axis=0)
    outgoing = padded[member_idx].reshape(peers, owned, MOST, width)
    occupied = filled.astype(jnp.bfloat16).reshape(peers, owned, MOST)
    arrived = (
        lax.all_to_all(outgoing, "rows", split_axis=0, concat_axis=0, tiled=True),
        lax.all_to_all(occupied, "rows", split_axis=0, concat_axis=0, tiled=True),
    )
    best = cluster_best(arrived)
    returned = lax.all_to_all(best, "rows", split_axis=0, concat_axis=0, tiled=True)
    table = returned.reshape(CLUSTERS, MOST)
    per_row = jnp.dot(cluster_hot, table, precision=lax.Precision.HIGHEST)
    return jnp.sum(per_row * rank_hot, axis=1)


def solution(mesh):
    return jax.shard_map(
        local,
        mesh=mesh,
        in_specs=(P(("groups", "rows"), None), P(("groups", "rows"), None)),
        out_specs=P(("groups", "rows")),
        check_vma=False,
    )
```

profile of v0, /device:TPU:0, one launch (start us, length us, event | category | flops | bytes accessed | tf_op | source)
XLA Modules:
  0.0 409.9 jit_solution(11149258556919563116)
XLA Ops:
  0.0 5.3 %convert_reduce_fusion = s32[2048]{0:T(1024)S(1)} fusion(s32[2048]{0:T(1024)} %bitcast.39), kind=kLoop, calls=%fused_computation.11 | loop fusion | flops 20969472 | bytes 16384 | tf_op jit(solution)/shard_map/reduce_sum | solution.py:40
  5.3 1.5 fusion.21
  7.6 7.4 %all-to-all-start = ((bf16[16,2,256]{2,1,0:T(2,128)(2,1)}), bf16[16,2,256]{2,1,0:T(2,128)(2,1)S(1)}, u32[]{:S(2)}, u32[]{:S(2)}) async-start(bf16[16,2,256]{2,1,0:T(2,128)(2,1)} %reshape.77), calls=%async_computation | async-start | bytes 32768 | tf_op jit(solution)/shard_map/all_to_all | solution.py:55
  15.0 2.2 compare_select_fusion.1
  17.6 2.6 fusion.9
  21.0 34.5 %gather_fusion = bf16[8192,768]{1,0:T(8,128)(2,1)} fusion(bf16[2049,768]{1,0:T(8,128)(2,1)S(1)} %concatenate.3, s32[8192]{0:T(1024)S(1)} %broadcast_clamp_fusion), kind=kCustom, calls=%fused_computation | custom fusion | bytes 25198592 | tf_op jit(solution)/shard_map/gather | solution.py:51
  55.5 6.1 %all-to-all-start.1 = ((bf16[16,32,16,768]{3,2,1,0:T(8,128)(2,1)}), bf16[16,32,16,768]{3,2,1,0:T(8,128)(2,1)}, u32[]{:S(2)}, u32[]{:S(2)}) async-start(bf16[16,32,16,768]{3,2,1,0:T(8,128)(2,1)} %bitcast.31), calls=%async_computation.1 | async-start | bytes 25165824 | tf_op jit(solution)/shard_map/all_to_all | solution.py:54
  61.8 223.5 %all-to-all-done.1 = bf16[16,32,16,768]{3,2,1,0:T(8,128)(2,1)} async-done(((bf16[16,32,16,768]{3,2,1,0:T(8,128)(2,1)}), bf16[16,32,16,768]{3,2,1,0:T(8,128)(2,1)}, u32[]{:S(2)}, u32[]{:S(2)}) %all-to-all-start.1) | async-done | bytes 12582944 | tf_op jit(solution)/shard_map/all_to_all | solution.py:54
  285.3 10.9 %copy.13 = bf16[32,16,16,768]{3,2,1,0:T(8,128)(2,1)} copy(bf16[32,16,16,768]{3,2,0,1:T(8,128)(2,1)} %bitcast.5) | data formatting | bytes 25165824 | tf_op jit(solution)/shard_map/transpose | solution.py:14
  296.2 49.3 %while.11 = (s32[]{:T(128)}, f32[32,256]{1,0:T(8,128)S(1)}, pred[32,256]{1,0:T(8,128)(4,1)S(1)}, bf16[32,256,768]{2,1,0:T(8,128)(2,1)}, s32[]{:T(128)}, /*index=5*/s32[]{:T(128)}) while((s32[]{:T(128)}, f32[32,256]{1,0:T(8,128)S(1)}, pred[32,256]{1,0:T(8,128)(4,1)S(1)}, bf16[32,256,768]{2,1,0:T(8,128)(2,1)}, s32[]{:T(128)}, ...), condition=%wide.region_4.5_spmd.clone, body=%wide.region_2.4_spmd.clone.sunk | while | flops 100990720 | bytes 397645 | solution.py:24
  297.8 1.4 fusion.34
  300.8 1.4 fusion.34
  303.9 1.4 fusion.34
  305.4 1.4 fusion.34
  308.5 1.4 fusion.34
  311.5 1.4 fusion.34
  313.1 1.4 fusion.34
  316.1 1.4 fusion.34
  319.2 1.6 fusion.34
  320.8 1.4 fusion.34
  323.9 1.5 fusion.34
  325.5 1.5 fusion.34
  328.6 1.5 fusion.34
  330.2 1.4 fusion.34
  331.7 1.5 fusion.34
  334.8 1.4 fusion.34
  337.8 1.5 fusion.34
  339.4 1.5 fusion.34
  341.0 1.4 fusion.34
  344.1 1.4 fusion.34
  345.8 59.8 %all_to_all.15 = f32[16,1,512]{2,1,0:T(1,128)S(1)} all-to-all(f32[16,1,512]{2,1,0:T(1,128)S(1)} %reshape.79), channel_id=1, replica_groups=mesh['groups'=2,'rows'=16] {'rows'}, dimensions={0} | all-to-all | bytes 65536 | tf_op jit(solution)/shard_map/all_to_all | solution.py:58
  407.0 2.8 fusion.18
  (103 shorter events, 23.3 us)
Async XLA Ops:
  0.0 20.1 %copy-start = (bf16[2048,768]{1,0:T(8,128)(2,1)S(1)}, bf16[2048,768]{1,0:T(8,128)(2,1)}, u32[]{:S(2)}) copy-start(bf16[2048,768]{1,0:T(8,128)(2,1)} %param.4) | copy-start | bytes 9437188
  7.6 47.9 %all-to-all-start = ((bf16[16,2,256]{2,1,0:T(2,128)(2,1)}), bf16[16,2,256]{2,1,0:T(2,128)(2,1)S(1)}, u32[]{:S(2)}, u32[]{:S(2)}) async-start(bf16[16,2,256]{2,1,0:T(2,128)(2,1)} %reshape.77), calls=%async_computation | async-start | bytes 32768 | tf_op jit(solution)/shard_map/all_to_all | solution.py:55
  55.5 229.8 %all-to-all-start.1 = ((bf16[16,32,16,768]{3,2,1,0:T(8,128)(2,1)}), bf16[16,32,16,768]{3,2,1,0:T(8,128)(2,1)}, u32[]{:S(2)}, u32[]{:S(2)}) async-start(bf16[16,32,16,768]{3,2,1,0:T(8,128)(2,1)} %bitcast.31), calls=%async_computation.1 | async-start | bytes 25165824 | tf_op jit(solution)/shard_map/all_to_all | solution.py:54
  285.3 121.7 %copy-start.1 = (s32[2048,1]{0,1:T(1,128)S(1)}, s32[2048,1]{0,1:T(1,128)}, u32[]{:S(2)}) copy-start(s32[2048,1]{0,1:T(1,128)} %param.5) | copy-start | bytes 24580
where the time goes:
time: 411 us; the launch traced here: 410 us
  waiting for transfers between devices  224 us (55%)
  blocking collectives  59.8 us (15%)
  matrix products  53 us (13%)
  local copies, waits for them, and re-layouts  50.1 us (12%)
  starting transfers between devices  13.4 us (3%)
  other arithmetic  9.23 us (2%)
    all_to_all x1, waiting for transfers between devices, local(): lax.all_to_all(outgoing, 'rows', split_axis=0, concat_axis=0, tiled=True)  224 us
    all_to_all x1, blocking collectives, local(): lax.all_to_all(best, 'rows', split_axis=0, concat_axis=0, tiled=True)  59.8 us
    dot_general x32, matrix products, one_cluster(): gram = jnp.dot(rows_of, rows_of.T, preferred_element_type=jnp.float32)  46.5 us
    gather x1, local copies, waits for them, and re-layouts, local(): outgoing = padded[member_idx].reshape(peers, owned, MOST, width)  34.5 us
    transpose x1, local copies, waits for them, and re-layouts, cluster_best(): members = jnp.transpose(blocks, (1, 0, 2, 3)).reshape(owned, slots, width)  10.9 us
  transfers between devices with their start and end apart: 2, of which 1 were waited for; matrix products, arithmetic and copies ran while one was open for 10% of the time, Pallas kernels for 0%

commit v1 on v0

v1 whole, which is shorter than its diff:
```python
import functools

import jax
import jax.numpy as jnp
from jax import lax
from jax.experimental import pallas as pl
from jax.experimental.pallas import tpu as pltpu
from jax.sharding import PartitionSpec as P

CLUSTERS = 512
MOST = 16
LANES = 128
SLACK = 32
EXACT = lax.Precision.HIGHEST
BF16, F32, I32 = jnp.bfloat16, jnp.float32, jnp.int32
VMEM_LIMIT = 48 * 1024 * 1024
NT = (((1,), (1,)), ((), ()))


def iota(shape, dim):
    return lax.broadcasted_iota(I32, shape, dim)


def one_hot(mask):
    return jnp.where(mask, jnp.float32(1), jnp.float32(0)).astype(BF16)


def whole(count):
    return [pl.BlockSpec(memory_space=pltpu.VMEM)] * count


def rank_kernel(label_ref, rank_ref, count_ref):
    step = 256
    tri = one_hot((iota((step, step + LANES), 0) < iota((step, step + LANES), 1)) | (iota((step, step + LANES), 1) >= step))
    ones = jnp.ones((count_ref.shape[0], step), BF16)
    running = jnp.zeros((CLUSTERS, LANES), F32)
    counts = jnp.zeros(count_ref.shape, F32)
    for at in range(0, label_ref.shape[1], step):
        hot = label_ref[:, at : at + step] == iota((CLUSTERS, step), 0)
        hot_bf = one_hot(hot)
        before = jnp.dot(hot_bf, tri, preferred_element_type=F32)
        here = before[:, :step] + jnp.concatenate([running] * (step // LANES), axis=1)
        rank_ref[:, at : at + step] = jnp.sum(jnp.where(hot, here, 0.0), axis=0, keepdims=True).astype(I32)
        running = running + before[:, step:]
        counts = counts + lax.dot_general(ones, hot_bf, NT, preferred_element_type=F32)
    count_ref[...] = counts


def ranks_and_counts(labels, peers):
    return pl.pallas_call(
        rank_kernel,
        out_shape=(
            jax.ShapeDtypeStruct(labels.shape, I32),
            jax.ShapeDtypeStruct((peers, CLUSTERS), F32),
        ),
        in_specs=whole(1),
        out_specs=tuple(whole(2)),
        name="ranks",
    )(labels)


def unit_kernel(rows_ref, unit_ref):
    values = rows_ref[...].astype(F32)
    total = jnp.sum(values * values, axis=1, keepdims=True)
    unit_ref[...] = (values * lax.rsqrt(total + 1e-06)).astype(BF16)


def unit_rows(embeddings):
    count, width = embeddings.shape
    step = min(512, count)
    spec = pl.BlockSpec((step, width), lambda i: (i, 0))
    return pl.pallas_call(
        unit_kernel,
        out_shape=jax.ShapeDtypeStruct((count, width), BF16),
        grid=(count // step,),
        in_specs=[spec],
        out_specs=spec,
        cost_estimate=pl.CostEstimate(flops=4 * count * width, bytes_accessed=4 * count * width, transcendentals=count),
        name="unit",
    )(embeddings)


def place_kernel(cap, me_ref, count_ref, label_ref, rank_ref, dest_ref, ends_ref, ends_t_ref, most_ref):
    me = me_ref[0]
    counts = count_ref[...]
    peers = counts.shape[0]
    square = (CLUSTERS, CLUSTERS)
    total = jnp.sum(counts, axis=0, keepdims=True)
    total_col = jnp.transpose(jnp.broadcast_to(total, (LANES, CLUSTERS)))[:, :1]
    first, second = iota(square, 0), iota(square, 1)
    ahead = (total_col > total) | ((total_col == total) & (first < second))
    ahead = jnp.where(ahead, jnp.float32(1), jnp.float32(0))
    turn = jnp.sum(ahead, axis=0, keepdims=True).astype(I32)
    turn_col = (CLUSTERS - 1) - jnp.sum(ahead, axis=1, keepdims=True).astype(I32)

    def owner_of(place):
        lap = place // peers
        spot = place - lap * peers
        return jnp.where(lap % 2 == 0, spot, peers - 1 - spot), lap

    owner, lap = owner_of(turn)
    owner_col, lap_col = owner_of(turn_col)
    earlier = one_hot((owner_col == owner) & (lap_col < lap))
    offset = jnp.dot(counts.astype(BF16), earlier, preferred_element_type=F32)
    ends = offset + counts
    most_ref[...] = jnp.broadcast_to(jnp.max(ends, axis=(0, 1), keepdims=True), most_ref.shape)

    mine = jnp.sum(jnp.where(iota(counts.shape, 0) == me, offset, 0.0), axis=0, keepdims=True).astype(I32)
    upper = mine // MOST
    table = jnp.concatenate([owner, upper, mine - upper * MOST] + [jnp.zeros_like(owner)] * 5, axis=0)
    table = table.astype(F32).astype(BF16)
    step = 512
    for at in range(0, label_ref.shape[1], step):
        hot = one_hot(label_ref[:, at : at + step] == iota((CLUSTERS, step), 0))
        found = jnp.dot(table, hot, preferred_element_type=F32).astype(I32)
        spot = found[1:2] * MOST + found[2:3] + rank_ref[:, at : at + step]
        dest_ref[:, at : at + step] = jnp.where(spot < cap, found[0:1] * cap + spot, -1)

    chosen = jnp.where((owner == me) & (lap == iota((LANES, CLUSTERS), 0)), jnp.float32(1), jnp.float32(0))
    never = jnp.float32(1 << 20)
    owned = CLUSTERS // peers
    own = lax.dot_general(ends, chosen, NT, precision=EXACT, preferred_element_type=F32)
    ends_ref[...] = jnp.where(iota(own.shape, 1) < owned, own, never)
    own_t = lax.dot_general(chosen, ends, NT, precision=EXACT, preferred_element_type=F32)
    ends_t_ref[...] = jnp.where(iota(own_t.shape, 0) < owned, own_t, never)


def places(me, counts, labels, ranks, cap):
    peers = counts.shape[0]
    return pl.pallas_call(
        functools.partial(place_kernel, cap),
        out_shape=(
            jax.ShapeDtypeStruct(labels.shape, I32),
            jax.ShapeDtypeStruct((peers, LANES), F32),
            jax.ShapeDtypeStruct((LANES, peers), F32),
            jax.ShapeDtypeStruct((8, LANES), F32),
        ),
        in_specs=[pl.BlockSpec(memory_space=pltpu.SMEM)] + whole(3),
        out_specs=tuple(whole(4)),
        name="places",
    )(me, counts, labels, ranks)


def pack_kernel(dest_ref, unit_ref, block_ref):
    rows = block_ref.shape[0]
    slots = iota((rows, dest_ref.shape[1]), 0) + pl.program_id(0) * rows
    pick = one_hot(dest_ref[...] == slots)
    block_ref[...] = jnp.dot(pick, unit_ref[...], preferred_element_type=F32).astype(BF16)


def packed(dest, unit, peers, cap):
    count, width = unit.shape
    rows = cap * 4
    return pl.pallas_call(
        pack_kernel,
        out_shape=jax.ShapeDtypeStruct((peers * cap, width), BF16),
        grid=(peers // 4,),
        in_specs=[pl.BlockSpec((1, count), lambda i: (0, 0)), pl.BlockSpec((count, width), lambda i: (0, 0))],
        out_specs=pl.BlockSpec((rows, width), lambda i: (i, 0)),
        compiler_params=pltpu.CompilerParams(vmem_limit_bytes=VMEM_LIMIT),
        name="pack",
    )(dest, unit)


def best_kernel(cap, ends_ref, ends_t_ref, rows_ref, best_ref):
    slots = rows_ref.shape[0]
    peers = ends_ref.shape[0]
    step = 512 if slots % 512 == 0 else 256

    def spread(place):
        sender = place // cap
        return sender, (place - sender * cap).astype(F32)

    sender, spot = spread(iota((peers, slots), 1))
    from_peer = jnp.where(sender == iota((peers, slots), 0), jnp.float32(1), jnp.float32(0))
    ends_row = jnp.dot(ends_t_ref[...], from_peer, precision=EXACT, preferred_element_type=F32)
    key_row = jnp.sum(jnp.where(ends_row <= spot[:1], 1.0, 0.0), axis=0, keepdims=True)
    sender, spot = spread(iota((slots, peers), 0))
    from_peer = jnp.where(sender == iota((slots, peers), 1), jnp.float32(1), jnp.float32(0))
    ends_col = jnp.dot(from_peer, ends_ref[...], precision=EXACT, preferred_element_type=F32)
    key_col = jnp.sum(jnp.where(ends_col <= spot[:, :1], 1.0, 0.0), axis=1, keepdims=True)

    for left in range(0, slots, step):
        columns = rows_ref[left : left + step, :]
        top = jnp.full((1, step), -1.0, F32)
        for upper in range(0, slots, step):
            gram = lax.dot_general(rows_ref[upper : upper + step, :], columns, NT, preferred_element_type=F32)
            keep = key_col[upper : upper + step] == key_row[:, left : left + step]
            if upper == left:
                keep = keep & (iota((step, step), 0) != iota((step, step), 1))
            top = jnp.maximum(top, jnp.max(jnp.where(keep, gram, -1.0), axis=0, keepdims=True))
        best_ref[:, left : left + step] = top


def bests(ends, ends_t, rows, cap):
    slots, width = rows.shape
    return pl.pallas_call(
        functools.partial(best_kernel, cap),
        out_shape=jax.ShapeDtypeStruct((1, slots), F32),
        in_specs=whole(3),
        out_specs=whole(1)[0],
        compiler_params=pltpu.CompilerParams(vmem_limit_bytes=VMEM_LIMIT),
        name="similar",
    )(ends, ends_t, rows)


def result_kernel(dest_ref, back_ref, out_ref):
    peers, cap = back_ref.shape
    back = back_ref[...]
    high = back.astype(BF16)
    rest = back - high.astype(F32)
    middle = rest.astype(BF16)
    low = (rest - middle.astype(F32)).astype(BF16)
    step = 512
    for at in range(0, dest_ref.shape[1], step):
        dest = dest_ref[:, at : at + step]
        owner = dest // cap
        hot = one_hot(dest - owner * cap == iota((cap, step), 0))
        parts = [jnp.dot(part, hot, preferred_element_type=F32) for part in (high, middle, low)]
        found = parts[0] + (parts[1] + parts[2])
        out_ref[:, at : at + step] = jnp.sum(jnp.where(owner == iota((peers, step), 0), found, 0.0), axis=0, keepdims=True)


def results(dest, back):
    return pl.pallas_call(
        result_kernel,
        out_shape=jax.ShapeDtypeStruct(dest.shape, F32),
        in_specs=whole(2),
        out_specs=whole(1)[0],
        name="results",
    )(dest, back)


def cluster_best(pair):
    blocks, flags = pair
    peers, owned, most, width = blocks.shape
    slots = peers * most
    members = jnp.transpose(blocks, (1, 0, 2, 3)).reshape(owned, slots, width)
    valid = jnp.transpose(flags, (1, 0, 2)).reshape(owned, slots) > 0.5
    off_diagonal = jnp.logical_not(jnp.eye(slots, dtype=bool))

    def one_cluster(item):
        rows_of, valid_of = item
        gram = jnp.dot(rows_of, rows_of.T, preferred_element_type=jnp.float32)
        keep = valid_of[None, :] & off_diagonal
        return jnp.max(jnp.where(keep, gram, jnp.float32(-1.0)), axis=1)

    best = lax.map(one_cluster, (members, valid))
    return jnp.transpose(best.reshape(owned, peers, most), (1, 0, 2))


def roomy(labels, ranks, unit):
    count, width = unit.shape
    peers = lax.axis_size("rows")
    owned = CLUSTERS // peers
    cluster_hot = (labels[:, None] == jnp.arange(CLUSTERS, dtype=I32)[None, :]).astype(F32)
    rank_hot = (ranks[:, None] == jnp.arange(MOST, dtype=I32)[None, :]).astype(F32)
    numbered = rank_hot * jnp.arange(1, count + 1, dtype=F32)[:, None]
    filled = jnp.dot(cluster_hot.T, rank_hot, precision=EXACT)
    member_idx = jnp.dot(cluster_hot.T, numbered, precision=EXACT).astype(I32) - 1
    member_idx = jnp.where(member_idx < 0, count, member_idx).reshape(CLUSTERS * MOST)
    padded = jnp.concatenate([unit, jnp.zeros((1, width), BF16)], axis=0)
    outgoing = padded[member_idx].reshape(peers, owned, MOST, width)
    occupied = filled.astype(BF16).reshape(peers, owned, MOST)
    best = cluster_best((exchange(outgoing), exchange(occupied)))
    table = exchange(best).reshape(CLUSTERS, MOST)
    per_row = jnp.dot(cluster_hot, table, precision=EXACT)
    return jnp.sum(per_row * rank_hot, axis=1)


def exchange(blocks):
    return lax.all_to_all(blocks, "rows", split_axis=0, concat_axis=0, tiled=True)


def local(embeddings, cluster_id):
    count, width = embeddings.shape
    peers = lax.axis_size("rows")
    cap = -(-(count // peers + SLACK) // 16) * 16
    labels = cluster_id.reshape(1, count)
    ranks, counts = ranks_and_counts(labels, peers)
    counts = exchange(counts.reshape(peers, 1, CLUSTERS)).reshape(peers, CLUSTERS)
    unit = unit_rows(embeddings)
    me = lax.axis_index("rows").reshape(1)
    dest, ends, ends_t, most = places(me, counts, labels, ranks, cap)
    arrived = exchange(packed(dest, unit, peers, cap).reshape(peers, cap, width))
    best = bests(ends, ends_t, arrived.reshape(peers * cap, width), cap)
    back = exchange(best.reshape(peers, 1, cap)).reshape(peers, cap)
    nearest = results(dest, back).reshape(count)
    return lax.cond(
        most[0, 0] > cap,
        lambda labels, ranks, unit, nearest: roomy(labels.reshape(count), ranks.reshape(count), unit),
        lambda labels, ranks, unit, nearest: nearest,
        labels, ranks, unit, nearest,
    )


def solution(mesh):
    return jax.shard_map(
        local,
        mesh=mesh,
        in_specs=(P(("groups", "rows"), None), P(("groups", "rows"), None)),
        out_specs=P(("groups", "rows")),
        check_vma=False,
    )
```

time: 411 us -> 150 us (0.36)
  waiting for transfers between devices: 224 us -> 8.26 us
  matrix products: 53 us -> 0 us
  local copies, waits for them, and re-layouts: 50.1 us -> 5.78 us
  Pallas kernels: 0 us -> 32.4 us
  blocking collectives: 59.8 us -> 90.4 us
  other arithmetic: 9.23 us -> 0.03 us
    all_to_all x2, waiting for transfers between devices: 224 us -> 8.26 us  [exchange(): lax.all_to_all(blocks, 'rows', split_axis=0, concat_axis=0, tiled=True)]
    dot_general x35 -> x0, matrix products: 53 us -> none  [the longest x32 46.5 us: one_cluster(): gram = jnp.dot(rows_of, rows_of.T, preferred_element_type=jnp.float32)]
    gather x1 -> x0, local copies, waits for them, and re-layouts: 34.5 us -> none  [local(): outgoing = padded[member_idx].reshape(peers, owned, MOST, width)]
    pallas_call x0 -> x6, Pallas kernels: none -> 32.4 us  [the longest x1 13.1 us: bests(): pl.pallas_call(functools.partial(best_kernel, cap), out_shape=jax.ShapeDt...]
    all_to_all x1, blocking collectives: 59.8 us -> 90.4 us  [exchange(): lax.all_to_all(blocks, 'rows', split_axis=0, concat_axis=0, tiled=True)]
    transpose x1 -> x0, local copies, waits for them, and re-layouts: 10.9 us -> none  [cluster_best(): members = jnp.transpose(blocks, (1, 0, 2, 3)).reshape(owned, slots, width)]
    reduce_sum x2 -> x0, other arithmetic: 7.85 us -> none  [the longest x1 5.28 us: local(): ranks = jnp.sum(same_before.astype(jnp.int32), axis=1)]
  transfers between devices with their start and end apart: 2 -> 2, of which waited for: 1 -> 2; matrix products, arithmetic and copies ran while one was open for 10% -> 1% of each run, Pallas kernels for 0% -> 2%
where the time goes in v1:
time: 150 us; the launch traced here: 149 us
  blocking collectives  90.4 us (60%)
  Pallas kernels  32.4 us (22%)
  starting transfers between devices  11.2 us (7%)
  waiting for transfers between devices  8.26 us (6%)
  local copies, waits for them, and re-layouts  5.78 us (4%)
    all_to_all x1, blocking collectives, exchange(): lax.all_to_all(blocks, 'rows', split_axis=0, concat_axis=0, tiled=True)  90.4 us
    pallas_call x1, Pallas kernels, bests(): pl.pallas_call(functools.partial(best_kernel, cap), out_shape=jax.ShapeDt...  13.1 us
    all_to_all x2, starting transfers between devices, exchange(): lax.all_to_all(blocks, 'rows', split_axis=0, concat_axis=0, tiled=True)  11.2 us
    pallas_call x1, Pallas kernels, packed(): pl.pallas_call(pack_kernel, out_shape=jax.ShapeDtypeStruct((peers * cap,...  8.81 us
    all_to_all x2, waiting for transfers between devices, exchange(): lax.all_to_all(blocks, 'rows', split_axis=0, concat_axis=0, tiled=True)  8.26 us
    pallas_call x1, Pallas kernels, ranks_and_counts(): pl.pallas_call(rank_kernel, out_shape=(jax.ShapeDtypeStruct(labels.shape,...  3.18 us
    pallas_call x1, Pallas kernels, places(): pl.pallas_call(functools.partial(place_kernel, cap), out_shape=(jax.Shape...  3.16 us
    pallas_call x1, Pallas kernels, unit_rows(): pl.pallas_call(unit_kernel, out_shape=jax.ShapeDtypeStruct((count, width)...  3.1 us
  transfers between devices with their start and end apart: 2, of which 2 were waited for; matrix products, arithmetic and copies ran while one was open for 1% of the time, Pallas kernels for 2%

profile of v1, /device:TPU:0, one launch (start us, length us, event | category | flops | bytes accessed | tf_op | source)
XLA Modules:
  0.0 148.8 jit_solution(2605615990811770035)
XLA Ops:
  0.0 0.0 copy-start.4
  0.0 3.2 %ranks.1 = (s32[1,2048]{1,0:T(1,128)S(1)}, f32[16,512]{1,0:T(8,128)}) custom-call(s32[1,2048]{1,0:T(1,128)} %bitcast.56), custom_call_target="tpu_custom_call" | custom-call | tf_op jit(solution)/shard_map/ranks/pallas_call | solution.py:50
  3.2 1.4 copy.19
  4.6 7.4 %all-to-all-start.3 = ((f32[16,1,512]{2,1,0:T(1,128)}), f32[16,1,512]{2,1,0:T(1,128)S(1)}, u32[]{:S(2)}, u32[]{:S(2)}) async-start(f32[16,1,512]{2,1,0:T(1,128)} %copy.19), calls=%async_computation.3 | async-start | bytes 65536 | tf_op jit(solution)/shard_map/all_to_all | solution.py:272
  12.0 3.1 %unit.1.unit_ref = bf16[2048,768]{1,0:T(8,128)(2,1)S(1)} custom-call(bf16[2048,768]{1,0:T(8,128)(2,1)} %rows_ref.1), custom_call_target="tpu_custom_call" | custom-call | flops 6291456 | bytes 6291456 | tf_op jit(solution)/shard_map/unit/pallas_call | solution.py:72
  15.1 0.0 copy-start.3
  15.1 3.5 %all-to-all-done.3 = f32[16,1,512]{2,1,0:T(1,128)S(1)} async-done(((f32[16,1,512]{2,1,0:T(1,128)}), f32[16,1,512]{2,1,0:T(1,128)S(1)}, u32[]{:S(2)}, u32[]{:S(2)}) %all-to-all-start.3) | async-done | bytes 32800 | tf_op jit(solution)/shard_map/all_to_all | solution.py:272
  18.6 0.6 copy.27
  19.2 0.0 copy-done.4
  19.2 3.2 %places.1 = (s32[1,2048]{1,0:T(1,128)}, f32[16,128]{1,0:T(8,128)}, f32[128,16]{1,0:T(8,128)}, f32[8,128]{1,0:T(8,128)}) custom-call(s32[1]{0:T(128)} %bitcast.11.me_ref, f32[16,512]{1,0:T(8,128)} %bitcast.53, s32[1,2048]{1,0:T(1,128)S(1)} %bitcast.57, s32[1,2048]{1,0:T(1,128)S(1)} %get-tuple-element.54.rank_ref), custom_call_target="tpu_custom_call" | custom-call | tf_op jit(solution)/shard_map/places/pallas_call | solution.py:130
  22.4 0.0 copy-start.1
  22.4 0.7 copy-done.1
  23.1 8.8 %pack.1 = bf16[2560,768]{1,0:T(8,128)(2,1)S(1)} custom-call(s32[1,2048]{1,0:T(1,128)S(1)} %copy-done.1, bf16[2048,768]{1,0:T(8,128)(2,1)S(1)} %unit.1.unit_ref), custom_call_target="tpu_custom_call" | custom-call | tf_op jit(solution)/shard_map/pack/pallas_call | solution.py:154
  31.9 0.0 copy-start
  31.9 0.0 copy-start.2
  31.9 90.4 %all_to_all.28 = bf16[16,160,768]{2,1,0:T(8,128)(2,1)S(1)} all-to-all(bf16[16,160,768]{2,1,0:T(8,128)(2,1)S(1)} %bitcast.46), channel_id=1, replica_groups=mesh['groups'=2,'rows'=16] {'rows'}, dimensions={0} | all-to-all | bytes 7864320 | tf_op jit(solution)/shard_map/all_to_all | solution.py:272
  122.3 0.0 copy-done.3
  122.3 0.0 copy-done
  122.3 0.0 copy-done.2
  122.3 13.1 %similar.1 = f32[1,2560]{1,0:T(1,128)S(1)} custom-call(f32[16,128]{1,0:T(8,128)S(1)} %copy-done.2, f32[128,16]{1,0:T(8,128)S(1)} %copy-done, bf16[2560,768]{1,0:T(8,128)(2,1)S(1)} %bitcast.45), custom_call_target="tpu_custom_call" | custom-call | tf_op jit(solution)/shard_map/similar/pallas_call | solution.py:197
  135.5 0.7 reshape.106
  136.1 3.8 %all-to-all-start.5 = ((f32[16,1,160]{2,1,0:T(1,128)}), f32[16,1,160]{2,1,0:T(1,128)S(1)}, u32[]{:S(2)}, u32[]{:S(2)}) async-start(f32[16,1,160]{2,1,0:T(1,128)} %reshape.106), calls=%async_computation.5 | async-start | bytes 32768 | tf_op jit(solution)/shard_map/all_to_all | solution.py:272
  140.0 1.2 slice.3
  141.7 4.8 %all-to-all-done.5 = f32[16,1,160]{2,1,0:T(1,128)S(1)} async-done(((f32[16,1,160]{2,1,0:T(1,128)}), f32[16,1,160]{2,1,0:T(1,128)S(1)}, u32[]{:S(2)}, u32[]{:S(2)}) %all-to-all-start.5) | async-done | bytes 10272 | tf_op jit(solution)/shard_map/all_to_all | solution.py:272
  146.5 0.6 copy.28
  147.1 1.1 results.1
  148.2 0.0 copy-start.5
  148.3 0.6 copy-done.5
  (2 shorter events, 0.0 us)
Async XLA Ops:
  0.0 19.2 %copy-start.4 = (s32[2048,1]{0,1:T(1,128)S(1)}, s32[2048,1]{0,1:T(1,128)}, u32[]{:S(2)}) copy-start(s32[2048,1]{0,1:T(1,128)} %param.7) | copy-start | bytes 24580
  4.6 14.0 %all-to-all-start.3 = ((f32[16,1,512]{2,1,0:T(1,128)}), f32[16,1,512]{2,1,0:T(1,128)S(1)}, u32[]{:S(2)}, u32[]{:S(2)}) async-start(f32[16,1,512]{2,1,0:T(1,128)} %copy.19), calls=%async_computation.3 | async-start | bytes 65536 | tf_op jit(solution)/shard_map/all_to_all | solution.py:272
  15.1 107.3 %copy-start.3 = (bf16[2048,768]{1,0:T(8,128)(2,1)}, bf16[2048,768]{1,0:T(8,128)(2,1)S(1)}, u32[]{:S(2)}) copy-start(bf16[2048,768]{1,0:T(8,128)(2,1)S(1)} %unit.1.unit_ref) | copy-start | bytes 9437188
  22.4 0.7 copy-start.1
  31.9 90.4 %copy-start = (f32[128,16]{1,0:T(8,128)S(1)}, f32[128,16]{1,0:T(8,128)}, u32[]{:S(2)}) copy-start(f32[128,16]{1,0:T(8,128)} %get-tuple-element.58.ends_t_ref) | copy-start | bytes 24580
  31.9 90.4 %copy-start.2 = (f32[16,128]{1,0:T(8,128)S(1)}, f32[16,128]{1,0:T(8,128)}, u32[]{:S(2)}) copy-start(f32[16,128]{1,0:T(8,128)} %get-tuple-element.57.ends_ref) | copy-start | bytes 24580
  136.1 10.3 %all-to-all-start.5 = ((f32[16,1,160]{2,1,0:T(1,128)}), f32[16,1,160]{2,1,0:T(1,128)S(1)}, u32[]{:S(2)}, u32[]{:S(2)}) async-start(f32[16,1,160]{2,1,0:T(1,128)} %reshape.106), calls=%async_computation.5 | async-start | bytes 32768 | tf_op jit(solution)/shard_map/all_to_all | solution.py:272
  148.2 0.6 copy-start.5

commit v2 on v1

--- a/solution.py
+++ b/solution.py
@@ -10,7 +10,8 @@
 CLUSTERS = 512
 MOST = 16
 LANES = 128
-SLACK = 32
+SLACK = 16
+ROUNDS = 8
 EXACT = lax.Precision.HIGHEST
 BF16, F32, I32 = jnp.bfloat16, jnp.float32, jnp.int32
 VMEM_LIMIT = 48 * 1024 * 1024
@@ -29,32 +30,45 @@
     return [pl.BlockSpec(memory_space=pltpu.VMEM)] * count
 
 
-def rank_kernel(label_ref, rank_ref, count_ref):
+def count_kernel(label_ref, count_ref):
+    step = 512
+    ones = jnp.ones((count_ref.shape[0], step), BF16)
+    counts = jnp.zeros((count_ref.shape[0], CLUSTERS), F32)
+    for at in range(0, label_ref.shape[1], step):
+        hot = one_hot(label_ref[:, at : at + step] == iota((CLUSTERS, step), 0))
+        counts = counts + lax.dot_general(ones, hot, NT, preferred_element_type=F32)
+    count_ref[:, 0, :] = counts
+
+
+def counted(labels, peers):
+    return pl.pallas_call(
+        count_kernel,
+        out_shape=jax.ShapeDtypeStruct((peers, 1, CLUSTERS), F32),
+        in_specs=whole(1),
+        out_specs=whole(1)[0],
+        name="counts",
+    )(labels)
+
+
+def rank_kernel(label_ref, rank_ref):
     step = 256
     tri = one_hot((iota((step, step + LANES), 0) < iota((step, step + LANES), 1)) | (iota((step, step + LANES), 1) >= step))
-    ones = jnp.ones((count_ref.shape[0], step), BF16)
     running = jnp.zeros((CLUSTERS, LANES), F32)
-    counts = jnp.zeros(count_ref.shape, F32)
     for at in range(0, label_ref.shape[1], step):
         hot = label_ref[:, at : at + step] == iota((CLUSTERS, step), 0)
-        hot_bf = one_hot(hot)
-        before = jnp.dot(hot_bf, tri, preferred_element_type=F32)
+        before = jnp.dot(one_hot(hot), tri, preferred_element_type=F32)
         here = before[:, :step] + jnp.concatenate([running] * (step // LANES), axis=1)
         rank_ref[:, at : at + step] = jnp.sum(jnp.where(hot, here, 0.0), axis=0, keepdims=True).astype(I32)
         running = running + before[:, step:]
-        counts = counts + lax.dot_general(ones, hot_bf, NT, preferred_element_type=F32)
-    count_ref[...] = counts
-
-
-def ranks_and_counts(labels, peers):
+
+
+def ranked(labels):
     return pl.pallas_call(
         rank_kernel,
-        out_shape=(
-            jax.ShapeDtypeStruct(labels.shape, I32),
-            jax.ShapeDtypeStruct((peers, CLUSTERS), F32),
-        ),
+        out_shape=jax.ShapeDtypeStruct(labels.shape, I32),
         in_specs=whole(1),
-        out_specs=tuple(whole(2)),
+        out_specs=whole(1)[0],
+        cost_estimate=pl.CostEstimate(flops=labels.shape[1] * CLUSTERS * 8, bytes_accessed=1 << 22, transcendentals=0),
         name="ranks",
     )(labels)
 
@@ -80,43 +94,79 @@
     )(embeddings)
 
 
+def swapped_evenly(table, peers):
+    pieces = [table[:, at : at + LANES] for at in range(0, CLUSTERS, LANES)]
+    lane = iota((1, LANES), 1)
+
+    def over_laps(parts, combine):
+        found = functools.reduce(combine, parts)
+        shift = peers
+        while shift < LANES:
+            found = combine(found, pltpu.roll(found, shift, 1))
+            shift *= 2
+        return found
+
+    bits = [1 << i for i in range(peers.bit_length() - 1)]
+    for bit in (bits * ROUNDS)[:ROUNDS]:
+
+        def partner(x):
+            return jnp.where((lane & bit) == 0, pltpu.roll(x, LANES - bit, 1), pltpu.roll(x, bit, 1))
+
+        load = over_laps([piece[:peers] for piece in pieces], jnp.add)
+        excess = load - partner(load)
+        others = [partner(piece) for piece in pieces]
+        gains = []
+        for piece, other in zip(pieces, others):
+            moved = piece[:peers] - other[:peers]
+            gains.append(jnp.sum(moved * (excess - moved), axis=0, keepdims=True))
+        best = over_laps(gains, jnp.maximum)
+        pieces = [
+            jnp.where((gain == best) & (gain > 0.0), other, piece) for gain, other, piece in zip(gains, others, pieces)
+        ]
+    return jnp.concatenate(pieces, axis=1)
+
+
 def place_kernel(cap, me_ref, count_ref, label_ref, rank_ref, dest_ref, ends_ref, ends_t_ref, most_ref):
     me = me_ref[0]
-    counts = count_ref[...]
+    counts = count_ref[:, 0, :]
     peers = counts.shape[0]
     square = (CLUSTERS, CLUSTERS)
     total = jnp.sum(counts, axis=0, keepdims=True)
     total_col = jnp.transpose(jnp.broadcast_to(total, (LANES, CLUSTERS)))[:, :1]
     first, second = iota(square, 0), iota(square, 1)
     ahead = (total_col > total) | ((total_col == total) & (first < second))
-    ahead = jnp.where(ahead, jnp.float32(1), jnp.float32(0))
-    turn = jnp.sum(ahead, axis=0, keepdims=True).astype(I32)
-    turn_col = (CLUSTERS - 1) - jnp.sum(ahead, axis=1, keepdims=True).astype(I32)
-
-    def owner_of(place):
-        lap = place // peers
-        spot = place - lap * peers
-        return jnp.where(lap % 2 == 0, spot, peers - 1 - spot), lap
-
-    owner, lap = owner_of(turn)
-    owner_col, lap_col = owner_of(turn_col)
-    earlier = one_hot((owner_col == owner) & (lap_col < lap))
+    turn = (CLUSTERS - 1) - jnp.sum(jnp.where(ahead, 1.0, 0.0), axis=1, keepdims=True).astype(I32)
+    lap = turn // peers
+    spot = turn - lap * peers
+    place = lap * peers + jnp.where(lap % 2 == 0, spot, peers - 1 - spot)
+    number = iota((8, CLUSTERS), 1)
+    digits = jnp.where(iota((8, CLUSTERS), 0) == 0, number // MOST, number % MOST).astype(F32)
+    table = jnp.concatenate([counts, digits], axis=0).astype(BF16)
+    table = jnp.dot(table, one_hot(place == second), preferred_element_type=F32)
+    table = swapped_evenly(table, peers)
+
+    counts = table[:peers]
+    cluster = table[peers : peers + 1] * MOST + table[peers + 1 : peers + 2]
+    cluster_col = jnp.transpose(jnp.broadcast_to(cluster, (LANES, CLUSTERS)))[:, :1].astype(I32)
+    earlier = one_hot((first % peers == second % peers) & (first // peers < second // peers))
     offset = jnp.dot(counts.astype(BF16), earlier, preferred_element_type=F32)
     ends = offset + counts
     most_ref[...] = jnp.broadcast_to(jnp.max(ends, axis=(0, 1), keepdims=True), most_ref.shape)
 
     mine = jnp.sum(jnp.where(iota(counts.shape, 0) == me, offset, 0.0), axis=0, keepdims=True).astype(I32)
     upper = mine // MOST
-    table = jnp.concatenate([owner, upper, mine - upper * MOST] + [jnp.zeros_like(owner)] * 5, axis=0)
-    table = table.astype(F32).astype(BF16)
+    lane = iota((1, CLUSTERS), 1)
+    find = jnp.concatenate([lane % peers, upper, mine - upper * MOST] + [jnp.zeros_like(mine)] * 5, axis=0)
+    find = find.astype(F32).astype(BF16)
     step = 512
     for at in range(0, label_ref.shape[1], step):
-        hot = one_hot(label_ref[:, at : at + step] == iota((CLUSTERS, step), 0))
-        found = jnp.dot(table, hot, preferred_element_type=F32).astype(I32)
-        spot = found[1:2] * MOST + found[2:3] + rank_ref[:, at : at + step]
-        dest_ref[:, at : at + step] = jnp.where(spot < cap, found[0:1] * cap + spot, -1)
-
-    chosen = jnp.where((owner == me) & (lap == iota((LANES, CLUSTERS), 0)), jnp.float32(1), jnp.float32(0))
+        hot = one_hot(label_ref[:, at : at + step] == cluster_col)
+        found = jnp.dot(find, hot, preferred_element_type=F32).astype(I32)
+        slot = found[1:2] * MOST + found[2:3] + rank_ref[:, at : at + step]
+        dest_ref[:, at : at + step] = jnp.where(slot < cap, found[0:1] * cap + slot, -1)
+
+    chosen = lane == iota((LANES, CLUSTERS), 0) * peers + me
+    chosen = jnp.where(chosen, jnp.float32(1), jnp.float32(0))
     never = jnp.float32(1 << 20)
     owned = CLUSTERS // peers
     own = lax.dot_general(ends, chosen, NT, precision=EXACT, preferred_element_type=F32)
@@ -162,51 +212,125 @@
     )(dest, unit)
 
 
-def best_kernel(cap, ends_ref, ends_t_ref, rows_ref, best_ref):
-    slots = rows_ref.shape[0]
+def chunk_depth(peers, cap):
+    return max(deep for deep in range(16, cap + 1, 16) if cap % deep == 0 and (deep == 16 or deep * peers <= 1024))
+
+
+def key_kernel(cap, deep, ends_ref, ends_t_ref, row_ref, col_ref, meet_ref):
     peers = ends_ref.shape[0]
-    step = 512 if slots % 512 == 0 else 256
-
-    def spread(place):
-        sender = place // cap
-        return sender, (place - sender * cap).astype(F32)
-
-    sender, spot = spread(iota((peers, slots), 1))
+    owned = CLUSTERS // peers
+    size = peers * deep
+    chunks = cap // deep
+    slots = peers * cap
+
+    def spread(shape, dim):
+        index = iota(shape, dim)
+        chunk = index // size
+        within = index - chunk * size
+        sender = within // deep
+        return sender, (chunk * deep + within - sender * deep).astype(F32)
+
+    sender, spot = spread((peers, slots), 1)
     from_peer = jnp.where(sender == iota((peers, slots), 0), jnp.float32(1), jnp.float32(0))
-    ends_row = jnp.dot(ends_t_ref[...], from_peer, precision=EXACT, preferred_element_type=F32)
-    key_row = jnp.sum(jnp.where(ends_row <= spot[:1], 1.0, 0.0), axis=0, keepdims=True)
-    sender, spot = spread(iota((slots, peers), 0))
+    ends = jnp.dot(ends_t_ref[...], from_peer, precision=EXACT, preferred_element_type=F32)
+    row = jnp.sum(jnp.where(ends <= spot[:1], 1.0, 0.0), axis=0, keepdims=True)
+    sender, spot = spread((slots, peers), 0)
     from_peer = jnp.where(sender == iota((slots, peers), 1), jnp.float32(1), jnp.float32(0))
-    ends_col = jnp.dot(from_peer, ends_ref[...], precision=EXACT, preferred_element_type=F32)
-    key_col = jnp.sum(jnp.where(ends_col <= spot[:, :1], 1.0, 0.0), axis=1, keepdims=True)
-
-    for left in range(0, slots, step):
-        columns = rows_ref[left : left + step, :]
-        top = jnp.full((1, step), -1.0, F32)
-        for upper in range(0, slots, step):
-            gram = lax.dot_general(rows_ref[upper : upper + step, :], columns, NT, preferred_element_type=F32)
-            keep = key_col[upper : upper + step] == key_row[:, left : left + step]
-            if upper == left:
-                keep = keep & (iota((step, step), 0) != iota((step, step), 1))
-            top = jnp.maximum(top, jnp.max(jnp.where(keep, gram, -1.0), axis=0, keepdims=True))
-        best_ref[:, left : left + step] = top
-
-
-def bests(ends, ends_t, rows, cap):
-    slots, width = rows.shape
-    return pl.pallas_call(
-        functools.partial(best_kernel, cap),
-        out_shape=jax.ShapeDtypeStruct((1, slots), F32),
-        in_specs=whole(3),
+    ends = jnp.dot(from_peer, ends_ref[...], precision=EXACT, preferred_element_type=F32)
+    col = jnp.sum(jnp.where(ends <= spot[:, :1], 1.0, 0.0), axis=1, keepdims=True)
+    lows, highs = [], []
+    for chunk in range(chunks):
+        part = row[:, chunk * size : (chunk + 1) * size]
+        row_ref[chunk] = part
+        col_ref[chunk] = col[chunk * size : (chunk + 1) * size]
+        lows.append(jnp.min(part))
+        highs.append(jnp.max(jnp.where(part < owned, part, -1.0)))
+    for left in range(chunks):
+        for right in range(left, chunks):
+            overlap = (lows[left] <= highs[right]) & (lows[right] <= highs[left])
+            meet_ref[left * chunks + right] = jnp.where(overlap, 1, 0)
+
+
+def keys(ends, ends_t, cap, deep):
+    peers = ends.shape[0]
+    chunks, size = cap // deep, peers * deep
+    return pl.pallas_call(
+        functools.partial(key_kernel, cap, deep),
+        out_shape=(
+            jax.ShapeDtypeStruct((chunks, 1, size), F32),
+            jax.ShapeDtypeStruct((chunks, size, 1), F32),
+            jax.ShapeDtypeStruct((chunks * chunks,), I32),
+        ),
+        in_specs=whole(2),
+        out_specs=tuple(whole(2) + [pl.BlockSpec(memory_space=pltpu.SMEM)]),
+        cost_estimate=pl.CostEstimate(flops=1 << 28, bytes_accessed=1 << 22, transcendentals=0),
+        compiler_params=pltpu.CompilerParams(vmem_limit_bytes=VMEM_LIMIT),
+        name="keys",
+    )(ends, ends_t)
+
+
+def best_kernel(deep, meet_ref, row_ref, col_ref, rows_ref, best_ref, held, top, side, arrived):
+    peers, cap, width = rows_ref.shape
+    chunks, size = held.shape[0], peers * deep
+    step = 256
+    copies = []
+    for chunk in range(chunks):
+        copy = pltpu.make_async_copy(rows_ref.at[:, pl.ds(chunk * deep, deep), :], held.at[chunk], arrived.at[chunk])
+        copy.start()
+        copies.append(copy)
+    top[...] = jnp.full(top.shape, -1.0, F32)
+    side[...] = jnp.full(side.shape, -1.0, F32)
+    for right in range(chunks):
+        copies[right].wait()
+
+        def with_left(left, carry):
+            @pl.when(meet_ref[left * chunks + right] == 1)
+            def _():
+                upper = held[left].reshape(size, width)
+                key_col = col_ref[left]
+                for at in range(0, size, step):
+                    lower = held[right].reshape(size, width)[at : at + step]
+                    gram = lax.dot_general(upper, lower, NT, preferred_element_type=F32)
+                    keep = key_col == row_ref[right, :, at : at + step]
+                    same = iota((size, step), 0) - iota((size, step), 1) == jnp.where(left == right, at, -size)
+                    gram = jnp.where(keep & jnp.logical_not(same), gram, -1.0)
+                    top[right, :, at : at + step] = jnp.maximum(
+                        top[right, :, at : at + step], jnp.max(gram, axis=0, keepdims=True)
+                    )
+                    halves = [gram[:, i : i + LANES] for i in range(0, step, LANES)]
+                    side[left] = functools.reduce(jnp.maximum, halves, side[left])
+
+            return carry
+
+        lax.fori_loop(0, right + 1, with_left, 0)
+    for chunk in range(chunks):
+        found = jnp.maximum(top[chunk], jnp.max(jnp.transpose(side[chunk]), axis=0, keepdims=True))
+        for sender in range(peers):
+            best_ref[sender, :, chunk * deep : (chunk + 1) * deep] = found[:, sender * deep : (sender + 1) * deep]
+
+
+def bests(meet, key_row, key_col, rows, deep):
+    peers, cap, width = rows.shape
+    chunks, size = cap // deep, peers * deep
+    return pl.pallas_call(
+        functools.partial(best_kernel, deep),
+        out_shape=jax.ShapeDtypeStruct((peers, 1, cap), F32),
+        in_specs=[pl.BlockSpec(memory_space=pltpu.SMEM)] + whole(2) + [pl.BlockSpec(memory_space=pl.ANY)],
         out_specs=whole(1)[0],
+        scratch_shapes=[
+            pltpu.VMEM((chunks, peers, deep, width), BF16),
+            pltpu.VMEM((chunks, 1, size), F32),
+            pltpu.VMEM((chunks, size, LANES), F32),
+            pltpu.SemaphoreType.DMA((chunks,)),
+        ],
         compiler_params=pltpu.CompilerParams(vmem_limit_bytes=VMEM_LIMIT),
         name="similar",
-    )(ends, ends_t, rows)
+    )(meet, key_row, key_col, rows)
 
 
 def result_kernel(dest_ref, back_ref, out_ref):
-    peers, cap = back_ref.shape
-    back = back_ref[...]
+    peers, _, cap = back_ref.shape
+    back = back_ref[:, 0, :]
     high = back.astype(BF16)
     rest = back - high.astype(F32)
     middle = rest.astype(BF16)
@@ -276,15 +400,16 @@
     count, width = embeddings.shape
     peers = lax.axis_size("rows")
     cap = -(-(count // peers + SLACK) // 16) * 16
+    deep = chunk_depth(peers, cap)
     labels = cluster_id.reshape(1, count)
-    ranks, counts = ranks_and_counts(labels, peers)
-    counts = exchange(counts.reshape(peers, 1, CLUSTERS)).reshape(peers, CLUSTERS)
+    counts = exchange(counted(labels, peers))
+    ranks = ranked(labels)
     unit = unit_rows(embeddings)
     me = lax.axis_index("rows").reshape(1)
     dest, ends, ends_t, most = places(me, counts, labels, ranks, cap)
     arrived = exchange(packed(dest, unit, peers, cap).reshape(peers, cap, width))
-    best = bests(ends, ends_t, arrived.reshape(peers * cap, width), cap)
-    back = exchange(best.reshape(peers, 1, cap)).reshape(peers, cap)
+    key_row, key_col, meet = keys(ends, ends_t, cap, deep)
+    back = exchange(bests(meet, key_row, key_col, arrived, deep))
     nearest = results(dest, back).reshape(count)
     return lax.cond(
         most[0, 0] > cap,

time: 150 us -> 141 us (0.940)
  blocking collectives: 90.4 us -> 0 us
  waiting for transfers between devices: 8.26 us -> 67.3 us
  starting transfers between devices: 11.2 us -> 28.3 us
  Pallas kernels: 32.4 us -> 36.1 us
  local copies, waits for them, and re-layouts: 5.78 us -> 7.49 us
    all_to_all x1 -> x0, blocking collectives: 90.4 us -> none  [exchange(): lax.all_to_all(blocks, 'rows', split_axis=0, concat_axis=0, tiled=True)]
    all_to_all x2 -> x3, waiting for transfers between devices: 8.26 us -> 67.3 us  [exchange(): lax.all_to_all(blocks, 'rows', split_axis=0, concat_axis=0, tiled=True)]
    all_to_all x2 -> x3, starting transfers between devices: 11.2 us -> 28.3 us  [exchange(): lax.all_to_all(blocks, 'rows', split_axis=0, concat_axis=0, tiled=True)]
    pallas_call x1, Pallas kernels: 3.16 us -> 7.5 us  [places(): pl.pallas_call(functools.partial(place_kernel, cap), out_shape=(jax.Shape...]
    unnamed x14 -> x22, local copies, waits for them, and re-layouts: 2.51 us -> 6.32 us
    reshape x2 -> x0, local copies, waits for them, and re-layouts: 2.09 us -> none  [the longest x1 1.4 us: local(): counts.reshape(peers, 1, CLUSTERS)]
    pallas_call x2 -> x4, Pallas kernels: 16.3 us -> 15.4 us  [the longest x1 8.72 us: bests(): pl.pallas_call(functools.partial(best_kernel, deep), out_shape=jax.ShapeD...]
  transfers between devices with their start and end apart: 2 -> 3, of which waited for: 2 -> 3; matrix products, arithmetic and copies ran while one was open for 1% -> 1% of each run, Pallas kernels for 2% -> 6%
where the time goes in v2:
time: 141 us; the launch traced here: 140 us
  waiting for transfers between devices  67.3 us (48%)
  Pallas kernels  36.1 us (26%)
  starting transfers between devices  28.3 us (20%)
  local copies, waits for them, and re-layouts  7.49 us (5%)
    all_to_all x3, waiting for transfers between devices, exchange(): lax.all_to_all(blocks, 'rows', split_axis=0, concat_axis=0, tiled=True)  67.3 us
    all_to_all x3, starting transfers between devices, exchange(): lax.all_to_all(blocks, 'rows', split_axis=0, concat_axis=0, tiled=True)  28.3 us
    pallas_call x1, Pallas kernels, packed(): pl.pallas_call(pack_kernel, out_shape=jax.ShapeDtypeStruct((peers * cap,...  8.94 us
    pallas_call x1, Pallas kernels, bests(): pl.pallas_call(functools.partial(best_kernel, deep), out_shape=jax.ShapeD...  8.72 us
    pallas_call x1, Pallas kernels, places(): pl.pallas_call(functools.partial(place_kernel, cap), out_shape=(jax.Shape...  7.5 us
    unnamed x22, local copies, waits for them, and re-layouts  6.32 us
    pallas_call x1, Pallas kernels, keys(): pl.pallas_call(functools.partial(key_kernel, cap, deep), out_shape=(jax.S...  3.22 us
    pallas_call x1, Pallas kernels, unit_rows(): pl.pallas_call(unit_kernel, out_shape=jax.ShapeDtypeStruct((count, width)...  3.1 us
  transfers between devices with their start and end apart: 3, of which 3 were waited for; matrix products, arithmetic and copies ran while one was open for 1% of the time, Pallas kernels for 6%

profile of v2, /device:TPU:0, one launch (start us, length us, event | category | flops | bytes accessed | tf_op | source)
XLA Modules:
  0.0 139.9 jit_solution(3335758684896966713)
XLA Ops:
  0.0 0.0 copy-start.8
  0.0 2.0 %counts.1 = f32[16,1,512]{2,1,0:T(1,128)} custom-call(s32[1,2048]{1,0:T(1,128)} %bitcast.44), custom_call_target="tpu_custom_call" | custom-call | tf_op jit(solution)/shard_map/counts/pallas_call | solution.py:44
  2.0 7.4 %all-to-all-start.3 = ((f32[16,1,512]{2,1,0:T(1,128)}), f32[16,1,512]{2,1,0:T(1,128)S(1)}, u32[]{:S(2)}, u32[]{:S(2)}) async-start(f32[16,1,512]{2,1,0:T(1,128)} %counts.1), calls=%async_computation.3 | async-start | bytes 65536 | tf_op jit(solution)/shard_map/all_to_all | solution.py:396
  9.4 3.1 %unit.1.unit_ref = bf16[2048,768]{1,0:T(8,128)(2,1)S(1)} custom-call(bf16[2048,768]{1,0:T(8,128)(2,1)} %rows_ref.1), custom_call_target="tpu_custom_call" | custom-call | flops 6291456 | bytes 6291456 | tf_op jit(solution)/shard_map/unit/pallas_call | solution.py:86
  12.5 0.0 copy-done.8
  12.6 0.0 copy-start.5
  12.6 1.4 ranks.1.rank_ref
  14.0 0.0 copy-start.10
  14.0 2.1 %all-to-all-done.3.count_ref = f32[16,1,512]{2,1,0:T(1,128)S(1)} async-done(((f32[16,1,512]{2,1,0:T(1,128)}), f32[16,1,512]{2,1,0:T(1,128)S(1)}, u32[]{:S(2)}, u32[]{:S(2)}) %all-to-all-start.3) | async-done | bytes 32800 | tf_op jit(solution)/shard_map/all_to_all | solution.py:396
  16.1 0.6 copy-done.6
  16.7 7.5 %places.1 = (s32[1,2048]{1,0:T(1,128)}, f32[16,128]{1,0:T(8,128)}, f32[128,16]{1,0:T(8,128)}, f32[8,128]{1,0:T(8,128)}) custom-call(s32[1]{0:T(128)} %bitcast.11.me_ref, f32[16,1,512]{2,1,0:T(1,128)} %copy-done.6, s32[1,2048]{1,0:T(1,128)S(1)} %bitcast.46, s32[1,2048]{1,0:T(1,128)S(1)} %ranks.1.rank_ref), custom_call_target="tpu_custom_call" | custom-call | tf_op jit(solution)/shard_map/places/pallas_call | solution.py:180
  24.2 0.7 copy-done.2
  24.9 8.9 %pack.1 = bf16[2304,768]{1,0:T(8,128)(2,1)} custom-call(s32[1,2048]{1,0:T(1,128)S(1)} %copy-done.2, bf16[2048,768]{1,0:T(8,128)(2,1)S(1)} %unit.1.unit_ref), custom_call_target="tpu_custom_call" | custom-call | tf_op jit(solution)/shard_map/pack/pallas_call | solution.py:204
  33.8 0.0 copy-done.5
  33.8 0.0 copy-done.10
  33.8 3.9 %all-to-all-start.4 = ((bf16[16,144,768]{2,1,0:T(8,128)(2,1)}), bf16[16,144,768]{2,1,0:T(8,128)(2,1)S(1)}, u32[]{:S(2)}, u32[]{:S(2)}) async-start(bf16[16,144,768]{2,1,0:T(8,128)(2,1)} %bitcast.14), calls=%async_computation.4 | async-start | bytes 7077888 | tf_op jit(solution)/shard_map/all_to_all | solution.py:396
  37.7 0.0 copy-start.3
  37.7 0.8 copy-done.3
  38.6 0.7 copy-done.4
  39.3 3.2 %keys.1 = (f32[3,1,768]{2,1,0:T(1,128)S(1)}, f32[3,768,1]{2,1,0:T(8,128)S(1)}, s32[9]{0:T(128)S(1)}) custom-call(f32[16,128]{1,0:T(8,128)S(1)} %copy-done.4, f32[128,16]{1,0:T(8,128)S(1)} %copy-done.3), custom_call_target="tpu_custom_call" | custom-call | flops 268435456 | bytes 4194304 | tf_op jit(solution)/shard_map/keys/pallas_call | solution.py:257
  42.5 0.0 copy-start
  42.5 1.0 copy-done
  43.5 60.4 %all-to-all-done.4.rows_ref = bf16[16,144,768]{2,1,0:T(8,128)(2,1)S(1)} async-done(((bf16[16,144,768]{2,1,0:T(8,128)(2,1)}), bf16[16,144,768]{2,1,0:T(8,128)(2,1)S(1)}, u32[]{:S(2)}, u32[]{:S(2)}) %all-to-all-start.4) | async-done | bytes 3538976 | tf_op jit(solution)/shard_map/all_to_all | solution.py:396
  103.9 1.3 copy-done.1
  105.2 8.7 %similar.1 = f32[16,1,144]{2,1,0:T(1,128)} custom-call(s32[9]{0:T(128)S(1)} %get-tuple-element.58.meet_ref, f32[3,1,768]{2,1,0:T(1,128)S(1)} %get-tuple-element.59.row_ref, f32[3,768,1]{2,1,0:T(8,128)S(1)} %copy-done.1, bf16[16,144,768]{2,1,0:T(8,128)(2,1)S(1)} %all-to-all-done.4.rows_ref), custom_call_target="tpu_custom_call" | custom-call | tf_op jit(solution)/shard_map/similar/pallas_call | solution.py:315
  113.9 17.0 %all-to-all-start.5 = ((f32[16,1,144]{2,1,0:T(1,128)}), f32[16,1,144]{2,1,0:T(1,128)S(1)}, u32[]{:S(2)}, u32[]{:S(2)}) async-start(f32[16,1,144]{2,1,0:T(1,128)} %similar.1), calls=%async_computation.5 | async-start | bytes 32768 | tf_op jit(solution)/shard_map/all_to_all | solution.py:396
  131.0 1.2 slice.3
  132.7 4.8 %all-to-all-done.5.back_ref = f32[16,1,144]{2,1,0:T(1,128)S(1)} async-done(((f32[16,1,144]{2,1,0:T(1,128)}), f32[16,1,144]{2,1,0:T(1,128)S(1)}, u32[]{:S(2)}, u32[]{:S(2)}) %all-to-all-start.5) | async-done | bytes 9248 | tf_op jit(solution)/shard_map/all_to_all | solution.py:396
  137.5 0.6 copy-done.7
  138.1 1.2 results.1
  139.3 0.0 copy-start.12
  139.3 0.6 copy-done.12
  (6 shorter events, 0.0 us)
Async XLA Ops:
  0.0 12.5 %copy-start.8 = (s32[2048,1]{0,1:T(1,128)S(1)}, s32[2048,1]{0,1:T(1,128)}, u32[]{:S(2)}) copy-start(s32[2048,1]{0,1:T(1,128)} %param.7) | copy-start | bytes 24580
  2.0 14.0 %all-to-all-start.3 = ((f32[16,1,512]{2,1,0:T(1,128)}), f32[16,1,512]{2,1,0:T(1,128)S(1)}, u32[]{:S(2)}, u32[]{:S(2)}) async-start(f32[16,1,512]{2,1,0:T(1,128)} %counts.1), calls=%async_computation.3 | async-start | bytes 65536 | tf_op jit(solution)/shard_map/all_to_all | solution.py:396
  12.6 21.3 %copy-start.5 = (bf16[2048,768]{1,0:T(8,128)(2,1)}, bf16[2048,768]{1,0:T(8,128)(2,1)S(1)}, u32[]{:S(2)}) copy-start(bf16[2048,768]{1,0:T(8,128)(2,1)S(1)} %unit.1.unit_ref) | copy-start | bytes 9437188
  14.0 19.9 %copy-start.10 = (s32[1,2048]{1,0:T(1,128)}, s32[1,2048]{1,0:T(1,128)S(1)}, u32[]{:S(2)}) copy-start(s32[1,2048]{1,0:T(1,128)S(1)} %ranks.1.rank_ref) | copy-start | bytes 24580
  16.1 0.6 copy-start.6
  24.2 0.7 copy-start.2
  33.8 70.1 %all-to-all-start.4 = ((bf16[16,144,768]{2,1,0:T(8,128)(2,1)}), bf16[16,144,768]{2,1,0:T(8,128)(2,1)S(1)}, u32[]{:S(2)}, u32[]{:S(2)}) async-start(bf16[16,144,768]{2,1,0:T(8,128)(2,1)} %bitcast.14), calls=%async_computation.4 | async-start | bytes 7077888 | tf_op jit(solution)/shard_map/all_to_all | solution.py:396
  37.7 0.8 copy-start.3
  38.6 0.7 copy-start.4
  42.5 1.0 copy-start
  103.9 1.3 copy-start.1
  113.9 23.5 %all-to-all-start.5 = ((f32[16,1,144]{2,1,0:T(1,128)}), f32[16,1,144]{2,1,0:T(1,128)S(1)}, u32[]{:S(2)}, u32[]{:S(2)}) async-start(f32[16,1,144]{2,1,0:T(1,128)} %similar.1), calls=%async_computation.5 | async-start | bytes 32768 | tf_op jit(solution)/shard_map/all_to_all | solution.py:396
  137.5 0.6 copy-start.7
  139.3 0.6 copy-start.12

commit v3 on v2

v3 whole, which is shorter than its diff:
```python
import functools

import jax
import jax.numpy as jnp
import numpy as np
from jax import lax
from jax.experimental import pallas as pl
from jax.experimental.pallas import tpu as pltpu
from jax.sharding import PartitionSpec as P

CLUSTERS = 512
MOST = 16
LANES = 128
SLACK = 16
ROUNDS = 6
EARLY = 3
LATE = 3
EXACT = lax.Precision.HIGHEST
BF16, F32, I32 = jnp.bfloat16, jnp.float32, jnp.int32
VMEM_LIMIT = 24 * 1024 * 1024
SMALL_VMEM = 12 * 1024 * 1024
NT = (((1,), (1,)), ((), ()))


def iota(shape, dim):
    return lax.broadcasted_iota(I32, shape, dim)


def one_hot(mask):
    return jnp.where(mask, jnp.float32(1), jnp.float32(0)).astype(BF16)


def quotient(index, by, limit):
    numbers = np.arange(limit)
    for shift in range(8, 24):
        factor = -(-(1 << shift) // by)
        if limit * factor < 1 << 31 and np.array_equal(numbers * factor >> shift, numbers // by):
            return (index * factor) >> shift
    raise ValueError("no factor")


def whole(count):
    return [pl.BlockSpec(memory_space=pltpu.VMEM)] * count


def count_kernel(label_ref, count_ref):
    step = 512
    ones = jnp.ones((count_ref.shape[0], step), BF16)
    counts = jnp.zeros((count_ref.shape[0], CLUSTERS), F32)
    for at in range(0, label_ref.shape[1], step):
        hot = one_hot(label_ref[:, at : at + step] == iota((CLUSTERS, step), 0))
        counts = counts + lax.dot_general(ones, hot, NT, preferred_element_type=F32)
    count_ref[:, 0, :] = counts


def counted(labels, peers):
    return pl.pallas_call(
        count_kernel,
        out_shape=jax.ShapeDtypeStruct((peers, 1, CLUSTERS), F32),
        in_specs=whole(1),
        out_specs=whole(1)[0],
        compiler_params=pltpu.CompilerParams(vmem_limit_bytes=SMALL_VMEM),
        name="counts",
    )(labels)


def rank_kernel(label_ref, rank_ref):
    step = 256
    tri = one_hot((iota((step, step + LANES), 0) < iota((step, step + LANES), 1)) | (iota((step, step + LANES), 1) >= step))
    running = jnp.zeros((CLUSTERS, LANES), F32)
    for at in range(0, label_ref.shape[1], step):
        hot = label_ref[:, at : at + step] == iota((CLUSTERS, step), 0)
        before = jnp.dot(one_hot(hot), tri, preferred_element_type=F32)
        here = before[:, :step] + jnp.concatenate([running] * (step // LANES), axis=1)
        rank_ref[:, at : at + step] = jnp.sum(jnp.where(hot, here, 0.0), axis=0, keepdims=True).astype(I32)
        running = running + before[:, step:]


def ranked(labels):
    return pl.pallas_call(
        rank_kernel,
        out_shape=jax.ShapeDtypeStruct(labels.shape, I32),
        in_specs=whole(1),
        out_specs=whole(1)[0],
        cost_estimate=pl.CostEstimate(flops=labels.shape[1] * CLUSTERS * 8, bytes_accessed=1 << 22, transcendentals=0),
        compiler_params=pltpu.CompilerParams(vmem_limit_bytes=SMALL_VMEM),
        name="ranks",
    )(labels)


def unit_kernel(rows_ref, unit_ref):
    values = rows_ref[...].astype(F32)
    total = jnp.sum(values * values, axis=1, keepdims=True)
    unit_ref[...] = (values * lax.rsqrt(total + 1e-06)).astype(BF16)


def unit_rows(embeddings):
    count, width = embeddings.shape
    step = min(512, count)
    spec = pl.BlockSpec((step, width), lambda i: (i, 0))
    return pl.pallas_call(
        unit_kernel,
        out_shape=jax.ShapeDtypeStruct((count, width), BF16),
        grid=(count // step,),
        in_specs=[spec],
        out_specs=spec,
        cost_estimate=pl.CostEstimate(flops=4 * count * width, bytes_accessed=4 * count * width, transcendentals=count),
        compiler_params=pltpu.CompilerParams(vmem_limit_bytes=SMALL_VMEM),
        name="unit",
    )(embeddings)


def swapped_evenly(table, peers):
    pieces = [table[:, at : at + LANES] for at in range(0, CLUSTERS, LANES)]
    lane = iota((1, LANES), 1)

    def over_laps(parts, combine):
        found = functools.reduce(combine, parts)
        shift = peers
        while shift < LANES:
            found = combine(found, pltpu.roll(found, shift, 1))
            shift *= 2
        return found

    bits = [1 << i for i in range(peers.bit_length() - 1)]
    for bit in (bits * ROUNDS)[:ROUNDS]:

        def partner(x):
            return jnp.where((lane & bit) == 0, pltpu.roll(x, LANES - bit, 1), pltpu.roll(x, bit, 1))

        load = over_laps([piece[:peers] for piece in pieces], jnp.add)
        excess = load - partner(load)
        others = [partner(piece) for piece in pieces]
        gains = []
        for piece, other in zip(pieces, others):
            moved = piece[:peers] - other[:peers]
            gains.append(jnp.sum(moved * (excess - moved), axis=0, keepdims=True))
        best = over_laps(gains, jnp.maximum)
        pieces = [
            jnp.where((gain == best) & (gain > 0.0), other, piece) for gain, other, piece in zip(gains, others, pieces)
        ]
    return jnp.concatenate(pieces, axis=1)


def offsets(table, peers):
    square = (CLUSTERS, CLUSTERS)
    bits = peers.bit_length() - 1
    first, second = iota(square, 0), iota(square, 1)
    earlier = one_hot((((first ^ second) & (peers - 1)) == 0) & ((first >> bits) < (second >> bits)))
    return jnp.dot(table[:peers].astype(BF16), earlier, preferred_element_type=F32)


def place_kernel(cap, me_ref, count_ref, label_ref, rank_ref, dest_ref, table_ref):
    me = me_ref[0]
    counts = count_ref[:, 0, :]
    peers = counts.shape[0]
    bits = peers.bit_length() - 1
    square = (CLUSTERS, CLUSTERS)
    total = jnp.sum(counts, axis=0, keepdims=True)
    total_col = jnp.transpose(jnp.broadcast_to(total, (LANES, CLUSTERS)))[:, :1]
    first, second = iota(square, 0), iota(square, 1)
    ahead = (total_col > total) | ((total_col == total) & (first < second))
    turn = (CLUSTERS - 1) - jnp.sum(jnp.where(ahead, 1.0, 0.0), axis=1, keepdims=True).astype(I32)
    place = jnp.where(((turn >> bits) & 1) == 0, turn, turn ^ (peers - 1))
    number = iota((8, CLUSTERS), 1)
    digits = jnp.where(iota((8, CLUSTERS), 0) == 0, number >> 4, number & 15).astype(F32)
    table = jnp.concatenate([counts, digits], axis=0).astype(BF16)
    table = jnp.dot(table, one_hot(place == second), preferred_element_type=F32)
    table = swapped_evenly(table, peers)
    table_ref[...] = table

    offset = offsets(table, peers)
    mine = jnp.sum(jnp.where(iota(counts.shape, 0) == me, offset, 0.0), axis=0, keepdims=True)
    base = mine + ((iota((1, CLUSTERS), 1) & (peers - 1)) * cap).astype(F32)
    cluster = table[peers : peers + 1] * 16.0 + table[peers + 1 : peers + 2]
    both = jnp.transpose(jnp.where(iota((LANES, CLUSTERS), 0) == 0, cluster, base))
    cluster_col, base_col = both[:, :1].astype(I32), both[:, 1:2]
    step = 512
    for at in range(0, label_ref.shape[1], step):
        hot = label_ref[:, at : at + step] == cluster_col
        slot = jnp.sum(jnp.where(hot, base_col, 0.0), axis=0, keepdims=True).astype(I32)
        dest_ref[:, at : at + step] = slot + rank_ref[:, at : at + step]


def places(me, counts, labels, ranks, cap):
    peers = counts.shape[0]
    return pl.pallas_call(
        functools.partial(place_kernel, cap),
        out_shape=(jax.ShapeDtypeStruct(labels.shape, I32), jax.ShapeDtypeStruct((peers + 8, CLUSTERS), F32)),
        in_specs=[pl.BlockSpec(memory_space=pltpu.SMEM)] + whole(3),
        out_specs=tuple(whole(2)),
        compiler_params=pltpu.CompilerParams(vmem_limit_bytes=SMALL_VMEM),
        name="places",
    )(me, counts, labels, ranks)


def sender_of(me, block, peers):
    half = peers // 2
    return jnp.where(block < half, (me & -half) + block, me ^ block)


def pack_kernel(cap, peers, numbers, me_ref, dest_ref, unit_ref, *block_refs):
    me = me_ref[0]
    count = dest_ref.shape[1]
    per_ref = block_refs[0].shape[0] // cap
    group = 4
    for at in range(0, len(numbers), group):
        some = numbers[at : at + group]
        index = iota((len(some) * cap, 1), 0)
        slots = index
        for i, number in enumerate(some):
            shift = (sender_of(me, number, peers) - i) * cap
            slots = jnp.where((index >= i * cap) & (index < (i + 1) * cap), index + shift, slots)
        pick = one_hot(dest_ref[...] == slots)
        rows = jnp.dot(pick, unit_ref[...], preferred_element_type=F32).astype(BF16)
        for i in range(len(some)):
            block, within = divmod(at + i, per_ref)
            block_refs[block][within * cap : (within + 1) * cap, :] = rows[i * cap : (i + 1) * cap]


def packed(me, dest, unit, cap, peers, numbers, per_block=1):
    count, width = unit.shape
    rows = len(numbers) * cap
    blocks = len(numbers) // per_block
    return pl.pallas_call(
        functools.partial(pack_kernel, cap, peers, numbers),
        out_shape=tuple([jax.ShapeDtypeStruct((per_block * cap, width), BF16)] * blocks),
        in_specs=[pl.BlockSpec(memory_space=pltpu.SMEM)] + whole(2),
        out_specs=tuple(whole(blocks)),
        cost_estimate=pl.CostEstimate(
            flops=2 * rows * count * width, bytes_accessed=2 * width * (count + rows), transcendentals=0
        ),
        compiler_params=pltpu.CompilerParams(vmem_limit_bytes=VMEM_LIMIT),
        name="pack",
    )(me, dest, unit)


def key_kernel(cap, me_ref, table_ref, row_ref, col_ref, most_ref):
    me = me_ref[0]
    peers = table_ref.shape[0] - 8
    bits = peers.bit_length() - 1
    owned = CLUSTERS // peers
    slots = peers * cap
    ends = offsets(table_ref[...], peers) + table_ref[:peers]
    most_ref[...] = jnp.broadcast_to(jnp.max(ends, axis=(0, 1), keepdims=True), most_ref.shape)
    chosen = iota((LANES, CLUSTERS), 1) == (iota((LANES, CLUSTERS), 0) << bits) + me
    chosen = jnp.where(chosen, jnp.float32(1), jnp.float32(0))
    own = lax.dot_general(chosen, ends, NT, precision=EXACT, preferred_element_type=F32)
    own = jnp.where(iota(own.shape, 0) < owned, own, jnp.float32(1 << 20))

    index = iota((1, slots), 1)
    block = quotient(index, cap, slots)
    spot = (index - block * cap).astype(F32)
    from_peer = sender_of(me, block, peers) == iota((peers, slots), 0)
    from_peer = jnp.where(from_peer, jnp.float32(1), jnp.float32(0))
    ends = jnp.dot(own, from_peer, precision=EXACT, preferred_element_type=F32)
    row = jnp.sum(jnp.where(ends <= spot, 1.0, 0.0), axis=0, keepdims=True)
    row_ref[...] = row
    col_ref[...] = jnp.transpose(jnp.broadcast_to(row, (LANES, slots)))


def keys(me, table, cap):
    peers = table.shape[0] - 8
    slots = peers * cap
    return pl.pallas_call(
        functools.partial(key_kernel, cap),
        out_shape=(
            jax.ShapeDtypeStruct((1, slots), F32),
            jax.ShapeDtypeStruct((slots, LANES), F32),
            jax.ShapeDtypeStruct((8, LANES), F32),
        ),
        in_specs=[pl.BlockSpec(memory_space=pltpu.SMEM)] + whole(1),
        out_specs=tuple(whole(3)),
        cost_estimate=pl.CostEstimate(flops=1 << 28, bytes_accessed=1 << 22, transcendentals=0),
        compiler_params=pltpu.CompilerParams(vmem_limit_bytes=SMALL_VMEM),
        name="keys",
    )(me, table)


def rows_of(refs, cap, start, count):
    found, at = [], 0
    for ref in refs:
        blocks = ref.shape[0] // cap
        low, high = max(start, at), min(start + count, at + blocks)
        if low < high:
            found.append(ref[(low - at) * cap : (high - at) * cap, :])
        at += blocks
    return found[0] if len(found) == 1 else jnp.concatenate(found, axis=0)


def masked_parts(rows, columns, key_col, key_row, itself):
    gram = lax.dot_general(rows, columns, NT, preferred_element_type=F32)
    height, width = gram.shape
    parts = []
    for lane in range(0, width, LANES):
        wide = min(LANES, width - lane)
        part = gram[:, lane : lane + wide]
        keep = key_col[:, :wide] == key_row[:, lane : lane + wide]
        if -width < itself < height:
            keep = keep & (iota(part.shape, 0) - iota(part.shape, 1) != itself + lane)
        parts.append(jnp.where(keep, part, -1.0))
    return parts


def largest(parts):
    return jnp.concatenate([jnp.max(part, axis=0, keepdims=True) for part in parts], axis=1)


def first_kernel(cap, known, row_ref, col_ref, *refs):
    *block_refs, best_ref = refs
    tall, broad = max(1, 576 // cap), max(1, 432 // cap)
    for left in range(0, known, broad):
        count = min(broad, known - left)
        columns = rows_of(block_refs, cap, left, count)
        key_row = row_ref[:, left * cap : (left + count) * cap]
        best = jnp.full((1, count * cap), -1.0, F32)
        for upper in range(0, known, tall):
            rows = rows_of(block_refs, cap, upper, min(tall, known - upper))
            key_col = col_ref[upper * cap : upper * cap + rows.shape[0], :]
            best = jnp.maximum(best, largest(masked_parts(rows, columns, key_col, key_row, (left - upper) * cap)))
        for i in range(count):
            best_ref[left + i] = best[:, i * cap : (i + 1) * cap]


def last_kernel(cap, known, me_ref, row_ref, col_ref, before_ref, *refs):
    *block_refs, best_ref = refs
    me = me_ref[0]
    peers = best_ref.shape[0]
    tall = max(1, 576 // cap)
    columns = rows_of(block_refs, cap, known, peers - known)
    key_row = row_ref[:, known * cap :]
    best = jnp.full((1, (peers - known) * cap), -1.0, F32)
    for upper in range(0, peers, tall):
        count = min(tall, peers - upper)
        rows = rows_of(block_refs, cap, upper, count)
        key_col = col_ref[upper * cap : (upper + count) * cap, :]
        parts = masked_parts(rows, columns, key_col, key_row, (known - upper) * cap)
        best = jnp.maximum(best, largest(parts))
        if upper < known:
            tail = parts[-1]
            if tail.shape[1] < LANES:
                tail = jnp.concatenate([tail, jnp.full((count * cap, LANES - tail.shape[1]), -1.0, F32)], axis=1)
            side = functools.reduce(jnp.maximum, parts[:-1] + [tail])
            for i in range(min(count, known - upper)):
                across = jnp.max(jnp.transpose(side[i * cap : (i + 1) * cap]), axis=0, keepdims=True)
                best_ref[sender_of(me, upper + i, peers)] = jnp.maximum(before_ref[upper + i], across)
    for i in range(peers - known):
        best_ref[sender_of(me, known + i, peers)] = best[:, i * cap : (i + 1) * cap]


def call_bests(kernel, scalars, arrays, blocks, out_blocks, fresh, cap):
    rows = sum(block.shape[0] for block in blocks)
    return pl.pallas_call(
        kernel,
        out_shape=jax.ShapeDtypeStruct((out_blocks, 1, cap), F32),
        in_specs=[pl.BlockSpec(memory_space=pltpu.SMEM)] * len(scalars) + whole(len(arrays) + len(blocks)),
        out_specs=whole(1)[0],
        cost_estimate=pl.CostEstimate(
            flops=2 * fresh * cap * rows * blocks[0].shape[1], bytes_accessed=1 << 23, transcendentals=0
        ),
        compiler_params=pltpu.CompilerParams(vmem_limit_bytes=VMEM_LIMIT),
        name="similar",
    )(*scalars, *arrays, *blocks)


def three_parts(values):
    high = values.astype(BF16)
    rest = values - high.astype(F32)
    middle = rest.astype(BF16)
    return high, middle, (rest - middle.astype(F32)).astype(BF16)


def result_kernel(dest_ref, back_ref, out_ref):
    peers, _, cap = back_ref.shape
    pieces = three_parts(back_ref[:, 0, :])
    step = 512
    for at in range(0, dest_ref.shape[1], step):
        dest = dest_ref[:, at : at + step]
        owner = dest // cap
        hot = one_hot(dest - owner * cap == iota((cap, step), 0))
        parts = [jnp.dot(part, hot, preferred_element_type=F32) for part in pieces]
        found = parts[0] + (parts[1] + parts[2])
        out_ref[:, at : at + step] = jnp.sum(jnp.where(owner == iota((peers, step), 0), found, 0.0), axis=0, keepdims=True)


def results(dest, back):
    return pl.pallas_call(
        result_kernel,
        out_shape=jax.ShapeDtypeStruct(dest.shape, F32),
        in_specs=whole(2),
        out_specs=whole(1)[0],
        compiler_params=pltpu.CompilerParams(vmem_limit_bytes=SMALL_VMEM),
        name="results",
    )(dest, back)


def cluster_best(pair):
    blocks, flags = pair
    peers, owned, most, width = blocks.shape
    slots = peers * most
    members = jnp.transpose(blocks, (1, 0, 2, 3)).reshape(owned, slots, width)
    valid = jnp.transpose(flags, (1, 0, 2)).reshape(owned, slots) > 0.5
    off_diagonal = jnp.logical_not(jnp.eye(slots, dtype=bool))

    def one_cluster(item):
        rows_of, valid_of = item
        gram = jnp.dot(rows_of, rows_of.T, preferred_element_type=jnp.float32)
        keep = valid_of[None, :] & off_diagonal
        return jnp.max(jnp.where(keep, gram, jnp.float32(-1.0)), axis=1)

    best = lax.map(one_cluster, (members, valid))
    return jnp.transpose(best.reshape(owned, peers, most), (1, 0, 2))


def roomy(labels, ranks, unit):
    count, width = unit.shape
    peers = lax.axis_size("rows")
    owned = CLUSTERS // peers
    cluster_hot = (labels[:, None] == jnp.arange(CLUSTERS, dtype=I32)[None, :]).astype(F32)
    rank_hot = (ranks[:, None] == jnp.arange(MOST, dtype=I32)[None, :]).astype(F32)
    numbered = rank_hot * jnp.arange(1, count + 1, dtype=F32)[:, None]
    filled = jnp.dot(cluster_hot.T, rank_hot, precision=EXACT)
    member_idx = jnp.dot(cluster_hot.T, numbered, precision=EXACT).astype(I32) - 1
    member_idx = jnp.where(member_idx < 0, count, member_idx).reshape(CLUSTERS * MOST)
    padded = jnp.concatenate([unit, jnp.zeros((1, width), BF16)], axis=0)
    outgoing = padded[member_idx].reshape(peers, owned, MOST, width)
    occupied = filled.astype(BF16).reshape(peers, owned, MOST)
    best = cluster_best((exchange(outgoing), exchange(occupied)))
    table = exchange(best).reshape(CLUSTERS, MOST)
    per_row = jnp.dot(cluster_hot, table, precision=EXACT)
    return jnp.sum(per_row * rank_hot, axis=1)


def exchange(blocks, groups=None):
    return lax.all_to_all(blocks, "rows", split_axis=0, concat_axis=0, tiled=True, axis_index_groups=groups)


def swap(block, number, peers):
    return lax.ppermute(block, "rows", [(i, i ^ number) for i in range(peers)])


def local(embeddings, cluster_id):
    count, width = embeddings.shape
    peers = lax.axis_size("rows")
    cap = -(-(count // peers + SLACK) // 16) * 16
    labels = cluster_id.reshape(1, count)
    counts = exchange(counted(labels, peers))
    ranks = ranked(labels)
    unit = unit_rows(embeddings)
    me = lax.axis_index("rows").reshape(1)
    dest, table = places(me, counts, labels, ranks, cap)

    half = peers // 2
    across = list(range(half, peers))
    leaving = packed(me, dest, unit, cap, peers, across[:EARLY])
    later, _ = lax.optimization_barrier((dest, leaving[0]))
    leaving += packed(me, later, unit, cap, peers, across[EARLY:])
    (inside,) = packed(me, later, unit, cap, peers, list(range(half)), half)
    arrived = [swap(block, number, peers) for block, number in zip(leaving, across)]
    inside, _, *arrived[:EARLY] = lax.optimization_barrier((inside, leaving[EARLY], *arrived[:EARLY]))
    inside = exchange(inside.reshape(half, cap, width), [list(range(half)), list(range(half, peers))])
    blocks = [inside.reshape(half * cap, width)] + arrived
    key_row, key_col, most = keys(me, table, cap)
    known = peers - LATE
    first = functools.partial(first_kernel, cap, known)
    best = call_bests(first, [], [key_row, key_col], blocks[: len(blocks) - LATE], known, known, cap)
    last = functools.partial(last_kernel, cap, known)
    best = call_bests(last, [me], [key_row, key_col, best], blocks, peers, LATE, cap)
    back = exchange(best)
    nearest = results(dest, back).reshape(count)
    return lax.cond(
        most[0, 0] > cap,
        lambda labels, ranks, unit, nearest: roomy(labels.reshape(count), ranks.reshape(count), unit),
        lambda labels, ranks, unit, nearest: nearest,
        labels, ranks, unit, nearest,
    )


def solution(mesh):
    return jax.shard_map(
        local,
        mesh=mesh,
        in_specs=(P(("groups", "rows"), None), P(("groups", "rows"), None)),
        out_specs=P(("groups", "rows")),
        check_vma=False,
    )
```

time: 141 us -> 126 us (0.89)
  waiting for transfers between devices: 67.3 us -> 47.7 us
  starting transfers between devices: 28.3 us -> 34.1 us
  Pallas kernels: 36.1 us -> 34.6 us
    all_to_all x3, waiting for transfers between devices: 67.3 us -> 7.62 us  [exchange(): lax.all_to_all(blocks, 'rows', split_axis=0, concat_axis=0, tiled=True, a...]
    ppermute x0 -> x8, waiting for transfers between devices: none -> 40.1 us  [swap(): return lax.ppermute(block, 'rows', [(i, i ^ number) for i in range(peers)])]
    ppermute x0 -> x8, starting transfers between devices: none -> 13.8 us  [swap(): return lax.ppermute(block, 'rows', [(i, i ^ number) for i in range(peers)])]
    all_to_all x3, starting transfers between devices: 28.3 us -> 20.3 us  [exchange(): lax.all_to_all(blocks, 'rows', split_axis=0, concat_axis=0, tiled=True, a...]
    pallas_call x3 -> x6, Pallas kernels: 20.9 us -> 25 us  [the longest x3 11.6 us: packed(): pl.pallas_call(functools.partial(pack_kernel, cap, peers, numbers), out_s...]
    pallas_call x1, Pallas kernels: 7.5 us -> 4.69 us  [places(): pl.pallas_call(functools.partial(place_kernel, cap), out_shape=(jax.Shape...]
    pallas_call x1, Pallas kernels: 3.1 us -> 1.02 us  [unit_rows(): pl.pallas_call(unit_kernel, out_shape=jax.ShapeDtypeStruct((count, width)...]
    unnamed x22 -> x28, local copies, waits for them, and re-layouts: 6.32 us -> 8.17 us
  transfers between devices with their start and end apart: 3 -> 11, of which waited for: 3 -> 9; matrix products, arithmetic and copies ran while one was open for 1% -> 0% of each run, Pallas kernels for 6% -> 17%
where the time goes in v3:
time: 126 us
  waiting for transfers between devices  47.7 us (38%)
  Pallas kernels  34.6 us (27%)
  starting transfers between devices  34.1 us (27%)
  local copies, waits for them, and re-layouts  8.72 us (7%)
    ppermute x8, waiting for transfers between devices, swap(): return lax.ppermute(block, 'rows', [(i, i ^ number) for i in range(peers)])  40.1 us
    all_to_all x3, starting transfers between devices, exchange(): lax.all_to_all(blocks, 'rows', split_axis=0, concat_axis=0, tiled=True, a...  20.3 us
    ppermute x8, starting transfers between devices, swap(): return lax.ppermute(block, 'rows', [(i, i ^ number) for i in range(peers)])  13.8 us
    pallas_call x3, Pallas kernels, packed(): pl.pallas_call(functools.partial(pack_kernel, cap, peers, numbers), out_s...  11.6 us
    pallas_call x2, Pallas kernels, call_bests(): pl.pallas_call(kernel, out_shape=jax.ShapeDtypeStruct((out_blocks, 1, cap...  11.4 us
    unnamed x28, local copies, waits for them, and re-layouts  8.17 us
    all_to_all x3, waiting for transfers between devices, exchange(): lax.all_to_all(blocks, 'rows', split_axis=0, concat_axis=0, tiled=True, a...  7.62 us
    pallas_call x1, Pallas kernels, places(): pl.pallas_call(functools.partial(place_kernel, cap), out_shape=(jax.Shape...  4.69 us
  transfers between devices with their start and end apart: 11, of which 9 were waited for; matrix products, arithmetic and copies ran while one was open for 0% of the time, Pallas kernels for 17%

profile of v3, /device:TPU:0, one launch (start us, length us, event | category | flops | bytes accessed | tf_op | source)
XLA Modules:
  0.0 125.9 jit_solution(16825266076168587368)
XLA Ops:
  0.0 2.0 %counts.1 = f32[16,1,512]{2,1,0:T(1,128)} custom-call(s32[1,2048]{1,0:T(1,128)} %bitcast.47), custom_call_target="tpu_custom_call" | custom-call | tf_op jit(solution)/shard_map/counts/pallas_call | solution.py:57
  2.0 7.4 %all-to-all-start.3 = ((f32[16,1,512]{2,1,0:T(1,128)}), f32[16,1,512]{2,1,0:T(1,128)S(1)}, u32[]{:S(2)}, u32[]{:S(2)}) async-start(f32[16,1,512]{2,1,0:T(1,128)} %counts.1), calls=%async_computation.3 | async-start | bytes 65536 | tf_op jit(solution)/shard_map/all_to_all | solution.py:435
  9.4 1.9 %copy-done = bf16[2048,768]{1,0:T(8,128)(2,1)S(1)} copy-done((bf16[2048,768]{1,0:T(8,128)(2,1)S(1)}, bf16[2048,768]{1,0:T(8,128)(2,1)}, u32[]{:S(2)}) %copy-start) | copy-done | bytes 3145752
  11.3 1.0 unit.1.unit_ref
  12.4 1.4 %ranks.1.rank_ref = s32[1,2048]{1,0:T(1,128)S(1)} custom-call(s32[1,2048]{1,0:T(1,128)S(1)} %bitcast.48), custom_call_target="tpu_custom_call" | custom-call | flops 8388608 | bytes 4194304 | tf_op jit(solution)/shard_map/ranks/pallas_call | solution.py:80
  13.8 2.3 %all-to-all-done.3.count_ref = f32[16,1,512]{2,1,0:T(1,128)S(1)} async-done(((f32[16,1,512]{2,1,0:T(1,128)}), f32[16,1,512]{2,1,0:T(1,128)S(1)}, u32[]{:S(2)}, u32[]{:S(2)}) %all-to-all-start.3) | async-done | bytes 32800 | tf_op jit(solution)/shard_map/all_to_all | solution.py:435
  16.1 4.7 %places.1 = (s32[1,2048]{1,0:T(1,128)S(1)}, f32[24,512]{1,0:T(8,128)S(1)}) custom-call(s32[1]{0:T(128)} %bitcast.11.me_ref, f32[16,1,512]{2,1,0:T(1,128)S(1)} %all-to-all-done.3.count_ref, s32[1,2048]{1,0:T(1,128)S(1)} %bitcast.49, s32[1,2048]{1,0:T(1,128)S(1)} %ranks.1.rank_ref), custom_call_target="tpu_custom_call" | custom-call | tf_op jit(solution)/shard_map/places/pallas_call | solution.py:187
  21.4 1.6 %pack.3 = (bf16[144,768]{1,0:T(8,128)(2,1)S(1)}, bf16[144,768]{1,0:T(8,128)(2,1)S(1)}, bf16[144,768]{1,0:T(8,128)(2,1)S(1)}) custom-call(s32[1]{0:T(128)} %bitcast.11.me_ref, s32[1,2048]{1,0:T(1,128)S(1)} %get-tuple-element.71.dest_ref, bf16[2048,768]{1,0:T(8,128)(2,1)S(1)} %unit.1.unit_ref), custom_call_target="tpu_custom_call" | custom-call | flops 1358954496 | bytes 3809280 | tf_op jit(solution)/shard_map/pack/pallas_call | solution.py:225
  23.6 1.4 %collective-permute-start.1 = (bf16[144,768]{1,0:T(8,128)(2,1)S(1)}, bf16[144,768]{1,0:T(8,128)(2,1)S(1)}, u32[]{:S(2)}, u32[]{:S(2)}) collective-permute-start(bf16[144,768]{1,0:T(8,128)(2,1)S(1)} %get-tuple-element.73), channel_id=1, source_target_pairs={{0,9},{1,8},{2,11},{3,10},{4,13},{5,12},{6,15},{7,14},{8,1},{9,0},... | collective-permute-start | bytes 663560 | tf_op jit(solution)/shard_map/ppermute | solution.py:439
  25.0 1.9 %collective-permute-start.2 = (bf16[144,768]{1,0:T(8,128)(2,1)S(1)}, bf16[144,768]{1,0:T(8,128)(2,1)S(1)}, u32[]{:S(2)}, u32[]{:S(2)}) collective-permute-start(bf16[144,768]{1,0:T(8,128)(2,1)S(1)} %get-tuple-element.74), channel_id=1, source_target_pairs={{0,10},{1,11},{2,8},{3,9},{4,14},{5,15},{6,12},{7,13},{8,2},{9,3},... | collective-permute-start | bytes 663560 | tf_op jit(solution)/shard_map/ppermute | solution.py:439
  26.9 6.9 %pack.4 = bf16[1152,768]{1,0:T(8,128)(2,1)} custom-call(s32[1]{0:T(128)} %bitcast.11.me_ref, s32[1,2048]{1,0:T(1,128)S(1)} %get-tuple-element.71.dest_ref, bf16[2048,768]{1,0:T(8,128)(2,1)} %copy-done.9), custom_call_target="tpu_custom_call" | custom-call | flops 3623878656 | bytes 4915200 | tf_op jit(solution)/shard_map/pack/pallas_call | solution.py:225
  33.8 3.1 %pack.5 = (bf16[144,768]{1,0:T(8,128)(2,1)}, bf16[144,768]{1,0:T(8,128)(2,1)S(1)}, bf16[144,768]{1,0:T(8,128)(2,1)S(1)}, bf16[144,768]{1,0:T(8,128)(2,1)S(1)}, bf16[144,768]{1,0:T(8,128)(2,1)S(1)}) custom-call(s32[1]{0:T(128)} %bitcast.11.me_ref, s32[1,2048]{1,0:T(1,128)S(1)} %get-tuple-element.71.dest_ref, bf16[2048,768]{1,0:T(8,128)(2,1)S(1)} %copy-done.10), custom_call_target="tpu_custom_call" | custom-call | flops 2264924160 | bytes 4251648 | tf_op jit(solution)/shard_map/pack/pallas_call | solution.py:225
  37.6 7.9 %collective-permute-done.refs_1_ = bf16[144,768]{1,0:T(8,128)(2,1)S(1)} collective-permute-done((bf16[144,768]{1,0:T(8,128)(2,1)S(1)}, bf16[144,768]{1,0:T(8,128)(2,1)S(1)}, u32[]{:S(2)}, u32[]{:S(2)}) %collective-permute-start) | collective-permute-done | bytes 221216 | tf_op jit(solution)/shard_map/ppermute | solution.py:439
  45.5 4.1 %collective-permute-done.1.refs_2_ = bf16[144,768]{1,0:T(8,128)(2,1)S(1)} collective-permute-done((bf16[144,768]{1,0:T(8,128)(2,1)S(1)}, bf16[144,768]{1,0:T(8,128)(2,1)S(1)}, u32[]{:S(2)}, u32[]{:S(2)}) %collective-permute-start.1) | collective-permute-done | bytes 221216 | tf_op jit(solution)/shard_map/ppermute | solution.py:439
  49.6 5.3 %collective-permute-done.2.refs_3_ = bf16[144,768]{1,0:T(8,128)(2,1)S(1)} collective-permute-done((bf16[144,768]{1,0:T(8,128)(2,1)S(1)}, bf16[144,768]{1,0:T(8,128)(2,1)S(1)}, u32[]{:S(2)}, u32[]{:S(2)}) %collective-permute-start.2) | collective-permute-done | bytes 221216 | tf_op jit(solution)/shard_map/ppermute | solution.py:439
  54.9 3.8 %all-to-all-start.4 = ((bf16[8,144,768]{2,1,0:T(8,128)(2,1)}), bf16[8,144,768]{2,1,0:T(8,128)(2,1)S(1)}, u32[]{:S(2)}, u32[]{:S(2)}) async-start(bf16[8,144,768]{2,1,0:T(8,128)(2,1)} %bitcast.14), calls=%async_computation.4 | async-start | bytes 3538944 | tf_op jit(solution)/shard_map/all_to_all | solution.py:435
  58.6 1.9 %collective-permute-start.3 = (bf16[144,768]{1,0:T(8,128)(2,1)}, bf16[144,768]{1,0:T(8,128)(2,1)S(1)}, u32[]{:S(2)}, u32[]{:S(2)}) collective-permute-start(bf16[144,768]{1,0:T(8,128)(2,1)} %get-tuple-element.72), channel_id=1, source_target_pairs={{0,11},{1,10},{2,9},{3,8},{4,15},{5,14},{6,13},{7,12},{8,3},{9,2},... | collective-permute-start | bytes 663560 | tf_op jit(solution)/shard_map/ppermute | solution.py:439
  60.5 2.9 %collective-permute-start.4 = (bf16[144,768]{1,0:T(8,128)(2,1)}, bf16[144,768]{1,0:T(8,128)(2,1)S(1)}, u32[]{:S(2)}, u32[]{:S(2)}) collective-permute-start(bf16[144,768]{1,0:T(8,128)(2,1)} %copy-done.1), channel_id=1, source_target_pairs={{0,12},{1,13},{2,14},{3,15},{4,8},{5,9},{6,10},{7,11},{8,4},{9,5},... | collective-permute-start | bytes 663560 | tf_op jit(solution)/shard_map/ppermute | solution.py:439
  64.0 2.9 %collective-permute-start.6 = (bf16[144,768]{1,0:T(8,128)(2,1)S(1)}, bf16[144,768]{1,0:T(8,128)(2,1)}, u32[]{:S(2)}, u32[]{:S(2)}) collective-permute-start(bf16[144,768]{1,0:T(8,128)(2,1)S(1)} %get-tuple-element.81), channel_id=1, source_target_pairs={{0,14},{1,15},{2,12},{3,13},{4,10},{5,11},{6,8},{7,9},{8,6},{9,7},... | collective-permute-start | bytes 663560 | tf_op jit(solution)/shard_map/ppermute | solution.py:439
  66.9 1.6 %collective-permute-start.7 = (bf16[144,768]{1,0:T(8,128)(2,1)S(1)}, bf16[144,768]{1,0:T(8,128)(2,1)}, u32[]{:S(2)}, u32[]{:S(2)}) collective-permute-start(bf16[144,768]{1,0:T(8,128)(2,1)S(1)} %get-tuple-element.82), channel_id=1, source_target_pairs={{0,15},{1,14},{2,13},{3,12},{4,11},{5,10},{6,9},{7,8},{8,7},{9,6},... | collective-permute-start | bytes 663560 | tf_op jit(solution)/shard_map/ppermute | solution.py:439
  68.5 0.8 copy-done.3
  69.3 2.0 %keys.1 = (f32[1,2304]{1,0:T(1,128)S(1)}, f32[2304,128]{1,0:T(8,128)S(1)}, f32[8,128]{1,0:T(8,128)S(1)}) custom-call(s32[1]{0:T(128)} %bitcast.11.me_ref, f32[24,512]{1,0:T(8,128)S(1)} %copy-done.3), custom_call_target="tpu_custom_call" | custom-call | flops 268435456 | bytes 4194304 | tf_op jit(solution)/shard_map/keys/pallas_call | solution.py:265
  71.3 1.0 copy-done.4
  72.9 10.7 %collective-permute-done.3.refs_4_ = bf16[144,768]{1,0:T(8,128)(2,1)S(1)} collective-permute-done((bf16[144,768]{1,0:T(8,128)(2,1)}, bf16[144,768]{1,0:T(8,128)(2,1)S(1)}, u32[]{:S(2)}, u32[]{:S(2)}) %collective-permute-start.3) | collective-permute-done | bytes 221216 | tf_op jit(solution)/shard_map/ppermute | solution.py:439
  83.6 7.7 %collective-permute-done.4.refs_5_ = bf16[144,768]{1,0:T(8,128)(2,1)S(1)} collective-permute-done((bf16[144,768]{1,0:T(8,128)(2,1)}, bf16[144,768]{1,0:T(8,128)(2,1)S(1)}, u32[]{:S(2)}, u32[]{:S(2)}) %collective-permute-start.4) | collective-permute-done | bytes 221216 | tf_op jit(solution)/shard_map/ppermute | solution.py:439
  91.4 1.3 %copy-done.5 = f32[2304,128]{1,0:T(8,128)S(1)} copy-done((f32[2304,128]{1,0:T(8,128)S(1)}, f32[2304,128]{1,0:T(8,128)}, u32[]{:S(2)}) %copy-start.5) | copy-done | bytes 1179672
  92.6 0.7 copy-done.7
  93.3 7.5 %similar.2.before_ref = f32[13,1,144]{2,1,0:T(1,128)S(1)} custom-call(f32[1,2304]{1,0:T(1,128)S(1)} %copy-done.7, f32[2304,128]{1,0:T(8,128)S(1)} %copy-done.5, bf16[1152,768]{1,0:T(8,128)(2,1)S(1)} %bitcast.38, bf16[144,768]{1,0:T(8,128)(2,1)S(1)} %collective-permute-done.refs_1_, bf16[144,768]{1,0:T(8,128)(2,1)S(1)} %collective-permute-done.1.refs_2_, ...), custom_call_target="tpu_custom_call" | custom-call | flops 5382733824 | bytes 8388608 | tf_op jit(solution)/shard_map/similar/pallas_call | solution.py:353
  101.5 3.8 %collective-permute-done.7.refs_8_ = bf16[144,768]{1,0:T(8,128)(2,1)} collective-permute-done((bf16[144,768]{1,0:T(8,128)(2,1)S(1)}, bf16[144,768]{1,0:T(8,128)(2,1)}, u32[]{:S(2)}, u32[]{:S(2)}) %collective-permute-start.7) | collective-permute-done | bytes 221216 | tf_op jit(solution)/shard_map/ppermute | solution.py:439
  105.2 3.9 %similar.3 = f32[16,1,144]{2,1,0:T(1,128)} custom-call(s32[1]{0:T(128)} %bitcast.11.me_ref, f32[1,2304]{1,0:T(1,128)S(1)} %copy-done.8, f32[2304,128]{1,0:T(8,128)S(1)} %copy-done.5, f32[13,1,144]{2,1,0:T(1,128)S(1)} %similar.2.before_ref, bf16[1152,768]{1,0:T(8,128)(2,1)S(1)} %bitcast.39, bf16[144,768]{1,0:T(8,128)(2,1)S(1)} %collective-permute-done.refs_1_, ...), custom_call_target="tpu_custom_call" | custom-call | flops 1528823808 | bytes 8388608 | tf_op jit(solution)/shard_map/similar/pallas_call | solution.py:353
  109.2 9.2 %all-to-all-start.5 = ((f32[16,1,144]{2,1,0:T(1,128)}), f32[16,1,144]{2,1,0:T(1,128)S(1)}, u32[]{:S(2)}, u32[]{:S(2)}) async-start(f32[16,1,144]{2,1,0:T(1,128)} %similar.3), calls=%async_computation.5 | async-start | bytes 32768 | tf_op jit(solution)/shard_map/all_to_all | solution.py:435
  119.5 5.3 %all-to-all-done.5.back_ref = f32[16,1,144]{2,1,0:T(1,128)S(1)} async-done(((f32[16,1,144]{2,1,0:T(1,128)}), f32[16,1,144]{2,1,0:T(1,128)S(1)}, u32[]{:S(2)}, u32[]{:S(2)}) %all-to-all-start.5) | async-done | bytes 9248 | tf_op jit(solution)/shard_map/all_to_all | solution.py:435
  (31 shorter events, 5.4 us)
Async XLA Ops:
  0.0 12.4 %copy-start.11 = (s32[2048,1]{0,1:T(1,128)S(1)}, s32[2048,1]{0,1:T(1,128)}, u32[]{:S(2)}) copy-start(s32[2048,1]{0,1:T(1,128)} %param.7) | copy-start | bytes 24580
  2.0 14.0 %all-to-all-start.3 = ((f32[16,1,512]{2,1,0:T(1,128)}), f32[16,1,512]{2,1,0:T(1,128)S(1)}, u32[]{:S(2)}, u32[]{:S(2)}) async-start(f32[16,1,512]{2,1,0:T(1,128)} %counts.1), calls=%async_computation.3 | async-start | bytes 65536 | tf_op jit(solution)/shard_map/all_to_all | solution.py:435
  9.4 1.9 %copy-start = (bf16[2048,768]{1,0:T(8,128)(2,1)S(1)}, bf16[2048,768]{1,0:T(8,128)(2,1)}, u32[]{:S(2)}) copy-start(bf16[2048,768]{1,0:T(8,128)(2,1)} %rows_ref.1) | copy-start | bytes 9437188
  12.4 10.6 %copy-start.9 = (bf16[2048,768]{1,0:T(8,128)(2,1)}, bf16[2048,768]{1,0:T(8,128)(2,1)S(1)}, u32[]{:S(2)}) copy-start(bf16[2048,768]{1,0:T(8,128)(2,1)S(1)} %unit.1.unit_ref) | copy-start | bytes 9437188
  13.8 20.1 %copy-start.13 = (s32[1,2048]{1,0:T(1,128)}, s32[1,2048]{1,0:T(1,128)S(1)}, u32[]{:S(2)}) copy-start(s32[1,2048]{1,0:T(1,128)S(1)} %ranks.1.rank_ref) | copy-start | bytes 24580
  20.8 0.6 copy-start.2
  23.0 22.5 %collective-permute-start = (bf16[144,768]{1,0:T(8,128)(2,1)S(1)}, bf16[144,768]{1,0:T(8,128)(2,1)S(1)}, u32[]{:S(2)}, u32[]{:S(2)}) collective-permute-start(bf16[144,768]{1,0:T(8,128)(2,1)S(1)} %get-tuple-element.70), channel_id=1, source_target_pairs={{0,8},{1,9},{2,10},{3,11},{4,12},{5,13},{6,14},{7,15},{8,0},{9,1},... | collective-permute-start | bytes 663560 | tf_op jit(solution)/shard_map/ppermute | solution.py:439
  23.6 26.0 %collective-permute-start.1 = (bf16[144,768]{1,0:T(8,128)(2,1)S(1)}, bf16[144,768]{1,0:T(8,128)(2,1)S(1)}, u32[]{:S(2)}, u32[]{:S(2)}) collective-permute-start(bf16[144,768]{1,0:T(8,128)(2,1)S(1)} %get-tuple-element.73), channel_id=1, source_target_pairs={{0,9},{1,8},{2,11},{3,10},{4,13},{5,12},{6,15},{7,14},{8,1},{9,0},... | collective-permute-start | bytes 663560 | tf_op jit(solution)/shard_map/ppermute | solution.py:439
  25.0 8.9 %copy-start.10 = (bf16[2048,768]{1,0:T(8,128)(2,1)S(1)}, bf16[2048,768]{1,0:T(8,128)(2,1)}, u32[]{:S(2)}) copy-start(bf16[2048,768]{1,0:T(8,128)(2,1)} %copy-done.9) | copy-start | bytes 9437188
  25.0 29.9 %collective-permute-start.2 = (bf16[144,768]{1,0:T(8,128)(2,1)S(1)}, bf16[144,768]{1,0:T(8,128)(2,1)S(1)}, u32[]{:S(2)}, u32[]{:S(2)}) collective-permute-start(bf16[144,768]{1,0:T(8,128)(2,1)S(1)} %get-tuple-element.74), channel_id=1, source_target_pairs={{0,10},{1,11},{2,8},{3,9},{4,14},{5,15},{6,12},{7,13},{8,2},{9,3},... | collective-permute-start | bytes 663560 | tf_op jit(solution)/shard_map/ppermute | solution.py:439
  36.9 0.7 copy-start.1
  54.9 36.5 %all-to-all-start.4 = ((bf16[8,144,768]{2,1,0:T(8,128)(2,1)}), bf16[8,144,768]{2,1,0:T(8,128)(2,1)S(1)}, u32[]{:S(2)}, u32[]{:S(2)}) async-start(bf16[8,144,768]{2,1,0:T(8,128)(2,1)} %bitcast.14), calls=%async_computation.4 | async-start | bytes 3538944 | tf_op jit(solution)/shard_map/all_to_all | solution.py:435
  58.6 25.0 %collective-permute-start.3 = (bf16[144,768]{1,0:T(8,128)(2,1)}, bf16[144,768]{1,0:T(8,128)(2,1)S(1)}, u32[]{:S(2)}, u32[]{:S(2)}) collective-permute-start(bf16[144,768]{1,0:T(8,128)(2,1)} %get-tuple-element.72), channel_id=1, source_target_pairs={{0,11},{1,10},{2,9},{3,8},{4,15},{5,14},{6,13},{7,12},{8,3},{9,2},... | collective-permute-start | bytes 663560 | tf_op jit(solution)/shard_map/ppermute | solution.py:439
  60.5 30.8 %collective-permute-start.4 = (bf16[144,768]{1,0:T(8,128)(2,1)}, bf16[144,768]{1,0:T(8,128)(2,1)S(1)}, u32[]{:S(2)}, u32[]{:S(2)}) collective-permute-start(bf16[144,768]{1,0:T(8,128)(2,1)} %copy-done.1), channel_id=1, source_target_pairs={{0,12},{1,13},{2,14},{3,15},{4,8},{5,9},{6,10},{7,11},{8,4},{9,5},... | collective-permute-start | bytes 663560 | tf_op jit(solution)/shard_map/ppermute | solution.py:439
  63.4 37.4 %collective-permute-start.5 = (bf16[144,768]{1,0:T(8,128)(2,1)S(1)}, bf16[144,768]{1,0:T(8,128)(2,1)}, u32[]{:S(2)}, u32[]{:S(2)}) collective-permute-start(bf16[144,768]{1,0:T(8,128)(2,1)S(1)} %get-tuple-element.80), channel_id=1, source_target_pairs={{0,13},{1,12},{2,15},{3,14},{4,9},{5,8},{6,11},{7,10},{8,5},{9,4},... | collective-permute-start | bytes 663560 | tf_op jit(solution)/shard_map/ppermute | solution.py:439
  64.0 37.4 %collective-permute-start.6 = (bf16[144,768]{1,0:T(8,128)(2,1)S(1)}, bf16[144,768]{1,0:T(8,128)(2,1)}, u32[]{:S(2)}, u32[]{:S(2)}) collective-permute-start(bf16[144,768]{1,0:T(8,128)(2,1)S(1)} %get-tuple-element.81), channel_id=1, source_target_pairs={{0,14},{1,15},{2,12},{3,13},{4,10},{5,11},{6,8},{7,9},{8,6},{9,7},... | collective-permute-start | bytes 663560 | tf_op jit(solution)/shard_map/ppermute | solution.py:439
  66.9 38.3 %collective-permute-start.7 = (bf16[144,768]{1,0:T(8,128)(2,1)S(1)}, bf16[144,768]{1,0:T(8,128)(2,1)}, u32[]{:S(2)}, u32[]{:S(2)}) collective-permute-start(bf16[144,768]{1,0:T(8,128)(2,1)S(1)} %get-tuple-element.82), channel_id=1, source_target_pairs={{0,15},{1,14},{2,13},{3,12},{4,11},{5,10},{6,9},{7,8},{8,7},{9,6},... | collective-permute-start | bytes 663560 | tf_op jit(solution)/shard_map/ppermute | solution.py:439
  68.5 0.8 copy-start.3
  71.3 1.0 copy-start.4
  72.4 0.6 copy-start.6
  91.4 1.3 %copy-start.5 = (f32[2304,128]{1,0:T(8,128)S(1)}, f32[2304,128]{1,0:T(8,128)}, u32[]{:S(2)}) copy-start(f32[2304,128]{1,0:T(8,128)} %copy-done.4) | copy-start | bytes 3538948
  92.6 0.7 copy-start.7
  93.3 11.9 %copy-start.8 = (f32[1,2304]{1,0:T(1,128)S(1)}, f32[1,2304]{1,0:T(1,128)}, u32[]{:S(2)}) copy-start(f32[1,2304]{1,0:T(1,128)} %copy-done.6) | copy-start | bytes 27652
  109.2 15.7 %all-to-all-start.5 = ((f32[16,1,144]{2,1,0:T(1,128)}), f32[16,1,144]{2,1,0:T(1,128)S(1)}, u32[]{:S(2)}, u32[]{:S(2)}) async-start(f32[16,1,144]{2,1,0:T(1,128)} %similar.3), calls=%async_computation.5 | async-start | bytes 32768 | tf_op jit(solution)/shard_map/all_to_all | solution.py:435
  125.3 0.6 copy-start.15

commit v4 on v3

--- a/solution.py
+++ b/solution.py
@@ -45,12 +45,13 @@
 
 def count_kernel(label_ref, count_ref):
     step = 512
-    ones = jnp.ones((count_ref.shape[0], step), BF16)
-    counts = jnp.zeros((count_ref.shape[0], CLUSTERS), F32)
+    partial = jnp.zeros((CLUSTERS, LANES), F32)
     for at in range(0, label_ref.shape[1], step):
-        hot = one_hot(label_ref[:, at : at + step] == iota((CLUSTERS, step), 0))
-        counts = counts + lax.dot_general(ones, hot, NT, preferred_element_type=F32)
-    count_ref[:, 0, :] = counts
+        hot = label_ref[:, at : at + step] == iota((CLUSTERS, step), 0)
+        hot = jnp.where(hot, jnp.float32(1), jnp.float32(0))
+        partial = functools.reduce(jnp.add, [hot[:, lane : lane + LANES] for lane in range(0, step, LANES)], partial)
+    counts = jnp.sum(jnp.transpose(partial), axis=0, keepdims=True)
+    count_ref[...] = jnp.broadcast_to(counts[None], count_ref.shape)
 
 
 def counted(labels, peers):
@@ -194,9 +195,16 @@
     )(me, counts, labels, ranks)
 
 
+def owner_of(me, number, peers):
+    half = peers // 2
+    return (me & -half) + number if number < half else me ^ number
+
+
 def sender_of(me, block, peers):
     half = peers // 2
-    return jnp.where(block < half, (me & -half) + block, me ^ block)
+    early = half - LATE
+    inside = (me & -half) + block - early
+    return jnp.where(block < early, me ^ (block + half), jnp.where(block < early + half, inside, me ^ block))
 
 
 def pack_kernel(cap, peers, numbers, me_ref, dest_ref, unit_ref, *block_refs):
@@ -209,7 +217,7 @@
         index = iota((len(some) * cap, 1), 0)
         slots = index
         for i, number in enumerate(some):
-            shift = (sender_of(me, number, peers) - i) * cap
+            shift = (owner_of(me, number, peers) - i) * cap
             slots = jnp.where((index >= i * cap) & (index < (i + 1) * cap), index + shift, slots)
         pick = one_hot(dest_ref[...] == slots)
         rows = jnp.dot(pick, unit_ref[...], preferred_element_type=F32).astype(BF16)
@@ -271,7 +279,7 @@
         ),
         in_specs=[pl.BlockSpec(memory_space=pltpu.SMEM)] + whole(1),
         out_specs=tuple(whole(3)),
-        cost_estimate=pl.CostEstimate(flops=1 << 28, bytes_accessed=1 << 22, transcendentals=0),
+        cost_estimate=pl.CostEstimate(flops=1 << 36, bytes_accessed=1 << 22, transcendentals=0),
         compiler_params=pltpu.CompilerParams(vmem_limit_bytes=SMALL_VMEM),
         name="keys",
     )(me, table)
@@ -322,16 +330,20 @@
             best_ref[left + i] = best[:, i * cap : (i + 1) * cap]
 
 
-def last_kernel(cap, known, me_ref, row_ref, col_ref, before_ref, *refs):
+def next_kernel(cap, known, here, me_ref, row_ref, col_ref, before_ref, *refs):
     *block_refs, best_ref = refs
     me = me_ref[0]
-    peers = best_ref.shape[0]
+    peers = row_ref.shape[1] // cap
+
+    def place(block):
+        return sender_of(me, block, peers) if here == peers else block
+
     tall = max(1, 576 // cap)
-    columns = rows_of(block_refs, cap, known, peers - known)
-    key_row = row_ref[:, known * cap :]
-    best = jnp.full((1, (peers - known) * cap), -1.0, F32)
-    for upper in range(0, peers, tall):
-        count = min(tall, peers - upper)
+    columns = rows_of(block_refs, cap, known, here - known)
+    key_row = row_ref[:, known * cap : here * cap]
+    best = jnp.full((1, (here - known) * cap), -1.0, F32)
+    for upper in range(0, here, tall):
+        count = min(tall, here - upper)
         rows = rows_of(block_refs, cap, upper, count)
         key_col = col_ref[upper * cap : (upper + count) * cap, :]
         parts = masked_parts(rows, columns, key_col, key_row, (known - upper) * cap)
@@ -343,9 +355,9 @@
             side = functools.reduce(jnp.maximum, parts[:-1] + [tail])
             for i in range(min(count, known - upper)):
                 across = jnp.max(jnp.transpose(side[i * cap : (i + 1) * cap]), axis=0, keepdims=True)
-                best_ref[sender_of(me, upper + i, peers)] = jnp.maximum(before_ref[upper + i], across)
-    for i in range(peers - known):
-        best_ref[sender_of(me, known + i, peers)] = best[:, i * cap : (i + 1) * cap]
+                best_ref[place(upper + i)] = jnp.maximum(before_ref[upper + i], across)
+    for i in range(here - known):
+        best_ref[place(known + i)] = best[:, i * cap : (i + 1) * cap]
 
 
 def call_bests(kernel, scalars, arrays, blocks, out_blocks, fresh, cap):
@@ -459,12 +471,14 @@
     arrived = [swap(block, number, peers) for block, number in zip(leaving, across)]
     inside, _, *arrived[:EARLY] = lax.optimization_barrier((inside, leaving[EARLY], *arrived[:EARLY]))
     inside = exchange(inside.reshape(half, cap, width), [list(range(half)), list(range(half, peers))])
-    blocks = [inside.reshape(half * cap, width)] + arrived
     key_row, key_col, most = keys(me, table, cap)
-    known = peers - LATE
-    first = functools.partial(first_kernel, cap, known)
-    best = call_bests(first, [], [key_row, key_col], blocks[: len(blocks) - LATE], known, known, cap)
-    last = functools.partial(last_kernel, cap, known)
+    early = half - LATE
+    blocks = arrived[:early] + [inside.reshape(half * cap, width)] + arrived[early:]
+    first = functools.partial(first_kernel, cap, early)
+    best = call_bests(first, [], [key_row, key_col], blocks[:early], early, early, cap)
+    middle = functools.partial(next_kernel, cap, early, early + half)
+    best = call_bests(middle, [me], [key_row, key_col, best], blocks[: early + 1], early + half, half, cap)
+    last = functools.partial(next_kernel, cap, early + half, peers)
     best = call_bests(last, [me], [key_row, key_col, best], blocks, peers, LATE, cap)
     back = exchange(best)
     nearest = results(dest, back).reshape(count)

time: 126 us -> 125 us (level)
  starting transfers between devices: 34.1 us -> 30.7 us
  waiting for transfers between devices: 47.7 us -> 50.3 us
    all_to_all x3, waiting for transfers between devices: 7.62 us -> 15.2 us  [exchange(): lax.all_to_all(blocks, 'rows', split_axis=0, concat_axis=0, tiled=True, a...]
    all_to_all x3, starting transfers between devices: 20.3 us -> 14.6 us  [exchange(): lax.all_to_all(blocks, 'rows', split_axis=0, concat_axis=0, tiled=True, a...]
    ppermute x8, waiting for transfers between devices: 40.1 us -> 35.1 us  [swap(): return lax.ppermute(block, 'rows', [(i, i ^ number) for i in range(peers)])]
    ppermute x8, starting transfers between devices: 13.8 us -> 16 us  [swap(): return lax.ppermute(block, 'rows', [(i, i ^ number) for i in range(peers)])]
    pallas_call x2 -> x3, Pallas kernels: 11.4 us -> 9.72 us  [call_bests(): pl.pallas_call(kernel, out_shape=jax.ShapeDtypeStruct((out_blocks, 1, cap...]
    pallas_call x1, Pallas kernels: 1.02 us -> 2.6 us  [unit_rows(): pl.pallas_call(unit_kernel, out_shape=jax.ShapeDtypeStruct((count, width)...]
    unnamed x28 -> x26, local copies, waits for them, and re-layouts: 8.17 us -> 7.56 us
  transfers between devices with their start and end apart: 11 -> 11, of which waited for: 9 -> 8; matrix products, arithmetic and copies ran while one was open for 0% -> 0% of each run, Pallas kernels for 17% -> 16%
where the time goes in v4:
time: 125 us; the launch traced here: 124 us
  waiting for transfers between devices  50.3 us (40%)
  Pallas kernels  34.4 us (28%)
  starting transfers between devices  30.7 us (25%)
  local copies, waits for them, and re-layouts  8.1 us (6%)
    ppermute x8, waiting for transfers between devices, swap(): return lax.ppermute(block, 'rows', [(i, i ^ number) for i in range(peers)])  35.1 us
    ppermute x8, starting transfers between devices, swap(): return lax.ppermute(block, 'rows', [(i, i ^ number) for i in range(peers)])  16 us
    all_to_all x3, waiting for transfers between devices, exchange(): lax.all_to_all(blocks, 'rows', split_axis=0, concat_axis=0, tiled=True, a...  15.2 us
    all_to_all x3, starting transfers between devices, exchange(): lax.all_to_all(blocks, 'rows', split_axis=0, concat_axis=0, tiled=True, a...  14.6 us
    pallas_call x3, Pallas kernels, packed(): pl.pallas_call(functools.partial(pack_kernel, cap, peers, numbers), out_s...  11.6 us
    pallas_call x3, Pallas kernels, call_bests(): pl.pallas_call(kernel, out_shape=jax.ShapeDtypeStruct((out_blocks, 1, cap...  9.72 us
    unnamed x26, local copies, waits for them, and re-layouts  7.56 us
    pallas_call x1, Pallas kernels, places(): pl.pallas_call(functools.partial(place_kernel, cap), out_shape=(jax.Shape...  4.69 us
  transfers between devices with their start and end apart: 11, of which 8 were waited for; matrix products, arithmetic and copies ran while one was open for 0% of the time, Pallas kernels for 16%

profile of v4, /device:TPU:0, one launch (start us, length us, event | category | flops | bytes accessed | tf_op | source)
XLA Modules:
  0.0 124.2 jit_solution(171136254664997371)
XLA Ops:
  0.0 1.9 %counts.1 = f32[16,1,512]{2,1,0:T(1,128)} custom-call(s32[1,2048]{1,0:T(1,128)} %bitcast.47), custom_call_target="tpu_custom_call" | custom-call | tf_op jit(solution)/shard_map/counts/pallas_call | solution.py:58
  1.9 7.4 %all-to-all-start.3 = ((f32[16,1,512]{2,1,0:T(1,128)}), f32[16,1,512]{2,1,0:T(1,128)S(1)}, u32[]{:S(2)}, u32[]{:S(2)}) async-start(f32[16,1,512]{2,1,0:T(1,128)} %counts.1), calls=%async_computation.3 | async-start | bytes 65536 | tf_op jit(solution)/shard_map/all_to_all | solution.py:447
  9.3 1.9 %copy-done = bf16[2048,768]{1,0:T(8,128)(2,1)S(1)} copy-done((bf16[2048,768]{1,0:T(8,128)(2,1)S(1)}, bf16[2048,768]{1,0:T(8,128)(2,1)}, u32[]{:S(2)}) %copy-start) | copy-done | bytes 3145752
  11.2 2.6 %unit.1.unit_ref = bf16[2048,768]{1,0:T(8,128)(2,1)} custom-call(bf16[2048,768]{1,0:T(8,128)(2,1)S(1)} %copy-done), custom_call_target="tpu_custom_call" | custom-call | flops 6291456 | bytes 6291456 | tf_op jit(solution)/shard_map/unit/pallas_call | solution.py:102
  13.8 1.4 %ranks.1.rank_ref = s32[1,2048]{1,0:T(1,128)S(1)} custom-call(s32[1,2048]{1,0:T(1,128)S(1)} %bitcast.48), custom_call_target="tpu_custom_call" | custom-call | flops 8388608 | bytes 4194304 | tf_op jit(solution)/shard_map/ranks/pallas_call | solution.py:81
  15.9 4.7 %places.1 = (s32[1,2048]{1,0:T(1,128)S(1)}, f32[24,512]{1,0:T(8,128)S(1)}) custom-call(s32[1]{0:T(128)} %bitcast.11.me_ref, f32[16,1,512]{2,1,0:T(1,128)S(1)} %all-to-all-done.3.count_ref, s32[1,2048]{1,0:T(1,128)S(1)} %bitcast.49, s32[1,2048]{1,0:T(1,128)S(1)} %ranks.1.rank_ref), custom_call_target="tpu_custom_call" | custom-call | tf_op jit(solution)/shard_map/places/pallas_call | solution.py:188
  20.6 3.4 %pack.3 = (bf16[144,768]{1,0:T(8,128)(2,1)S(1)}, bf16[144,768]{1,0:T(8,128)(2,1)S(1)}, bf16[144,768]{1,0:T(8,128)(2,1)S(1)}) custom-call(s32[1]{0:T(128)} %bitcast.11.me_ref, s32[1,2048]{1,0:T(1,128)S(1)} %get-tuple-element.71.dest_ref, bf16[2048,768]{1,0:T(8,128)(2,1)} %unit.1.unit_ref), custom_call_target="tpu_custom_call" | custom-call | flops 1358954496 | bytes 3809280 | tf_op jit(solution)/shard_map/pack/pallas_call | solution.py:233
  24.1 2.2 %collective-permute-start = (bf16[144,768]{1,0:T(8,128)(2,1)S(1)}, bf16[144,768]{1,0:T(8,128)(2,1)S(1)}, u32[]{:S(2)}, u32[]{:S(2)}) collective-permute-start(bf16[144,768]{1,0:T(8,128)(2,1)S(1)} %get-tuple-element.70), channel_id=1, source_target_pairs={{0,8},{1,9},{2,10},{3,11},{4,12},{5,13},{6,14},{7,15},{8,0},{9,1},... | collective-permute-start | bytes 663560 | tf_op jit(solution)/shard_map/ppermute | solution.py:451
  26.3 3.1 %pack.5 = (bf16[144,768]{1,0:T(8,128)(2,1)}, bf16[144,768]{1,0:T(8,128)(2,1)}, bf16[144,768]{1,0:T(8,128)(2,1)S(1)}, bf16[144,768]{1,0:T(8,128)(2,1)S(1)}, bf16[144,768]{1,0:T(8,128)(2,1)S(1)}) custom-call(s32[1]{0:T(128)} %bitcast.11.me_ref, s32[1,2048]{1,0:T(1,128)S(1)} %get-tuple-element.71.dest_ref, bf16[2048,768]{1,0:T(8,128)(2,1)S(1)} %copy-done.9), custom_call_target="tpu_custom_call" | custom-call | flops 2264924160 | bytes 4251648 | tf_op jit(solution)/shard_map/pack/pallas_call | solution.py:233
  29.4 3.3 %collective-permute-start.2 = (bf16[144,768]{1,0:T(8,128)(2,1)S(1)}, bf16[144,768]{1,0:T(8,128)(2,1)S(1)}, u32[]{:S(2)}, u32[]{:S(2)}) collective-permute-start(bf16[144,768]{1,0:T(8,128)(2,1)S(1)} %get-tuple-element.74), channel_id=1, source_target_pairs={{0,10},{1,11},{2,8},{3,9},{4,14},{5,15},{6,12},{7,13},{8,2},{9,3},... | collective-permute-start | bytes 663560 | tf_op jit(solution)/shard_map/ppermute | solution.py:451
  32.7 0.8 collective-permute-start.3
  33.5 3.0 %collective-permute-start.4 = (bf16[144,768]{1,0:T(8,128)(2,1)}, bf16[144,768]{1,0:T(8,128)(2,1)S(1)}, u32[]{:S(2)}, u32[]{:S(2)}) collective-permute-start(bf16[144,768]{1,0:T(8,128)(2,1)} %get-tuple-element.78), channel_id=1, source_target_pairs={{0,12},{1,13},{2,14},{3,15},{4,8},{5,9},{6,10},{7,11},{8,4},{9,5},... | collective-permute-start | bytes 663560 | tf_op jit(solution)/shard_map/ppermute | solution.py:451
  36.5 5.1 %pack.4 = bf16[1152,768]{1,0:T(8,128)(2,1)} custom-call(s32[1]{0:T(128)} %bitcast.11.me_ref, s32[1,2048]{1,0:T(1,128)S(1)} %get-tuple-element.71.dest_ref, bf16[2048,768]{1,0:T(8,128)(2,1)S(1)} %copy-done.9), custom_call_target="tpu_custom_call" | custom-call | flops 3623878656 | bytes 4915200 | tf_op jit(solution)/shard_map/pack/pallas_call | solution.py:233
  41.5 15.5 %collective-permute-done.refs_0_ = bf16[144,768]{1,0:T(8,128)(2,1)S(1)} collective-permute-done((bf16[144,768]{1,0:T(8,128)(2,1)S(1)}, bf16[144,768]{1,0:T(8,128)(2,1)S(1)}, u32[]{:S(2)}, u32[]{:S(2)}) %collective-permute-start) | collective-permute-done | bytes 221216 | tf_op jit(solution)/shard_map/ppermute | solution.py:451
  57.0 2.3 %collective-permute-done.1.refs_1_ = bf16[144,768]{1,0:T(8,128)(2,1)S(1)} collective-permute-done((bf16[144,768]{1,0:T(8,128)(2,1)S(1)}, bf16[144,768]{1,0:T(8,128)(2,1)S(1)}, u32[]{:S(2)}, u32[]{:S(2)}) %collective-permute-start.1) | collective-permute-done | bytes 221216 | tf_op jit(solution)/shard_map/ppermute | solution.py:451
  59.3 7.9 %collective-permute-done.2.refs_2_ = bf16[144,768]{1,0:T(8,128)(2,1)S(1)} collective-permute-done((bf16[144,768]{1,0:T(8,128)(2,1)S(1)}, bf16[144,768]{1,0:T(8,128)(2,1)S(1)}, u32[]{:S(2)}, u32[]{:S(2)}) %collective-permute-start.2) | collective-permute-done | bytes 221216 | tf_op jit(solution)/shard_map/ppermute | solution.py:451
  67.1 3.8 %all-to-all-start.4 = ((bf16[8,144,768]{2,1,0:T(8,128)(2,1)}), bf16[8,144,768]{2,1,0:T(8,128)(2,1)S(1)}, u32[]{:S(2)}, u32[]{:S(2)}) async-start(bf16[8,144,768]{2,1,0:T(8,128)(2,1)} %bitcast.14), calls=%async_computation.4 | async-start | bytes 3538944 | tf_op jit(solution)/shard_map/all_to_all | solution.py:447
  70.9 0.8 copy-done.2
  71.7 2.0 %keys.1 = (f32[1,2304]{1,0:T(1,128)S(1)}, f32[2304,128]{1,0:T(8,128)S(1)}, f32[8,128]{1,0:T(8,128)S(1)}) custom-call(s32[1]{0:T(128)} %bitcast.11.me_ref, f32[24,512]{1,0:T(8,128)S(1)} %copy-done.2), custom_call_target="tpu_custom_call" | custom-call | flops 68719476736 | bytes 4194304 | tf_op jit(solution)/shard_map/keys/pallas_call | solution.py:273
  73.8 2.1 %collective-permute-start.5 = (bf16[144,768]{1,0:T(8,128)(2,1)S(1)}, bf16[144,768]{1,0:T(8,128)(2,1)}, u32[]{:S(2)}, u32[]{:S(2)}) collective-permute-start(bf16[144,768]{1,0:T(8,128)(2,1)S(1)} %get-tuple-element.80), channel_id=1, source_target_pairs={{0,13},{1,12},{2,15},{3,14},{4,9},{5,8},{6,11},{7,10},{8,5},{9,4},... | collective-permute-start | bytes 663560 | tf_op jit(solution)/shard_map/ppermute | solution.py:451
  75.9 2.7 %collective-permute-start.6 = (bf16[144,768]{1,0:T(8,128)(2,1)S(1)}, bf16[144,768]{1,0:T(8,128)(2,1)}, u32[]{:S(2)}, u32[]{:S(2)}) collective-permute-start(bf16[144,768]{1,0:T(8,128)(2,1)S(1)} %get-tuple-element.81), channel_id=1, source_target_pairs={{0,14},{1,15},{2,12},{3,13},{4,10},{5,11},{6,8},{7,9},{8,6},{9,7},... | collective-permute-start | bytes 663560 | tf_op jit(solution)/shard_map/ppermute | solution.py:451
  78.6 1.9 %collective-permute-start.7 = (bf16[144,768]{1,0:T(8,128)(2,1)S(1)}, bf16[144,768]{1,0:T(8,128)(2,1)}, u32[]{:S(2)}, u32[]{:S(2)}) collective-permute-start(bf16[144,768]{1,0:T(8,128)(2,1)S(1)} %get-tuple-element.82), channel_id=1, source_target_pairs={{0,15},{1,14},{2,13},{3,12},{4,11},{5,10},{6,9},{7,8},{8,7},{9,6},... | collective-permute-start | bytes 663560 | tf_op jit(solution)/shard_map/ppermute | solution.py:451
  80.5 1.5 %similar.3.before_ref = f32[5,1,144]{2,1,0:T(1,128)S(1)} custom-call(f32[1,2304]{1,0:T(1,128)S(1)} %get-tuple-element.68.row_ref, f32[2304,128]{1,0:T(8,128)S(1)} %get-tuple-element.69.col_ref, bf16[144,768]{1,0:T(8,128)(2,1)S(1)} %collective-permute-done.refs_0_, bf16[144,768]{1,0:T(8,128)(2,1)S(1)} %collective-permute-done.1.refs_1_, ...), custom_call_target="tpu_custom_call" | custom-call | flops 796262400 | bytes 8388608 | tf_op jit(solution)/shard_map/similar/pallas_call | solution.py:365
  82.1 1.0 copy-done.3
  83.7 9.2 %all-to-all-done.4 = bf16[8,144,768]{2,1,0:T(8,128)(2,1)S(1)} async-done(((bf16[8,144,768]{2,1,0:T(8,128)(2,1)}), bf16[8,144,768]{2,1,0:T(8,128)(2,1)S(1)}, u32[]{:S(2)}, u32[]{:S(2)}) %all-to-all-start.4) | async-done | bytes 1769504 | tf_op jit(solution)/shard_map/all_to_all | solution.py:447
  92.8 1.3 %copy-done.4 = f32[2304,128]{1,0:T(8,128)S(1)} copy-done((f32[2304,128]{1,0:T(8,128)S(1)}, f32[2304,128]{1,0:T(8,128)}, u32[]{:S(2)}) %copy-start.4) | copy-done | bytes 1179672
  95.5 4.3 %similar.4.before_ref = f32[13,1,144]{2,1,0:T(1,128)S(1)} custom-call(s32[1]{0:T(128)} %bitcast.11.me_ref, f32[1,2304]{1,0:T(1,128)S(1)} %copy-done.6, f32[2304,128]{1,0:T(8,128)S(1)} %copy-done.4, f32[5,1,144]{2,1,0:T(1,128)S(1)} %copy-done.8, bf16[144,768]{1,0:T(8,128)(2,1)S(1)} %collective-permute-done.refs_0_, ...), custom_call_target="tpu_custom_call" | custom-call | flops 3312451584 | bytes 8388608 | tf_op jit(solution)/shard_map/similar/pallas_call | solution.py:365
  99.8 5.7 %collective-permute-done.6.refs_7_ = bf16[144,768]{1,0:T(8,128)(2,1)} collective-permute-done((bf16[144,768]{1,0:T(8,128)(2,1)S(1)}, bf16[144,768]{1,0:T(8,128)(2,1)}, u32[]{:S(2)}, u32[]{:S(2)}) %collective-permute-start.6) | collective-permute-done | bytes 221216 | tf_op jit(solution)/shard_map/ppermute | solution.py:451
  105.4 3.8 %collective-permute-done.7.refs_8_ = bf16[144,768]{1,0:T(8,128)(2,1)} collective-permute-done((bf16[144,768]{1,0:T(8,128)(2,1)S(1)}, bf16[144,768]{1,0:T(8,128)(2,1)}, u32[]{:S(2)}, u32[]{:S(2)}) %collective-permute-start.7) | collective-permute-done | bytes 221216 | tf_op jit(solution)/shard_map/ppermute | solution.py:451
  109.2 3.9 %similar.5 = f32[16,1,144]{2,1,0:T(1,128)} custom-call(s32[1]{0:T(128)} %bitcast.11.me_ref, f32[1,2304]{1,0:T(1,128)S(1)} %copy-done.6, f32[2304,128]{1,0:T(8,128)S(1)} %copy-done.4, f32[13,1,144]{2,1,0:T(1,128)S(1)} %similar.4.before_ref, bf16[144,768]{1,0:T(8,128)(2,1)S(1)} %collective-permute-done.refs_0_, ...), custom_call_target="tpu_custom_call" | custom-call | flops 1528823808 | bytes 8388608 | tf_op jit(solution)/shard_map/similar/pallas_call | solution.py:365
  113.2 3.5 %all-to-all-start.5 = ((f32[16,1,144]{2,1,0:T(1,128)}), f32[16,1,144]{2,1,0:T(1,128)S(1)}, u32[]{:S(2)}, u32[]{:S(2)}) async-start(f32[16,1,144]{2,1,0:T(1,128)} %similar.5), calls=%async_computation.5 | async-start | bytes 32768 | tf_op jit(solution)/shard_map/all_to_all | solution.py:447
  117.8 5.3 %all-to-all-done.5.back_ref = f32[16,1,144]{2,1,0:T(1,128)S(1)} async-done(((f32[16,1,144]{2,1,0:T(1,128)}), f32[16,1,144]{2,1,0:T(1,128)S(1)}, u32[]{:S(2)}, u32[]{:S(2)}) %all-to-all-start.5) | async-done | bytes 9248 | tf_op jit(solution)/shard_map/all_to_all | solution.py:447
  (30 shorter events, 4.3 us)
Async XLA Ops:
  0.0 13.8 %copy-start.10 = (s32[2048,1]{0,1:T(1,128)S(1)}, s32[2048,1]{0,1:T(1,128)}, u32[]{:S(2)}) copy-start(s32[2048,1]{0,1:T(1,128)} %param.7) | copy-start | bytes 24580
  1.9 14.0 %all-to-all-start.3 = ((f32[16,1,512]{2,1,0:T(1,128)}), f32[16,1,512]{2,1,0:T(1,128)S(1)}, u32[]{:S(2)}, u32[]{:S(2)}) async-start(f32[16,1,512]{2,1,0:T(1,128)} %counts.1), calls=%async_computation.3 | async-start | bytes 65536 | tf_op jit(solution)/shard_map/all_to_all | solution.py:447
  9.3 1.9 %copy-start = (bf16[2048,768]{1,0:T(8,128)(2,1)S(1)}, bf16[2048,768]{1,0:T(8,128)(2,1)}, u32[]{:S(2)}) copy-start(bf16[2048,768]{1,0:T(8,128)(2,1)} %rows_ref.1) | copy-start | bytes 9437188
  15.2 8.9 %copy-start.12 = (s32[1,2048]{1,0:T(1,128)}, s32[1,2048]{1,0:T(1,128)S(1)}, u32[]{:S(2)}) copy-start(s32[1,2048]{1,0:T(1,128)S(1)} %ranks.1.rank_ref) | copy-start | bytes 24580
  15.9 10.4 %copy-start.9 = (bf16[2048,768]{1,0:T(8,128)(2,1)S(1)}, bf16[2048,768]{1,0:T(8,128)(2,1)}, u32[]{:S(2)}) copy-start(bf16[2048,768]{1,0:T(8,128)(2,1)} %unit.1.unit_ref) | copy-start | bytes 9437188
  20.6 8.8 %copy-start.1 = (f32[24,512]{1,0:T(8,128)}, f32[24,512]{1,0:T(8,128)S(1)}, u32[]{:S(2)}) copy-start(f32[24,512]{1,0:T(8,128)S(1)} %get-tuple-element.65.table_ref) | copy-start | bytes 147460
  24.1 32.9 %collective-permute-start = (bf16[144,768]{1,0:T(8,128)(2,1)S(1)}, bf16[144,768]{1,0:T(8,128)(2,1)S(1)}, u32[]{:S(2)}, u32[]{:S(2)}) collective-permute-start(bf16[144,768]{1,0:T(8,128)(2,1)S(1)} %get-tuple-element.70), channel_id=1, source_target_pairs={{0,8},{1,9},{2,10},{3,11},{4,12},{5,13},{6,14},{7,15},{8,0},{9,1},... | collective-permute-start | bytes 663560 | tf_op jit(solution)/shard_map/ppermute | solution.py:451
  29.4 29.9 %collective-permute-start.1 = (bf16[144,768]{1,0:T(8,128)(2,1)S(1)}, bf16[144,768]{1,0:T(8,128)(2,1)S(1)}, u32[]{:S(2)}, u32[]{:S(2)}) collective-permute-start(bf16[144,768]{1,0:T(8,128)(2,1)S(1)} %get-tuple-element.73), channel_id=1, source_target_pairs={{0,9},{1,8},{2,11},{3,10},{4,13},{5,12},{6,15},{7,14},{8,1},{9,0},... | collective-permute-start | bytes 663560 | tf_op jit(solution)/shard_map/ppermute | solution.py:451
  29.4 37.8 %collective-permute-start.2 = (bf16[144,768]{1,0:T(8,128)(2,1)S(1)}, bf16[144,768]{1,0:T(8,128)(2,1)S(1)}, u32[]{:S(2)}, u32[]{:S(2)}) collective-permute-start(bf16[144,768]{1,0:T(8,128)(2,1)S(1)} %get-tuple-element.74), channel_id=1, source_target_pairs={{0,10},{1,11},{2,8},{3,9},{4,14},{5,15},{6,12},{7,13},{8,2},{9,3},... | collective-permute-start | bytes 663560 | tf_op jit(solution)/shard_map/ppermute | solution.py:451
  32.7 47.8 %collective-permute-start.3 = (bf16[144,768]{1,0:T(8,128)(2,1)}, bf16[144,768]{1,0:T(8,128)(2,1)S(1)}, u32[]{:S(2)}, u32[]{:S(2)}) collective-permute-start(bf16[144,768]{1,0:T(8,128)(2,1)} %get-tuple-element.72), channel_id=1, source_target_pairs={{0,11},{1,10},{2,9},{3,8},{4,15},{5,14},{6,13},{7,12},{8,3},{9,2},... | collective-permute-start | bytes 663560 | tf_op jit(solution)/shard_map/ppermute | solution.py:451
  33.5 47.1 %collective-permute-start.4 = (bf16[144,768]{1,0:T(8,128)(2,1)}, bf16[144,768]{1,0:T(8,128)(2,1)S(1)}, u32[]{:S(2)}, u32[]{:S(2)}) collective-permute-start(bf16[144,768]{1,0:T(8,128)(2,1)} %get-tuple-element.78), channel_id=1, source_target_pairs={{0,12},{1,13},{2,14},{3,15},{4,8},{5,9},{6,10},{7,11},{8,4},{9,5},... | collective-permute-start | bytes 663560 | tf_op jit(solution)/shard_map/ppermute | solution.py:451
  67.1 25.7 %all-to-all-start.4 = ((bf16[8,144,768]{2,1,0:T(8,128)(2,1)}), bf16[8,144,768]{2,1,0:T(8,128)(2,1)S(1)}, u32[]{:S(2)}, u32[]{:S(2)}) async-start(bf16[8,144,768]{2,1,0:T(8,128)(2,1)} %bitcast.14), calls=%async_computation.4 | async-start | bytes 3538944 | tf_op jit(solution)/shard_map/all_to_all | solution.py:447
  70.9 0.8 copy-start.2
  73.7 6.8 %copy-start.5 = (f32[1,2304]{1,0:T(1,128)}, f32[1,2304]{1,0:T(1,128)S(1)}, u32[]{:S(2)}) copy-start(f32[1,2304]{1,0:T(1,128)S(1)} %get-tuple-element.68.row_ref) | copy-start | bytes 27652
  73.8 26.0 %collective-permute-start.5 = (bf16[144,768]{1,0:T(8,128)(2,1)S(1)}, bf16[144,768]{1,0:T(8,128)(2,1)}, u32[]{:S(2)}, u32[]{:S(2)}) collective-permute-start(bf16[144,768]{1,0:T(8,128)(2,1)S(1)} %get-tuple-element.80), channel_id=1, source_target_pairs={{0,13},{1,12},{2,15},{3,14},{4,9},{5,8},{6,11},{7,10},{8,5},{9,4},... | collective-permute-start | bytes 663560 | tf_op jit(solution)/shard_map/ppermute | solution.py:451
  75.9 29.6 %collective-permute-start.6 = (bf16[144,768]{1,0:T(8,128)(2,1)S(1)}, bf16[144,768]{1,0:T(8,128)(2,1)}, u32[]{:S(2)}, u32[]{:S(2)}) collective-permute-start(bf16[144,768]{1,0:T(8,128)(2,1)S(1)} %get-tuple-element.81), channel_id=1, source_target_pairs={{0,14},{1,15},{2,12},{3,13},{4,10},{5,11},{6,8},{7,9},{8,6},{9,7},... | collective-permute-start | bytes 663560 | tf_op jit(solution)/shard_map/ppermute | solution.py:451
  78.6 30.6 %collective-permute-start.7 = (bf16[144,768]{1,0:T(8,128)(2,1)S(1)}, bf16[144,768]{1,0:T(8,128)(2,1)}, u32[]{:S(2)}, u32[]{:S(2)}) collective-permute-start(bf16[144,768]{1,0:T(8,128)(2,1)S(1)} %get-tuple-element.82), channel_id=1, source_target_pairs={{0,15},{1,14},{2,13},{3,12},{4,11},{5,10},{6,9},{7,8},{8,7},{9,6},... | collective-permute-start | bytes 663560 | tf_op jit(solution)/shard_map/ppermute | solution.py:451
  82.1 1.0 copy-start.3
  83.1 0.6 copy-start.7
  92.8 1.3 %copy-start.4 = (f32[2304,128]{1,0:T(8,128)S(1)}, f32[2304,128]{1,0:T(8,128)}, u32[]{:S(2)}) copy-start(f32[2304,128]{1,0:T(8,128)} %copy-done.3) | copy-start | bytes 3538948
  94.1 0.7 copy-start.6
  94.8 0.7 copy-start.8
  113.2 10.0 %all-to-all-start.5 = ((f32[16,1,144]{2,1,0:T(1,128)}), f32[16,1,144]{2,1,0:T(1,128)S(1)}, u32[]{:S(2)}, u32[]{:S(2)}) async-start(f32[16,1,144]{2,1,0:T(1,128)} %similar.5), calls=%async_computation.5 | async-start | bytes 32768 | tf_op jit(solution)/shard_map/all_to_all | solution.py:447
  123.6 0.6 copy-start.14

commit v5 on v4

--- a/solution.py
+++ b/solution.py
@@ -19,6 +19,7 @@
 BF16, F32, I32 = jnp.bfloat16, jnp.float32, jnp.int32
 VMEM_LIMIT = 24 * 1024 * 1024
 SMALL_VMEM = 12 * 1024 * 1024
+LARGE_VMEM = 60 * 1024 * 1024
 NT = (((1,), (1,)), ((), ()))
 
 
@@ -97,7 +98,7 @@
 
 def unit_rows(embeddings):
     count, width = embeddings.shape
-    step = min(512, count)
+    step = min(1024, count)
     spec = pl.BlockSpec((step, width), lambda i: (i, 0))
     return pl.pallas_call(
         unit_kernel,
@@ -106,7 +107,7 @@
         in_specs=[spec],
         out_specs=spec,
         cost_estimate=pl.CostEstimate(flops=4 * count * width, bytes_accessed=4 * count * width, transcendentals=count),
-        compiler_params=pltpu.CompilerParams(vmem_limit_bytes=SMALL_VMEM),
+        compiler_params=pltpu.CompilerParams(vmem_limit_bytes=LARGE_VMEM),
         name="unit",
     )(embeddings)
 
@@ -183,18 +184,6 @@
         dest_ref[:, at : at + step] = slot + rank_ref[:, at : at + step]
 
 
-def places(me, counts, labels, ranks, cap):
-    peers = counts.shape[0]
-    return pl.pallas_call(
-        functools.partial(place_kernel, cap),
-        out_shape=(jax.ShapeDtypeStruct(labels.shape, I32), jax.ShapeDtypeStruct((peers + 8, CLUSTERS), F32)),
-        in_specs=[pl.BlockSpec(memory_space=pltpu.SMEM)] + whole(3),
-        out_specs=tuple(whole(2)),
-        compiler_params=pltpu.CompilerParams(vmem_limit_bytes=SMALL_VMEM),
-        name="places",
-    )(me, counts, labels, ranks)
-
-
 def owner_of(me, number, peers):
     half = peers // 2
     return (me & -half) + number if number < half else me ^ number
@@ -207,9 +196,7 @@
     return jnp.where(block < early, me ^ (block + half), jnp.where(block < early + half, inside, me ^ block))
 
 
-def pack_kernel(cap, peers, numbers, me_ref, dest_ref, unit_ref, *block_refs):
-    me = me_ref[0]
-    count = dest_ref.shape[1]
+def pick_blocks(cap, peers, numbers, me, dest, unit_ref, block_refs):
     per_ref = block_refs[0].shape[0] // cap
     group = 4
     for at in range(0, len(numbers), group):
@@ -219,11 +206,43 @@
         for i, number in enumerate(some):
             shift = (owner_of(me, number, peers) - i) * cap
             slots = jnp.where((index >= i * cap) & (index < (i + 1) * cap), index + shift, slots)
-        pick = one_hot(dest_ref[...] == slots)
+        pick = one_hot(dest == slots)
         rows = jnp.dot(pick, unit_ref[...], preferred_element_type=F32).astype(BF16)
         for i in range(len(some)):
             block, within = divmod(at + i, per_ref)
             block_refs[block][within * cap : (within + 1) * cap, :] = rows[i * cap : (i + 1) * cap]
+
+
+def pack_kernel(cap, peers, numbers, me_ref, dest_ref, unit_ref, *block_refs):
+    pick_blocks(cap, peers, numbers, me_ref[0], dest_ref[...], unit_ref, block_refs)
+
+
+def place_pack_kernel(cap, peers, numbers, me_ref, count_ref, label_ref, rank_ref, unit_ref, dest_ref, table_ref, *refs):
+    *block_refs, held, arrived = refs
+    copy = pltpu.make_async_copy(unit_ref, held, arrived)
+    copy.start()
+    place_kernel(cap, me_ref, count_ref, label_ref, rank_ref, dest_ref, table_ref)
+    copy.wait()
+    pick_blocks(cap, peers, numbers, me_ref[0], dest_ref[...], held, block_refs)
+
+
+def places_and_packed(me, counts, labels, ranks, unit, cap, numbers):
+    peers = counts.shape[0]
+    width = unit.shape[1]
+    dest, table, *blocks = pl.pallas_call(
+        functools.partial(place_pack_kernel, cap, peers, numbers),
+        out_shape=(
+            jax.ShapeDtypeStruct(labels.shape, I32),
+            jax.ShapeDtypeStruct((peers + 8, CLUSTERS), F32),
+            *[jax.ShapeDtypeStruct((cap, width), BF16)] * len(numbers),
+        ),
+        in_specs=[pl.BlockSpec(memory_space=pltpu.SMEM)] + whole(3) + [pl.BlockSpec(memory_space=pl.ANY)],
+        out_specs=tuple(whole(2 + len(numbers))),
+        scratch_shapes=[pltpu.VMEM(unit.shape, BF16), pltpu.SemaphoreType.DMA(())],
+        compiler_params=pltpu.CompilerParams(vmem_limit_bytes=VMEM_LIMIT),
+        name="places",
+    )(me, counts, labels, ranks, unit)
+    return dest, table, blocks
 
 
 def packed(me, dest, unit, cap, peers, numbers, per_block=1):
@@ -460,13 +479,12 @@
     ranks = ranked(labels)
     unit = unit_rows(embeddings)
     me = lax.axis_index("rows").reshape(1)
-    dest, table = places(me, counts, labels, ranks, cap)
 
     half = peers // 2
     across = list(range(half, peers))
-    leaving = packed(me, dest, unit, cap, peers, across[:EARLY])
+    dest, table, leaving = places_and_packed(me, counts, labels, ranks, unit, cap, across[:EARLY])
     later, _ = lax.optimization_barrier((dest, leaving[0]))
-    leaving += packed(me, later, unit, cap, peers, across[EARLY:])
+    leaving += list(packed(me, later, unit, cap, peers, across[EARLY:]))
     (inside,) = packed(me, later, unit, cap, peers, list(range(half)), half)
     arrived = [swap(block, number, peers) for block, number in zip(leaving, across)]
     inside, _, *arrived[:EARLY] = lax.optimization_barrier((inside, leaving[EARLY], *arrived[:EARLY]))

time: 125 us -> 121 us (0.968)
  starting transfers between devices: 30.7 us -> 28.1 us
  local copies, waits for them, and re-layouts: 8.1 us -> 6.27 us
    ppermute x8, starting transfers between devices: 16 us -> 13.5 us  [swap(): return lax.ppermute(block, 'rows', [(i, i ^ number) for i in range(peers)])]
    all_to_all x3, waiting for transfers between devices: 15.2 us -> 17.6 us  [exchange(): lax.all_to_all(blocks, 'rows', split_axis=0, concat_axis=0, tiled=True, a...]
    ppermute x8, waiting for transfers between devices: 35.1 us -> 33 us  [swap(): return lax.ppermute(block, 'rows', [(i, i ^ number) for i in range(peers)])]
    unnamed x26, local copies, waits for them, and re-layouts: 7.56 us -> 5.68 us
    pallas_call x1, Pallas kernels: 4.69 us -> 6.46 us  [places_and_packed(): pl.pallas_call(functools.partial(place_pack_kernel, cap, peers, numbers),...]
    pallas_call x3 -> x2, Pallas kernels: 11.6 us -> 10.3 us  [packed(): pl.pallas_call(functools.partial(pack_kernel, cap, peers, numbers), out_s...]
  transfers between devices with their start and end apart: 11 -> 11, of which waited for: 8 -> 8; matrix products, arithmetic and copies ran while one was open for 0% -> 0% of each run, Pallas kernels for 16% -> 18%
where the time goes in v5:
time: 121 us; the launch traced here: 120 us
  waiting for transfers between devices  50.6 us (42%)
  Pallas kernels  34.6 us (29%)
  starting transfers between devices  28.1 us (23%)
  local copies, waits for them, and re-layouts  6.27 us (5%)
    ppermute x8, waiting for transfers between devices, swap(): return lax.ppermute(block, 'rows', [(i, i ^ number) for i in range(peers)])  33 us
    all_to_all x3, waiting for transfers between devices, exchange(): lax.all_to_all(blocks, 'rows', split_axis=0, concat_axis=0, tiled=True, a...  17.6 us
    all_to_all x3, starting transfers between devices, exchange(): lax.all_to_all(blocks, 'rows', split_axis=0, concat_axis=0, tiled=True, a...  14.6 us
    ppermute x8, starting transfers between devices, swap(): return lax.ppermute(block, 'rows', [(i, i ^ number) for i in range(peers)])  13.5 us
    pallas_call x2, Pallas kernels, packed(): pl.pallas_call(functools.partial(pack_kernel, cap, peers, numbers), out_s...  10.3 us
    pallas_call x3, Pallas kernels, call_bests(): pl.pallas_call(kernel, out_shape=jax.ShapeDtypeStruct((out_blocks, 1, cap...  9.73 us
    pallas_call x1, Pallas kernels, places_and_packed(): pl.pallas_call(functools.partial(place_pack_kernel, cap, peers, numbers),...  6.46 us
    unnamed x26, local copies, waits for them, and re-layouts  5.68 us
  transfers between devices with their start and end apart: 11, of which 8 were waited for; matrix products, arithmetic and copies ran while one was open for 0% of the time, Pallas kernels for 18%

profile of v5, /device:TPU:0, one launch (start us, length us, event | category | flops | bytes accessed | tf_op | source)
XLA Modules:
  0.0 120.5 jit_solution(17948583112981866057)
XLA Ops:
  0.0 1.9 %counts.1 = f32[16,1,512]{2,1,0:T(1,128)} custom-call(s32[1,2048]{1,0:T(1,128)} %bitcast.47), custom_call_target="tpu_custom_call" | custom-call | tf_op jit(solution)/shard_map/counts/pallas_call | solution.py:59
  1.9 7.4 %all-to-all-start.3 = ((f32[16,1,512]{2,1,0:T(1,128)}), f32[16,1,512]{2,1,0:T(1,128)S(1)}, u32[]{:S(2)}, u32[]{:S(2)}) async-start(f32[16,1,512]{2,1,0:T(1,128)} %counts.1), calls=%async_computation.3 | async-start | bytes 65536 | tf_op jit(solution)/shard_map/all_to_all | solution.py:466
  9.3 2.4 %unit.1.unit_ref = bf16[2048,768]{1,0:T(8,128)(2,1)S(1)} custom-call(bf16[2048,768]{1,0:T(8,128)(2,1)} %rows_ref.1), custom_call_target="tpu_custom_call" | custom-call | flops 6291456 | bytes 6291456 | tf_op jit(solution)/shard_map/unit/pallas_call | solution.py:103
  11.7 1.4 %ranks.1.rank_ref = s32[1,2048]{1,0:T(1,128)S(1)} custom-call(s32[1,2048]{1,0:T(1,128)S(1)} %bitcast.48), custom_call_target="tpu_custom_call" | custom-call | flops 8388608 | bytes 4194304 | tf_op jit(solution)/shard_map/ranks/pallas_call | solution.py:82
  13.1 2.8 %all-to-all-done.3.count_ref = f32[16,1,512]{2,1,0:T(1,128)S(1)} async-done(((f32[16,1,512]{2,1,0:T(1,128)}), f32[16,1,512]{2,1,0:T(1,128)S(1)}, u32[]{:S(2)}, u32[]{:S(2)}) %all-to-all-start.3) | async-done | bytes 32800 | tf_op jit(solution)/shard_map/all_to_all | solution.py:466
  15.9 6.5 %places.1 = (s32[1,2048]{1,0:T(1,128)S(1)}, f32[24,512]{1,0:T(8,128)S(1)}, bf16[144,768]{1,0:T(8,128)(2,1)S(1)}, bf16[144,768]{1,0:T(8,128)(2,1)S(1)}, bf16[144,768]{1,0:T(8,128)(2,1)S(1)}) custom-call(s32[1]{0:T(128)} %bitcast.11.me_ref, f32[16,1,512]{2,1,0:T(1,128)S(1)} %all-to-all-done.3.count_ref, s32[1,2048]{1,0:T(1,128)S(1)} %bitcast.49, ...), custom_call_target="tpu_custom_call" | custom-call | tf_op jit(solution)/shard_map/places/pallas_call | solution.py:232
  22.8 5.2 %pack.3 = (bf16[144,768]{1,0:T(8,128)(2,1)}, bf16[144,768]{1,0:T(8,128)(2,1)}, bf16[144,768]{1,0:T(8,128)(2,1)S(1)}, bf16[144,768]{1,0:T(8,128)(2,1)S(1)}, bf16[144,768]{1,0:T(8,128)(2,1)S(1)}) custom-call(s32[1]{0:T(128)} %bitcast.11.me_ref, s32[1,2048]{1,0:T(1,128)S(1)} %get-tuple-element.71.dest_ref, bf16[2048,768]{1,0:T(8,128)(2,1)} %copy-done.8), custom_call_target="tpu_custom_call" | custom-call | flops 2264924160 | bytes 4251648 | tf_op jit(solution)/shard_map/pack/pallas_call | solution.py:252
  28.0 1.6 %collective-permute-start.1 = (bf16[144,768]{1,0:T(8,128)(2,1)S(1)}, bf16[144,768]{1,0:T(8,128)(2,1)S(1)}, u32[]{:S(2)}, u32[]{:S(2)}) collective-permute-start(bf16[144,768]{1,0:T(8,128)(2,1)S(1)} %get-tuple-element.73), channel_id=1, source_target_pairs={{0,9},{1,8},{2,11},{3,10},{4,13},{5,12},{6,15},{7,14},{8,1},{9,0},... | collective-permute-start | bytes 663560 | tf_op jit(solution)/shard_map/ppermute | solution.py:470
  29.5 1.4 %collective-permute-start.2 = (bf16[144,768]{1,0:T(8,128)(2,1)S(1)}, bf16[144,768]{1,0:T(8,128)(2,1)S(1)}, u32[]{:S(2)}, u32[]{:S(2)}) collective-permute-start(bf16[144,768]{1,0:T(8,128)(2,1)S(1)} %get-tuple-element.74), channel_id=1, source_target_pairs={{0,10},{1,11},{2,8},{3,9},{4,14},{5,15},{6,12},{7,13},{8,2},{9,3},... | collective-permute-start | bytes 663560 | tf_op jit(solution)/shard_map/ppermute | solution.py:470
  31.0 2.8 %collective-permute-start.3 = (bf16[144,768]{1,0:T(8,128)(2,1)}, bf16[144,768]{1,0:T(8,128)(2,1)S(1)}, u32[]{:S(2)}, u32[]{:S(2)}) collective-permute-start(bf16[144,768]{1,0:T(8,128)(2,1)} %get-tuple-element.72), channel_id=1, source_target_pairs={{0,11},{1,10},{2,9},{3,8},{4,15},{5,14},{6,13},{7,12},{8,3},{9,2},... | collective-permute-start | bytes 663560 | tf_op jit(solution)/shard_map/ppermute | solution.py:470
  33.8 1.0 collective-permute-start.4
  34.8 5.1 %pack.2 = bf16[1152,768]{1,0:T(8,128)(2,1)} custom-call(s32[1]{0:T(128)} %bitcast.11.me_ref, s32[1,2048]{1,0:T(1,128)S(1)} %get-tuple-element.71.dest_ref, bf16[2048,768]{1,0:T(8,128)(2,1)S(1)} %copy-done.9), custom_call_target="tpu_custom_call" | custom-call | flops 3623878656 | bytes 4915200 | tf_op jit(solution)/shard_map/pack/pallas_call | solution.py:252
  39.9 14.5 %collective-permute-done.refs_0_ = bf16[144,768]{1,0:T(8,128)(2,1)S(1)} collective-permute-done((bf16[144,768]{1,0:T(8,128)(2,1)S(1)}, bf16[144,768]{1,0:T(8,128)(2,1)S(1)}, u32[]{:S(2)}, u32[]{:S(2)}) %collective-permute-start) | collective-permute-done | bytes 221216 | tf_op jit(solution)/shard_map/ppermute | solution.py:470
  54.4 4.1 %collective-permute-done.1.refs_1_ = bf16[144,768]{1,0:T(8,128)(2,1)S(1)} collective-permute-done((bf16[144,768]{1,0:T(8,128)(2,1)S(1)}, bf16[144,768]{1,0:T(8,128)(2,1)S(1)}, u32[]{:S(2)}, u32[]{:S(2)}) %collective-permute-start.1) | collective-permute-done | bytes 221216 | tf_op jit(solution)/shard_map/ppermute | solution.py:470
  58.5 5.4 %collective-permute-done.2.refs_2_ = bf16[144,768]{1,0:T(8,128)(2,1)S(1)} collective-permute-done((bf16[144,768]{1,0:T(8,128)(2,1)S(1)}, bf16[144,768]{1,0:T(8,128)(2,1)S(1)}, u32[]{:S(2)}, u32[]{:S(2)}) %collective-permute-start.2) | collective-permute-done | bytes 221216 | tf_op jit(solution)/shard_map/ppermute | solution.py:470
  63.9 3.8 %all-to-all-start.4 = ((bf16[8,144,768]{2,1,0:T(8,128)(2,1)}), bf16[8,144,768]{2,1,0:T(8,128)(2,1)S(1)}, u32[]{:S(2)}, u32[]{:S(2)}) async-start(bf16[8,144,768]{2,1,0:T(8,128)(2,1)} %bitcast.14), calls=%async_computation.4 | async-start | bytes 3538944 | tf_op jit(solution)/shard_map/all_to_all | solution.py:466
  67.7 0.8 copy-done.1
  68.5 2.0 %keys.1 = (f32[1,2304]{1,0:T(1,128)S(1)}, f32[2304,128]{1,0:T(8,128)S(1)}, f32[8,128]{1,0:T(8,128)S(1)}) custom-call(s32[1]{0:T(128)} %bitcast.11.me_ref, f32[24,512]{1,0:T(8,128)S(1)} %copy-done.1), custom_call_target="tpu_custom_call" | custom-call | flops 68719476736 | bytes 4194304 | tf_op jit(solution)/shard_map/keys/pallas_call | solution.py:292
  70.5 1.7 %collective-permute-start.5 = (bf16[144,768]{1,0:T(8,128)(2,1)S(1)}, bf16[144,768]{1,0:T(8,128)(2,1)}, u32[]{:S(2)}, u32[]{:S(2)}) collective-permute-start(bf16[144,768]{1,0:T(8,128)(2,1)S(1)} %get-tuple-element.80), channel_id=1, source_target_pairs={{0,13},{1,12},{2,15},{3,14},{4,9},{5,8},{6,11},{7,10},{8,5},{9,4},... | collective-permute-start | bytes 663560 | tf_op jit(solution)/shard_map/ppermute | solution.py:470
  72.2 3.2 %collective-permute-start.6 = (bf16[144,768]{1,0:T(8,128)(2,1)S(1)}, bf16[144,768]{1,0:T(8,128)(2,1)}, u32[]{:S(2)}, u32[]{:S(2)}) collective-permute-start(bf16[144,768]{1,0:T(8,128)(2,1)S(1)} %get-tuple-element.81), channel_id=1, source_target_pairs={{0,14},{1,15},{2,12},{3,13},{4,10},{5,11},{6,8},{7,9},{8,6},{9,7},... | collective-permute-start | bytes 663560 | tf_op jit(solution)/shard_map/ppermute | solution.py:470
  75.3 1.4 %collective-permute-start.7 = (bf16[144,768]{1,0:T(8,128)(2,1)S(1)}, bf16[144,768]{1,0:T(8,128)(2,1)}, u32[]{:S(2)}, u32[]{:S(2)}) collective-permute-start(bf16[144,768]{1,0:T(8,128)(2,1)S(1)} %get-tuple-element.82), channel_id=1, source_target_pairs={{0,15},{1,14},{2,13},{3,12},{4,11},{5,10},{6,9},{7,8},{8,7},{9,6},... | collective-permute-start | bytes 663560 | tf_op jit(solution)/shard_map/ppermute | solution.py:470
  76.8 1.5 %similar.3.before_ref = f32[5,1,144]{2,1,0:T(1,128)S(1)} custom-call(f32[1,2304]{1,0:T(1,128)S(1)} %get-tuple-element.68.row_ref, f32[2304,128]{1,0:T(8,128)S(1)} %get-tuple-element.69.col_ref, bf16[144,768]{1,0:T(8,128)(2,1)S(1)} %collective-permute-done.refs_0_, bf16[144,768]{1,0:T(8,128)(2,1)S(1)} %collective-permute-done.1.refs_1_, ...), custom_call_target="tpu_custom_call" | custom-call | flops 796262400 | bytes 8388608 | tf_op jit(solution)/shard_map/similar/pallas_call | solution.py:384
  78.3 1.0 copy-done.2
  79.9 9.7 %all-to-all-done.4 = bf16[8,144,768]{2,1,0:T(8,128)(2,1)S(1)} async-done(((bf16[8,144,768]{2,1,0:T(8,128)(2,1)}), bf16[8,144,768]{2,1,0:T(8,128)(2,1)S(1)}, u32[]{:S(2)}, u32[]{:S(2)}) %all-to-all-start.4) | async-done | bytes 1769504 | tf_op jit(solution)/shard_map/all_to_all | solution.py:466
  89.6 1.3 %copy-done.3 = f32[2304,128]{1,0:T(8,128)S(1)} copy-done((f32[2304,128]{1,0:T(8,128)S(1)}, f32[2304,128]{1,0:T(8,128)}, u32[]{:S(2)}) %copy-start.3) | copy-done | bytes 1179672
  90.9 0.7 copy-done.5
  92.3 4.3 %similar.4.before_ref = f32[13,1,144]{2,1,0:T(1,128)S(1)} custom-call(s32[1]{0:T(128)} %bitcast.11.me_ref, f32[1,2304]{1,0:T(1,128)S(1)} %copy-done.5, f32[2304,128]{1,0:T(8,128)S(1)} %copy-done.3, f32[5,1,144]{2,1,0:T(1,128)S(1)} %copy-done.7, bf16[144,768]{1,0:T(8,128)(2,1)S(1)} %collective-permute-done.refs_0_, ...), custom_call_target="tpu_custom_call" | custom-call | flops 3312451584 | bytes 8388608 | tf_op jit(solution)/shard_map/similar/pallas_call | solution.py:384
  96.5 5.2 %collective-permute-done.6.refs_7_ = bf16[144,768]{1,0:T(8,128)(2,1)} collective-permute-done((bf16[144,768]{1,0:T(8,128)(2,1)S(1)}, bf16[144,768]{1,0:T(8,128)(2,1)}, u32[]{:S(2)}, u32[]{:S(2)}) %collective-permute-start.6) | collective-permute-done | bytes 221216 | tf_op jit(solution)/shard_map/ppermute | solution.py:470
  101.7 3.8 %collective-permute-done.7.refs_8_ = bf16[144,768]{1,0:T(8,128)(2,1)} collective-permute-done((bf16[144,768]{1,0:T(8,128)(2,1)S(1)}, bf16[144,768]{1,0:T(8,128)(2,1)}, u32[]{:S(2)}, u32[]{:S(2)}) %collective-permute-start.7) | collective-permute-done | bytes 221216 | tf_op jit(solution)/shard_map/ppermute | solution.py:470
  105.5 3.9 %similar.5 = f32[16,1,144]{2,1,0:T(1,128)} custom-call(s32[1]{0:T(128)} %bitcast.11.me_ref, f32[1,2304]{1,0:T(1,128)S(1)} %copy-done.5, f32[2304,128]{1,0:T(8,128)S(1)} %copy-done.3, f32[13,1,144]{2,1,0:T(1,128)S(1)} %similar.4.before_ref, bf16[144,768]{1,0:T(8,128)(2,1)S(1)} %collective-permute-done.refs_0_, ...), custom_call_target="tpu_custom_call" | custom-call | flops 1528823808 | bytes 8388608 | tf_op jit(solution)/shard_map/similar/pallas_call | solution.py:384
  109.4 3.5 %all-to-all-start.5 = ((f32[16,1,144]{2,1,0:T(1,128)}), f32[16,1,144]{2,1,0:T(1,128)S(1)}, u32[]{:S(2)}, u32[]{:S(2)}) async-start(f32[16,1,144]{2,1,0:T(1,128)} %similar.5), calls=%async_computation.5 | async-start | bytes 32768 | tf_op jit(solution)/shard_map/all_to_all | solution.py:466
  114.2 5.2 %all-to-all-done.5.back_ref = f32[16,1,144]{2,1,0:T(1,128)S(1)} async-done(((f32[16,1,144]{2,1,0:T(1,128)}), f32[16,1,144]{2,1,0:T(1,128)S(1)}, u32[]{:S(2)}, u32[]{:S(2)}) %all-to-all-start.5) | async-done | bytes 9248 | tf_op jit(solution)/shard_map/all_to_all | solution.py:466
  (29 shorter events, 3.4 us)
Async XLA Ops:
  0.0 11.7 %copy-start.10 = (s32[2048,1]{0,1:T(1,128)S(1)}, s32[2048,1]{0,1:T(1,128)}, u32[]{:S(2)}) copy-start(s32[2048,1]{0,1:T(1,128)} %param.7) | copy-start | bytes 24580
  1.9 14.0 %all-to-all-start.3 = ((f32[16,1,512]{2,1,0:T(1,128)}), f32[16,1,512]{2,1,0:T(1,128)S(1)}, u32[]{:S(2)}, u32[]{:S(2)}) async-start(f32[16,1,512]{2,1,0:T(1,128)} %counts.1), calls=%async_computation.3 | async-start | bytes 65536 | tf_op jit(solution)/shard_map/all_to_all | solution.py:466
  11.7 10.7 %copy-start.8 = (bf16[2048,768]{1,0:T(8,128)(2,1)}, bf16[2048,768]{1,0:T(8,128)(2,1)S(1)}, u32[]{:S(2)}) copy-start(bf16[2048,768]{1,0:T(8,128)(2,1)S(1)} %unit.1.unit_ref) | copy-start | bytes 9437188
  13.1 14.9 %copy-start.12 = (s32[1,2048]{1,0:T(1,128)}, s32[1,2048]{1,0:T(1,128)S(1)}, u32[]{:S(2)}) copy-start(s32[1,2048]{1,0:T(1,128)S(1)} %ranks.1.rank_ref) | copy-start | bytes 24580
  22.4 7.2 %copy-start = (f32[24,512]{1,0:T(8,128)}, f32[24,512]{1,0:T(8,128)S(1)}, u32[]{:S(2)}) copy-start(f32[24,512]{1,0:T(8,128)S(1)} %get-tuple-element.65.table_ref) | copy-start | bytes 147460
  22.4 32.0 %collective-permute-start = (bf16[144,768]{1,0:T(8,128)(2,1)S(1)}, bf16[144,768]{1,0:T(8,128)(2,1)S(1)}, u32[]{:S(2)}, u32[]{:S(2)}) collective-permute-start(bf16[144,768]{1,0:T(8,128)(2,1)S(1)} %get-tuple-element.70), channel_id=1, source_target_pairs={{0,8},{1,9},{2,10},{3,11},{4,12},{5,13},{6,14},{7,15},{8,0},{9,1},... | collective-permute-start | bytes 663560 | tf_op jit(solution)/shard_map/ppermute | solution.py:470
  22.8 11.9 %copy-start.9 = (bf16[2048,768]{1,0:T(8,128)(2,1)S(1)}, bf16[2048,768]{1,0:T(8,128)(2,1)}, u32[]{:S(2)}) copy-start(bf16[2048,768]{1,0:T(8,128)(2,1)} %copy-done.8) | copy-start | bytes 9437188
  28.0 30.5 %collective-permute-start.1 = (bf16[144,768]{1,0:T(8,128)(2,1)S(1)}, bf16[144,768]{1,0:T(8,128)(2,1)S(1)}, u32[]{:S(2)}, u32[]{:S(2)}) collective-permute-start(bf16[144,768]{1,0:T(8,128)(2,1)S(1)} %get-tuple-element.73), channel_id=1, source_target_pairs={{0,9},{1,8},{2,11},{3,10},{4,13},{5,12},{6,15},{7,14},{8,1},{9,0},... | collective-permute-start | bytes 663560 | tf_op jit(solution)/shard_map/ppermute | solution.py:470
  29.5 34.3 %collective-permute-start.2 = (bf16[144,768]{1,0:T(8,128)(2,1)S(1)}, bf16[144,768]{1,0:T(8,128)(2,1)S(1)}, u32[]{:S(2)}, u32[]{:S(2)}) collective-permute-start(bf16[144,768]{1,0:T(8,128)(2,1)S(1)} %get-tuple-element.74), channel_id=1, source_target_pairs={{0,10},{1,11},{2,8},{3,9},{4,14},{5,15},{6,12},{7,13},{8,2},{9,3},... | collective-permute-start | bytes 663560 | tf_op jit(solution)/shard_map/ppermute | solution.py:470
  31.0 45.8 %collective-permute-start.3 = (bf16[144,768]{1,0:T(8,128)(2,1)}, bf16[144,768]{1,0:T(8,128)(2,1)S(1)}, u32[]{:S(2)}, u32[]{:S(2)}) collective-permute-start(bf16[144,768]{1,0:T(8,128)(2,1)} %get-tuple-element.72), channel_id=1, source_target_pairs={{0,11},{1,10},{2,9},{3,8},{4,15},{5,14},{6,13},{7,12},{8,3},{9,2},... | collective-permute-start | bytes 663560 | tf_op jit(solution)/shard_map/ppermute | solution.py:470
  33.8 43.0 %collective-permute-start.4 = (bf16[144,768]{1,0:T(8,128)(2,1)}, bf16[144,768]{1,0:T(8,128)(2,1)S(1)}, u32[]{:S(2)}, u32[]{:S(2)}) collective-permute-start(bf16[144,768]{1,0:T(8,128)(2,1)} %get-tuple-element.78), channel_id=1, source_target_pairs={{0,12},{1,13},{2,14},{3,15},{4,8},{5,9},{6,10},{7,11},{8,4},{9,5},... | collective-permute-start | bytes 663560 | tf_op jit(solution)/shard_map/ppermute | solution.py:470
  63.9 25.7 %all-to-all-start.4 = ((bf16[8,144,768]{2,1,0:T(8,128)(2,1)}), bf16[8,144,768]{2,1,0:T(8,128)(2,1)S(1)}, u32[]{:S(2)}, u32[]{:S(2)}) async-start(bf16[8,144,768]{2,1,0:T(8,128)(2,1)} %bitcast.14), calls=%async_computation.4 | async-start | bytes 3538944 | tf_op jit(solution)/shard_map/all_to_all | solution.py:466
  67.7 0.8 copy-start.1
  70.5 6.3 %copy-start.4 = (f32[1,2304]{1,0:T(1,128)}, f32[1,2304]{1,0:T(1,128)S(1)}, u32[]{:S(2)}) copy-start(f32[1,2304]{1,0:T(1,128)S(1)} %get-tuple-element.68.row_ref) | copy-start | bytes 27652
  70.5 26.0 %collective-permute-start.5 = (bf16[144,768]{1,0:T(8,128)(2,1)S(1)}, bf16[144,768]{1,0:T(8,128)(2,1)}, u32[]{:S(2)}, u32[]{:S(2)}) collective-permute-start(bf16[144,768]{1,0:T(8,128)(2,1)S(1)} %get-tuple-element.80), channel_id=1, source_target_pairs={{0,13},{1,12},{2,15},{3,14},{4,9},{5,8},{6,11},{7,10},{8,5},{9,4},... | collective-permute-start | bytes 663560 | tf_op jit(solution)/shard_map/ppermute | solution.py:470
  72.2 29.5 %collective-permute-start.6 = (bf16[144,768]{1,0:T(8,128)(2,1)S(1)}, bf16[144,768]{1,0:T(8,128)(2,1)}, u32[]{:S(2)}, u32[]{:S(2)}) collective-permute-start(bf16[144,768]{1,0:T(8,128)(2,1)S(1)} %get-tuple-element.81), channel_id=1, source_target_pairs={{0,14},{1,15},{2,12},{3,13},{4,10},{5,11},{6,8},{7,9},{8,6},{9,7},... | collective-permute-start | bytes 663560 | tf_op jit(solution)/shard_map/ppermute | solution.py:470
  75.3 30.2 %collective-permute-start.7 = (bf16[144,768]{1,0:T(8,128)(2,1)S(1)}, bf16[144,768]{1,0:T(8,128)(2,1)}, u32[]{:S(2)}, u32[]{:S(2)}) collective-permute-start(bf16[144,768]{1,0:T(8,128)(2,1)S(1)} %get-tuple-element.82), channel_id=1, source_target_pairs={{0,15},{1,14},{2,13},{3,12},{4,11},{5,10},{6,9},{7,8},{8,7},{9,6},... | collective-permute-start | bytes 663560 | tf_op jit(solution)/shard_map/ppermute | solution.py:470
  78.3 1.0 copy-start.2
  79.3 0.6 copy-start.6
  89.6 1.3 %copy-start.3 = (f32[2304,128]{1,0:T(8,128)S(1)}, f32[2304,128]{1,0:T(8,128)}, u32[]{:S(2)}) copy-start(f32[2304,128]{1,0:T(8,128)} %copy-done.2) | copy-start | bytes 3538948
  90.9 0.7 copy-start.5
  91.6 0.7 copy-start.7
  109.4 10.0 %all-to-all-start.5 = ((f32[16,1,144]{2,1,0:T(1,128)}), f32[16,1,144]{2,1,0:T(1,128)S(1)}, u32[]{:S(2)}, u32[]{:S(2)}) async-start(f32[16,1,144]{2,1,0:T(1,128)} %similar.5), calls=%async_computation.5 | async-start | bytes 32768 | tf_op jit(solution)/shard_map/all_to_all | solution.py:466
  119.9 0.6 copy-start.14

commit v6 on v5

--- a/solution.py
+++ b/solution.py
@@ -372,9 +372,10 @@
             if tail.shape[1] < LANES:
                 tail = jnp.concatenate([tail, jnp.full((count * cap, LANES - tail.shape[1]), -1.0, F32)], axis=1)
             side = functools.reduce(jnp.maximum, parts[:-1] + [tail])
+            across = jnp.max(jnp.transpose(side), axis=0, keepdims=True)
             for i in range(min(count, known - upper)):
-                across = jnp.max(jnp.transpose(side[i * cap : (i + 1) * cap]), axis=0, keepdims=True)
-                best_ref[place(upper + i)] = jnp.maximum(before_ref[upper + i], across)
+                found = jnp.maximum(before_ref[upper + i], across[:, i * cap : (i + 1) * cap])
+                best_ref[place(upper + i)] = found
     for i in range(here - known):
         best_ref[place(known + i)] = best[:, i * cap : (i + 1) * cap]
 

time: 121 us -> 121 us (level)
  no operation moved by 1% of the time
where the time goes in v6:
time: 121 us; the launch traced here: 120 us
  waiting for transfers between devices  50.6 us (42%)
  Pallas kernels  34.6 us (29%)
  starting transfers between devices  28.1 us (23%)
  local copies, waits for them, and re-layouts  6.27 us (5%)
    ppermute x8, waiting for transfers between devices, swap(): return lax.ppermute(block, 'rows', [(i, i ^ number) for i in range(peers)])  33 us
    all_to_all x3, waiting for transfers between devices, exchange(): lax.all_to_all(blocks, 'rows', split_axis=0, concat_axis=0, tiled=True, a...  17.6 us
    all_to_all x3, starting transfers between devices, exchange(): lax.all_to_all(blocks, 'rows', split_axis=0, concat_axis=0, tiled=True, a...  14.6 us
    ppermute x8, starting transfers between devices, swap(): return lax.ppermute(block, 'rows', [(i, i ^ number) for i in range(peers)])  13.5 us
    pallas_call x2, Pallas kernels, packed(): pl.pallas_call(functools.partial(pack_kernel, cap, peers, numbers), out_s...  10.3 us
    pallas_call x3, Pallas kernels, call_bests(): pl.pallas_call(kernel, out_shape=jax.ShapeDtypeStruct((out_blocks, 1, cap...  9.68 us
    pallas_call x1, Pallas kernels, places_and_packed(): pl.pallas_call(functools.partial(place_pack_kernel, cap, peers, numbers),...  6.46 us
    unnamed x26, local copies, waits for them, and re-layouts  5.68 us
  transfers between devices with their start and end apart: 11, of which 8 were waited for; matrix products, arithmetic and copies ran while one was open for 0% of the time, Pallas kernels for 18%

profile of v6, /device:TPU:0, one launch (start us, length us, event | category | flops | bytes accessed | tf_op | source)
XLA Modules:
  0.0 120.4 jit_solution(16797094332142763428)
XLA Ops:
  0.0 1.9 %counts.1 = f32[16,1,512]{2,1,0:T(1,128)} custom-call(s32[1,2048]{1,0:T(1,128)} %bitcast.47), custom_call_target="tpu_custom_call" | custom-call | tf_op jit(solution)/shard_map/counts/pallas_call | solution.py:59
  1.9 7.4 %all-to-all-start.3 = ((f32[16,1,512]{2,1,0:T(1,128)}), f32[16,1,512]{2,1,0:T(1,128)S(1)}, u32[]{:S(2)}, u32[]{:S(2)}) async-start(f32[16,1,512]{2,1,0:T(1,128)} %counts.1), calls=%async_computation.3 | async-start | bytes 65536 | tf_op jit(solution)/shard_map/all_to_all | solution.py:467
  9.3 2.4 %unit.1.unit_ref = bf16[2048,768]{1,0:T(8,128)(2,1)S(1)} custom-call(bf16[2048,768]{1,0:T(8,128)(2,1)} %rows_ref.1), custom_call_target="tpu_custom_call" | custom-call | flops 6291456 | bytes 6291456 | tf_op jit(solution)/shard_map/unit/pallas_call | solution.py:103
  11.7 1.4 %ranks.1.rank_ref = s32[1,2048]{1,0:T(1,128)S(1)} custom-call(s32[1,2048]{1,0:T(1,128)S(1)} %bitcast.48), custom_call_target="tpu_custom_call" | custom-call | flops 8388608 | bytes 4194304 | tf_op jit(solution)/shard_map/ranks/pallas_call | solution.py:82
  13.1 2.8 %all-to-all-done.3.count_ref = f32[16,1,512]{2,1,0:T(1,128)S(1)} async-done(((f32[16,1,512]{2,1,0:T(1,128)}), f32[16,1,512]{2,1,0:T(1,128)S(1)}, u32[]{:S(2)}, u32[]{:S(2)}) %all-to-all-start.3) | async-done | bytes 32800 | tf_op jit(solution)/shard_map/all_to_all | solution.py:467
  15.9 6.5 %places.1 = (s32[1,2048]{1,0:T(1,128)S(1)}, f32[24,512]{1,0:T(8,128)S(1)}, bf16[144,768]{1,0:T(8,128)(2,1)S(1)}, bf16[144,768]{1,0:T(8,128)(2,1)S(1)}, bf16[144,768]{1,0:T(8,128)(2,1)S(1)}) custom-call(s32[1]{0:T(128)} %bitcast.11.me_ref, f32[16,1,512]{2,1,0:T(1,128)S(1)} %all-to-all-done.3.count_ref, s32[1,2048]{1,0:T(1,128)S(1)} %bitcast.49, ...), custom_call_target="tpu_custom_call" | custom-call | tf_op jit(solution)/shard_map/places/pallas_call | solution.py:232
  22.8 5.2 %pack.3 = (bf16[144,768]{1,0:T(8,128)(2,1)}, bf16[144,768]{1,0:T(8,128)(2,1)}, bf16[144,768]{1,0:T(8,128)(2,1)S(1)}, bf16[144,768]{1,0:T(8,128)(2,1)S(1)}, bf16[144,768]{1,0:T(8,128)(2,1)S(1)}) custom-call(s32[1]{0:T(128)} %bitcast.11.me_ref, s32[1,2048]{1,0:T(1,128)S(1)} %get-tuple-element.71.dest_ref, bf16[2048,768]{1,0:T(8,128)(2,1)} %copy-done.8), custom_call_target="tpu_custom_call" | custom-call | flops 2264924160 | bytes 4251648 | tf_op jit(solution)/shard_map/pack/pallas_call | solution.py:252
  28.0 1.6 %collective-permute-start.1 = (bf16[144,768]{1,0:T(8,128)(2,1)S(1)}, bf16[144,768]{1,0:T(8,128)(2,1)S(1)}, u32[]{:S(2)}, u32[]{:S(2)}) collective-permute-start(bf16[144,768]{1,0:T(8,128)(2,1)S(1)} %get-tuple-element.73), channel_id=1, source_target_pairs={{0,9},{1,8},{2,11},{3,10},{4,13},{5,12},{6,15},{7,14},{8,1},{9,0},... | collective-permute-start | bytes 663560 | tf_op jit(solution)/shard_map/ppermute | solution.py:471
  29.5 1.4 %collective-permute-start.2 = (bf16[144,768]{1,0:T(8,128)(2,1)S(1)}, bf16[144,768]{1,0:T(8,128)(2,1)S(1)}, u32[]{:S(2)}, u32[]{:S(2)}) collective-permute-start(bf16[144,768]{1,0:T(8,128)(2,1)S(1)} %get-tuple-element.74), channel_id=1, source_target_pairs={{0,10},{1,11},{2,8},{3,9},{4,14},{5,15},{6,12},{7,13},{8,2},{9,3},... | collective-permute-start | bytes 663560 | tf_op jit(solution)/shard_map/ppermute | solution.py:471
  31.0 2.8 %collective-permute-start.3 = (bf16[144,768]{1,0:T(8,128)(2,1)}, bf16[144,768]{1,0:T(8,128)(2,1)S(1)}, u32[]{:S(2)}, u32[]{:S(2)}) collective-permute-start(bf16[144,768]{1,0:T(8,128)(2,1)} %get-tuple-element.72), channel_id=1, source_target_pairs={{0,11},{1,10},{2,9},{3,8},{4,15},{5,14},{6,13},{7,12},{8,3},{9,2},... | collective-permute-start | bytes 663560 | tf_op jit(solution)/shard_map/ppermute | solution.py:471
  33.8 1.0 collective-permute-start.4
  34.8 5.1 %pack.2 = bf16[1152,768]{1,0:T(8,128)(2,1)} custom-call(s32[1]{0:T(128)} %bitcast.11.me_ref, s32[1,2048]{1,0:T(1,128)S(1)} %get-tuple-element.71.dest_ref, bf16[2048,768]{1,0:T(8,128)(2,1)S(1)} %copy-done.9), custom_call_target="tpu_custom_call" | custom-call | flops 3623878656 | bytes 4915200 | tf_op jit(solution)/shard_map/pack/pallas_call | solution.py:252
  39.9 14.5 %collective-permute-done.refs_0_ = bf16[144,768]{1,0:T(8,128)(2,1)S(1)} collective-permute-done((bf16[144,768]{1,0:T(8,128)(2,1)S(1)}, bf16[144,768]{1,0:T(8,128)(2,1)S(1)}, u32[]{:S(2)}, u32[]{:S(2)}) %collective-permute-start) | collective-permute-done | bytes 221216 | tf_op jit(solution)/shard_map/ppermute | solution.py:471
  54.4 4.1 %collective-permute-done.1.refs_1_ = bf16[144,768]{1,0:T(8,128)(2,1)S(1)} collective-permute-done((bf16[144,768]{1,0:T(8,128)(2,1)S(1)}, bf16[144,768]{1,0:T(8,128)(2,1)S(1)}, u32[]{:S(2)}, u32[]{:S(2)}) %collective-permute-start.1) | collective-permute-done | bytes 221216 | tf_op jit(solution)/shard_map/ppermute | solution.py:471
  58.5 5.4 %collective-permute-done.2.refs_2_ = bf16[144,768]{1,0:T(8,128)(2,1)S(1)} collective-permute-done((bf16[144,768]{1,0:T(8,128)(2,1)S(1)}, bf16[144,768]{1,0:T(8,128)(2,1)S(1)}, u32[]{:S(2)}, u32[]{:S(2)}) %collective-permute-start.2) | collective-permute-done | bytes 221216 | tf_op jit(solution)/shard_map/ppermute | solution.py:471
  63.9 3.8 %all-to-all-start.4 = ((bf16[8,144,768]{2,1,0:T(8,128)(2,1)}), bf16[8,144,768]{2,1,0:T(8,128)(2,1)S(1)}, u32[]{:S(2)}, u32[]{:S(2)}) async-start(bf16[8,144,768]{2,1,0:T(8,128)(2,1)} %bitcast.14), calls=%async_computation.4 | async-start | bytes 3538944 | tf_op jit(solution)/shard_map/all_to_all | solution.py:467
  67.7 0.8 copy-done.1
  68.5 2.0 %keys.1 = (f32[1,2304]{1,0:T(1,128)S(1)}, f32[2304,128]{1,0:T(8,128)S(1)}, f32[8,128]{1,0:T(8,128)S(1)}) custom-call(s32[1]{0:T(128)} %bitcast.11.me_ref, f32[24,512]{1,0:T(8,128)S(1)} %copy-done.1), custom_call_target="tpu_custom_call" | custom-call | flops 68719476736 | bytes 4194304 | tf_op jit(solution)/shard_map/keys/pallas_call | solution.py:292
  70.5 1.7 %collective-permute-start.5 = (bf16[144,768]{1,0:T(8,128)(2,1)S(1)}, bf16[144,768]{1,0:T(8,128)(2,1)}, u32[]{:S(2)}, u32[]{:S(2)}) collective-permute-start(bf16[144,768]{1,0:T(8,128)(2,1)S(1)} %get-tuple-element.80), channel_id=1, source_target_pairs={{0,13},{1,12},{2,15},{3,14},{4,9},{5,8},{6,11},{7,10},{8,5},{9,4},... | collective-permute-start | bytes 663560 | tf_op jit(solution)/shard_map/ppermute | solution.py:471
  72.2 3.2 %collective-permute-start.6 = (bf16[144,768]{1,0:T(8,128)(2,1)S(1)}, bf16[144,768]{1,0:T(8,128)(2,1)}, u32[]{:S(2)}, u32[]{:S(2)}) collective-permute-start(bf16[144,768]{1,0:T(8,128)(2,1)S(1)} %get-tuple-element.81), channel_id=1, source_target_pairs={{0,14},{1,15},{2,12},{3,13},{4,10},{5,11},{6,8},{7,9},{8,6},{9,7},... | collective-permute-start | bytes 663560 | tf_op jit(solution)/shard_map/ppermute | solution.py:471
  75.3 1.4 %collective-permute-start.7 = (bf16[144,768]{1,0:T(8,128)(2,1)S(1)}, bf16[144,768]{1,0:T(8,128)(2,1)}, u32[]{:S(2)}, u32[]{:S(2)}) collective-permute-start(bf16[144,768]{1,0:T(8,128)(2,1)S(1)} %get-tuple-element.82), channel_id=1, source_target_pairs={{0,15},{1,14},{2,13},{3,12},{4,11},{5,10},{6,9},{7,8},{8,7},{9,6},... | collective-permute-start | bytes 663560 | tf_op jit(solution)/shard_map/ppermute | solution.py:471
  76.8 1.5 %similar.3.before_ref = f32[5,1,144]{2,1,0:T(1,128)S(1)} custom-call(f32[1,2304]{1,0:T(1,128)S(1)} %get-tuple-element.68.row_ref, f32[2304,128]{1,0:T(8,128)S(1)} %get-tuple-element.69.col_ref, bf16[144,768]{1,0:T(8,128)(2,1)S(1)} %collective-permute-done.refs_0_, bf16[144,768]{1,0:T(8,128)(2,1)S(1)} %collective-permute-done.1.refs_1_, ...), custom_call_target="tpu_custom_call" | custom-call | flops 796262400 | bytes 8388608 | tf_op jit(solution)/shard_map/similar/pallas_call | solution.py:385
  78.3 1.0 copy-done.2
  79.9 9.7 %all-to-all-done.4 = bf16[8,144,768]{2,1,0:T(8,128)(2,1)S(1)} async-done(((bf16[8,144,768]{2,1,0:T(8,128)(2,1)}), bf16[8,144,768]{2,1,0:T(8,128)(2,1)S(1)}, u32[]{:S(2)}, u32[]{:S(2)}) %all-to-all-start.4) | async-done | bytes 1769504 | tf_op jit(solution)/shard_map/all_to_all | solution.py:467
  89.6 1.3 %copy-done.3 = f32[2304,128]{1,0:T(8,128)S(1)} copy-done((f32[2304,128]{1,0:T(8,128)S(1)}, f32[2304,128]{1,0:T(8,128)}, u32[]{:S(2)}) %copy-start.3) | copy-done | bytes 1179672
  90.9 0.7 copy-done.5
  92.3 4.3 %similar.4.before_ref = f32[13,1,144]{2,1,0:T(1,128)S(1)} custom-call(s32[1]{0:T(128)} %bitcast.11.me_ref, f32[1,2304]{1,0:T(1,128)S(1)} %copy-done.5, f32[2304,128]{1,0:T(8,128)S(1)} %copy-done.3, f32[5,1,144]{2,1,0:T(1,128)S(1)} %copy-done.7, bf16[144,768]{1,0:T(8,128)(2,1)S(1)} %collective-permute-done.refs_0_, ...), custom_call_target="tpu_custom_call" | custom-call | flops 3312451584 | bytes 8388608 | tf_op jit(solution)/shard_map/similar/pallas_call | solution.py:385
  96.5 5.2 %collective-permute-done.6.refs_7_ = bf16[144,768]{1,0:T(8,128)(2,1)} collective-permute-done((bf16[144,768]{1,0:T(8,128)(2,1)S(1)}, bf16[144,768]{1,0:T(8,128)(2,1)}, u32[]{:S(2)}, u32[]{:S(2)}) %collective-permute-start.6) | collective-permute-done | bytes 221216 | tf_op jit(solution)/shard_map/ppermute | solution.py:471
  101.7 3.8 %collective-permute-done.7.refs_8_ = bf16[144,768]{1,0:T(8,128)(2,1)} collective-permute-done((bf16[144,768]{1,0:T(8,128)(2,1)S(1)}, bf16[144,768]{1,0:T(8,128)(2,1)}, u32[]{:S(2)}, u32[]{:S(2)}) %collective-permute-start.7) | collective-permute-done | bytes 221216 | tf_op jit(solution)/shard_map/ppermute | solution.py:471
  105.5 3.9 %similar.5 = f32[16,1,144]{2,1,0:T(1,128)} custom-call(s32[1]{0:T(128)} %bitcast.11.me_ref, f32[1,2304]{1,0:T(1,128)S(1)} %copy-done.5, f32[2304,128]{1,0:T(8,128)S(1)} %copy-done.3, f32[13,1,144]{2,1,0:T(1,128)S(1)} %similar.4.before_ref, bf16[144,768]{1,0:T(8,128)(2,1)S(1)} %collective-permute-done.refs_0_, ...), custom_call_target="tpu_custom_call" | custom-call | flops 1528823808 | bytes 8388608 | tf_op jit(solution)/shard_map/similar/pallas_call | solution.py:385
  109.4 3.5 %all-to-all-start.5 = ((f32[16,1,144]{2,1,0:T(1,128)}), f32[16,1,144]{2,1,0:T(1,128)S(1)}, u32[]{:S(2)}, u32[]{:S(2)}) async-start(f32[16,1,144]{2,1,0:T(1,128)} %similar.5), calls=%async_computation.5 | async-start | bytes 32768 | tf_op jit(solution)/shard_map/all_to_all | solution.py:467
  114.2 5.2 %all-to-all-done.5.back_ref = f32[16,1,144]{2,1,0:T(1,128)S(1)} async-done(((f32[16,1,144]{2,1,0:T(1,128)}), f32[16,1,144]{2,1,0:T(1,128)S(1)}, u32[]{:S(2)}, u32[]{:S(2)}) %all-to-all-start.5) | async-done | bytes 9248 | tf_op jit(solution)/shard_map/all_to_all | solution.py:467
  (29 shorter events, 3.4 us)
Async XLA Ops:
  0.0 11.7 %copy-start.10 = (s32[2048,1]{0,1:T(1,128)S(1)}, s32[2048,1]{0,1:T(1,128)}, u32[]{:S(2)}) copy-start(s32[2048,1]{0,1:T(1,128)} %param.7) | copy-start | bytes 24580
  1.9 14.0 %all-to-all-start.3 = ((f32[16,1,512]{2,1,0:T(1,128)}), f32[16,1,512]{2,1,0:T(1,128)S(1)}, u32[]{:S(2)}, u32[]{:S(2)}) async-start(f32[16,1,512]{2,1,0:T(1,128)} %counts.1), calls=%async_computation.3 | async-start | bytes 65536 | tf_op jit(solution)/shard_map/all_to_all | solution.py:467
  11.7 10.7 %copy-start.8 = (bf16[2048,768]{1,0:T(8,128)(2,1)}, bf16[2048,768]{1,0:T(8,128)(2,1)S(1)}, u32[]{:S(2)}) copy-start(bf16[2048,768]{1,0:T(8,128)(2,1)S(1)} %unit.1.unit_ref) | copy-start | bytes 9437188
  13.1 14.9 %copy-start.12 = (s32[1,2048]{1,0:T(1,128)}, s32[1,2048]{1,0:T(1,128)S(1)}, u32[]{:S(2)}) copy-start(s32[1,2048]{1,0:T(1,128)S(1)} %ranks.1.rank_ref) | copy-start | bytes 24580
  22.4 7.2 %copy-start = (f32[24,512]{1,0:T(8,128)}, f32[24,512]{1,0:T(8,128)S(1)}, u32[]{:S(2)}) copy-start(f32[24,512]{1,0:T(8,128)S(1)} %get-tuple-element.65.table_ref) | copy-start | bytes 147460
  22.4 32.0 %collective-permute-start = (bf16[144,768]{1,0:T(8,128)(2,1)S(1)}, bf16[144,768]{1,0:T(8,128)(2,1)S(1)}, u32[]{:S(2)}, u32[]{:S(2)}) collective-permute-start(bf16[144,768]{1,0:T(8,128)(2,1)S(1)} %get-tuple-element.70), channel_id=1, source_target_pairs={{0,8},{1,9},{2,10},{3,11},{4,12},{5,13},{6,14},{7,15},{8,0},{9,1},... | collective-permute-start | bytes 663560 | tf_op jit(solution)/shard_map/ppermute | solution.py:471
  22.8 11.9 %copy-start.9 = (bf16[2048,768]{1,0:T(8,128)(2,1)S(1)}, bf16[2048,768]{1,0:T(8,128)(2,1)}, u32[]{:S(2)}) copy-start(bf16[2048,768]{1,0:T(8,128)(2,1)} %copy-done.8) | copy-start | bytes 9437188
  28.0 30.5 %collective-permute-start.1 = (bf16[144,768]{1,0:T(8,128)(2,1)S(1)}, bf16[144,768]{1,0:T(8,128)(2,1)S(1)}, u32[]{:S(2)}, u32[]{:S(2)}) collective-permute-start(bf16[144,768]{1,0:T(8,128)(2,1)S(1)} %get-tuple-element.73), channel_id=1, source_target_pairs={{0,9},{1,8},{2,11},{3,10},{4,13},{5,12},{6,15},{7,14},{8,1},{9,0},... | collective-permute-start | bytes 663560 | tf_op jit(solution)/shard_map/ppermute | solution.py:471
  29.5 34.3 %collective-permute-start.2 = (bf16[144,768]{1,0:T(8,128)(2,1)S(1)}, bf16[144,768]{1,0:T(8,128)(2,1)S(1)}, u32[]{:S(2)}, u32[]{:S(2)}) collective-permute-start(bf16[144,768]{1,0:T(8,128)(2,1)S(1)} %get-tuple-element.74), channel_id=1, source_target_pairs={{0,10},{1,11},{2,8},{3,9},{4,14},{5,15},{6,12},{7,13},{8,2},{9,3},... | collective-permute-start | bytes 663560 | tf_op jit(solution)/shard_map/ppermute | solution.py:471
  31.0 45.8 %collective-permute-start.3 = (bf16[144,768]{1,0:T(8,128)(2,1)}, bf16[144,768]{1,0:T(8,128)(2,1)S(1)}, u32[]{:S(2)}, u32[]{:S(2)}) collective-permute-start(bf16[144,768]{1,0:T(8,128)(2,1)} %get-tuple-element.72), channel_id=1, source_target_pairs={{0,11},{1,10},{2,9},{3,8},{4,15},{5,14},{6,13},{7,12},{8,3},{9,2},... | collective-permute-start | bytes 663560 | tf_op jit(solution)/shard_map/ppermute | solution.py:471
  33.8 43.0 %collective-permute-start.4 = (bf16[144,768]{1,0:T(8,128)(2,1)}, bf16[144,768]{1,0:T(8,128)(2,1)S(1)}, u32[]{:S(2)}, u32[]{:S(2)}) collective-permute-start(bf16[144,768]{1,0:T(8,128)(2,1)} %get-tuple-element.78), channel_id=1, source_target_pairs={{0,12},{1,13},{2,14},{3,15},{4,8},{5,9},{6,10},{7,11},{8,4},{9,5},... | collective-permute-start | bytes 663560 | tf_op jit(solution)/shard_map/ppermute | solution.py:471
  63.9 25.7 %all-to-all-start.4 = ((bf16[8,144,768]{2,1,0:T(8,128)(2,1)}), bf16[8,144,768]{2,1,0:T(8,128)(2,1)S(1)}, u32[]{:S(2)}, u32[]{:S(2)}) async-start(bf16[8,144,768]{2,1,0:T(8,128)(2,1)} %bitcast.14), calls=%async_computation.4 | async-start | bytes 3538944 | tf_op jit(solution)/shard_map/all_to_all | solution.py:467
  67.7 0.8 copy-start.1
  70.5 6.3 %copy-start.4 = (f32[1,2304]{1,0:T(1,128)}, f32[1,2304]{1,0:T(1,128)S(1)}, u32[]{:S(2)}) copy-start(f32[1,2304]{1,0:T(1,128)S(1)} %get-tuple-element.68.row_ref) | copy-start | bytes 27652
  70.5 26.0 %collective-permute-start.5 = (bf16[144,768]{1,0:T(8,128)(2,1)S(1)}, bf16[144,768]{1,0:T(8,128)(2,1)}, u32[]{:S(2)}, u32[]{:S(2)}) collective-permute-start(bf16[144,768]{1,0:T(8,128)(2,1)S(1)} %get-tuple-element.80), channel_id=1, source_target_pairs={{0,13},{1,12},{2,15},{3,14},{4,9},{5,8},{6,11},{7,10},{8,5},{9,4},... | collective-permute-start | bytes 663560 | tf_op jit(solution)/shard_map/ppermute | solution.py:471
  72.2 29.5 %collective-permute-start.6 = (bf16[144,768]{1,0:T(8,128)(2,1)S(1)}, bf16[144,768]{1,0:T(8,128)(2,1)}, u32[]{:S(2)}, u32[]{:S(2)}) collective-permute-start(bf16[144,768]{1,0:T(8,128)(2,1)S(1)} %get-tuple-element.81), channel_id=1, source_target_pairs={{0,14},{1,15},{2,12},{3,13},{4,10},{5,11},{6,8},{7,9},{8,6},{9,7},... | collective-permute-start | bytes 663560 | tf_op jit(solution)/shard_map/ppermute | solution.py:471
  75.3 30.2 %collective-permute-start.7 = (bf16[144,768]{1,0:T(8,128)(2,1)S(1)}, bf16[144,768]{1,0:T(8,128)(2,1)}, u32[]{:S(2)}, u32[]{:S(2)}) collective-permute-start(bf16[144,768]{1,0:T(8,128)(2,1)S(1)} %get-tuple-element.82), channel_id=1, source_target_pairs={{0,15},{1,14},{2,13},{3,12},{4,11},{5,10},{6,9},{7,8},{8,7},{9,6},... | collective-permute-start | bytes 663560 | tf_op jit(solution)/shard_map/ppermute | solution.py:471
  78.3 1.0 copy-start.2
  79.3 0.6 copy-start.6
  89.6 1.3 %copy-start.3 = (f32[2304,128]{1,0:T(8,128)S(1)}, f32[2304,128]{1,0:T(8,128)}, u32[]{:S(2)}) copy-start(f32[2304,128]{1,0:T(8,128)} %copy-done.2) | copy-start | bytes 3538948
  90.9 0.7 copy-start.5
  91.6 0.7 copy-start.7
  109.4 10.0 %all-to-all-start.5 = ((f32[16,1,144]{2,1,0:T(1,128)}), f32[16,1,144]{2,1,0:T(1,128)S(1)}, u32[]{:S(2)}, u32[]{:S(2)}) async-start(f32[16,1,144]{2,1,0:T(1,128)} %similar.5), calls=%async_computation.5 | async-start | bytes 32768 | tf_op jit(solution)/shard_map/all_to_all | solution.py:467
  119.8 0.6 copy-start.14
